TPU v7x, 32 devices: a whole 2x2x4 slice. The times are simulated.
32 devices in a mesh: fsdp: 8 (over y, x, core), sp: 4 (over z).
Axes of the slice: x: 2, y: 2, z: 4, core: 2. Of those that a mesh axis runs over, the one named last changes fastest.
Arguments:
- land: bfloat16 [8, 32, 64, 512], P('fsdp', 'sp'), may hold values from -20 to 20
- port: bfloat16 [8, 64, 32, 512], P('fsdp', 'sp'), may hold values from -20 to 20
- to_local: bfloat16 [2, 9, 512, 128], P(None, None, ('fsdp', 'sp')), may hold values from -0.09375 to 0.09375
- to_global: bfloat16 [2, 9, 128, 384], P(None, None, None, ('fsdp', 'sp')), may hold values from -0.1875 to 0.1875
- reduce_weight: bfloat16 [2, 384, 192], P(None, ('fsdp', 'sp')), may hold values from -0.3125 to 0.3125
- freq_weight: bfloat16 [2, 384, 384], P(None, ('fsdp', 'sp')), may hold values from -0.3125 to 0.3125
- expand_weight: bfloat16 [2, 192, 384], P(None, None, ('fsdp', 'sp')), may hold values from -0.4375 to 0.4375
- spec_gain: float32 [2, 192], replicated, may hold values from 0.1 to 1.9
- spec_bias: float32 [2, 192], replicated, may hold values from -3 to 3
- freq_gain: float32 [2, 384], replicated, may hold values from 0.1 to 1.9
- freq_bias: float32 [2, 384], replicated, may hold values from -3 to 3
- out_gain: float32 [2, 512], replicated, may hold values from 0.1 to 1.9
- out_bias: float32 [2, 512], replicated, may hold values from -3 to 3
- cot_land: bfloat16 [8, 32, 64, 512], P('fsdp', 'sp'), may hold values from -6 to 6
- cot_port: bfloat16 [8, 64, 32, 512], P('fsdp', 'sp'), may hold values from -6 to 6
Outputs:
- land_out: bfloat16 [8, 32, 64, 512], P('fsdp', 'sp')
- port_out: bfloat16 [8, 64, 32, 512], P('fsdp', 'sp')
- land_grad: bfloat16 [8, 32, 64, 512], P('fsdp', 'sp')
- port_grad: bfloat16 [8, 64, 32, 512], P('fsdp', 'sp')
- to_local_grad: float32 [2, 9, 512, 128], P(None, None, ('fsdp', 'sp'))
- to_global_grad: float32 [2, 9, 128, 384], P(None, None, None, ('fsdp', 'sp'))
- reduce_grad: float32 [2, 384, 192], P(None, ('fsdp', 'sp'))
- freq_grad: float32 [2, 384, 384], P(None, ('fsdp', 'sp'))
- expand_grad: float32 [2, 192, 384], P(None, None, ('fsdp', 'sp'))
- spec_gain_grad: float32 [2, 192], replicated
- spec_bias_grad: float32 [2, 192], replicated
- freq_gain_grad: float32 [2, 384], replicated
- freq_bias_grad: float32 [2, 384], replicated
- out_gain_grad: float32 [2, 512], replicated
- out_bias_grad: float32 [2, 512], replicated
All inputs are finite; a program needn't handle non-finite values.
Results may differ from a plain program's by a relative error of at most 0.018.
Values may be sent and summed in bfloat16 or wider, within the bound.
No kernel may reach another device: no remote copies, remote signals or barrier semaphores. Data moves between devices by JAX's collectives and lax.ppermute only.
A program may use at most 192 MiB of HBM per device.

v0:
```python
import math

import jax
import jax.numpy as jnp
from jax import lax
from jax.sharding import PartitionSpec as P

epsilon = 1e-05
highest = lax.Precision.HIGHEST


def extended_2(block, sides, width):
    for axis, dim in sides:
        count = lax.axis_size(axis)
        forward = [(i, i + 1) for i in range(count - 1)]
        backward = [(target, source) for source, target in forward]
        low = lax.ppermute(
            lax.slice_in_dim(block, block.shape[dim] - width, None, axis=dim), axis, forward
        )
        high = lax.ppermute(lax.slice_in_dim(block, 0, width, axis=dim), axis, backward)
        block = jnp.concatenate([low, block, high], axis=dim)
    return block


def dft_tables(length, count):
    index_out = lax.iota(jnp.int32, count)
    index_in = lax.iota(jnp.int32, length)
    product = index_out[:, None] * index_in[None, :] % length
    angle = product.astype(jnp.float32) * (2.0 * math.pi / length)
    return (jnp.cos(angle), jnp.sin(angle))


def edge_weights(count, map_cols):
    index_out = lax.iota(jnp.int32, count)
    edges = (index_out == 0) | (index_out * 2 == map_cols)
    return jnp.where(edges, 1.0, 2.0).astype(jnp.float32)


def project(values, matrix):
    return lax.dot_general(
        values, matrix, (((3,), (0,)), ((), ())), preferred_element_type=jnp.float32
    )


def project_back(values, matrix):
    return lax.dot_general(
        values, matrix, (((3,), (1,)), ((), ())), preferred_element_type=jnp.float32
    )


def outer_sum(left, right):
    return lax.dot_general(
        left, right, (((0, 1, 2), (0, 1, 2)), ((), ())), preferred_element_type=jnp.float32
    )


def unfold(padded, rows_local, map_cols):
    return jnp.concatenate(
        [
            padded[:, tap // 3 : tap // 3 + rows_local, tap % 3 : tap % 3 + map_cols, :]
            for tap in range(9)
        ],
        axis=3,
    )


def padded_input(values):
    extended = extended_2(values, (("sp", 1),), 1)
    return jnp.pad(extended, ((0, 0), (0, 0), (1, 1), (0, 0)))


def padded_grad(values):
    extended = extended_2(values, (("sp", 1),), 1)
    return jnp.pad(extended, ((0, 0), (0, 0), (1, 1), (0, 0)))


def position_count(values):
    return values.shape[0] * values.shape[1] * values.shape[2] * lax.axis_size(("fsdp", "sp"))


def freq_position_count(images, map_rows, map_cols):
    return images * map_rows * (map_cols // 2 + 1) * lax.axis_size("fsdp")


def normalize(values, positions):
    local_sum = jnp.sum(values, axis=(0, 1, 2))
    center = lax.psum(local_sum, ("fsdp", "sp")) / positions
    centered = values - center
    squared = centered * centered
    spread = lax.psum(jnp.sum(squared, axis=(0, 1, 2)), ("fsdp", "sp")) / positions
    scale_inv = lax.rsqrt(spread + epsilon)
    return (centered * scale_inv, scale_inv)


def norm_back(grad_out, normed, gain, scale_inv, positions):
    bias_grad, gain_grad = lax.psum(
        (jnp.sum(grad_out, axis=(0, 1, 2)), jnp.sum(grad_out * normed, axis=(0, 1, 2))),
        ("fsdp", "sp"),
    )
    grad_in = gain * scale_inv * (grad_out - bias_grad / positions - normed * gain_grad / positions)
    return (grad_in, gain_grad, bias_grad)


def gelu_back(pre_act, grad):
    pullback = jax.vjp(jax.nn.gelu, pre_act)[1]
    return pullback(grad)[0]


def to_spectrum(values):
    rows_local = values.shape[1]
    map_cols = values.shape[2]
    channels = values.shape[3]
    map_rows = rows_local * lax.axis_size("sp")
    cos_rows, sin_rows = dft_tables(map_rows, map_rows)
    piece = lax.all_to_all(values, "sp", split_axis=2, concat_axis=1, tiled=True)
    real_part = jnp.einsum("kh,bhwc->bkwc", cos_rows, piece, precision=highest)
    imag_part = -jnp.einsum("kh,bhwc->bkwc", sin_rows, piece, precision=highest)
    columns = jnp.concatenate([real_part, imag_part], axis=3)
    spectral_rows = lax.all_to_all(columns, "sp", split_axis=1, concat_axis=2, tiled=True)
    freq_count = map_cols // 2 + 1
    cos_cols, sin_cols = dft_tables(map_cols, freq_count)
    real_in = spectral_rows[..., :channels]
    imag_in = spectral_rows[..., channels:]
    real_out = jnp.einsum("fw,bkwc->bkfc", cos_cols, real_in, precision=highest) + jnp.einsum(
        "fw,bkwc->bkfc", sin_cols, imag_in, precision=highest
    )
    imag_out = jnp.einsum("fw,bkwc->bkfc", cos_cols, imag_in, precision=highest) - jnp.einsum(
        "fw,bkwc->bkfc", sin_cols, real_in, precision=highest
    )
    return jnp.concatenate([real_out, imag_out], axis=3) * (1.0 / math.sqrt(map_rows * map_cols))


def from_spectrum(values, edge):
    rows_local = values.shape[1]
    freq_count = values.shape[2]
    channels = values.shape[3] // 2
    map_cols = 2 * (freq_count - 1)
    map_rows = rows_local * lax.axis_size("sp")
    cos_cols, sin_cols = dft_tables(map_cols, freq_count)
    cos_cols = cos_cols * edge[:, None]
    sin_cols = sin_cols * edge[:, None]
    real_in = values[..., :channels]
    imag_in = values[..., channels:]
    real_mid = jnp.einsum("fw,bkfc->bkwc", cos_cols, real_in, precision=highest) - jnp.einsum(
        "fw,bkfc->bkwc", sin_cols, imag_in, precision=highest
    )
    imag_mid = jnp.einsum("fw,bkfc->bkwc", sin_cols, real_in, precision=highest) + jnp.einsum(
        "fw,bkfc->bkwc", cos_cols, imag_in, precision=highest
    )
    middle = jnp.concatenate([real_mid, imag_mid], axis=3)
    cos_rows, sin_rows = dft_tables(map_rows, map_rows)
    piece = lax.all_to_all(middle, "sp", split_axis=2, concat_axis=1, tiled=True)
    real_part = jnp.einsum("kh,bkwc->bhwc", cos_rows, piece[..., :channels], precision=highest)
    columns = real_part - jnp.einsum(
        "kh,bkwc->bhwc", sin_rows, piece[..., channels:], precision=highest
    )
    restored = lax.all_to_all(columns, "sp", split_axis=1, concat_axis=2, tiled=True)
    return restored * (1.0 / math.sqrt(map_rows * map_cols))


def forward_transform(values, map_cols, with_edges):
    result = to_spectrum(values)
    if with_edges:
        result = result * edge_weights(result.shape[2], map_cols)[:, None]
    return result


def inverse_transform(values, map_cols, with_edges):
    freq_count = map_cols // 2 + 1
    if with_edges:
        edge = edge_weights(freq_count, map_cols)
    else:
        edge = jnp.ones((freq_count,), jnp.float32)
    return from_spectrum(values, edge)


def section_forward(values, weights, gains):
    local_kernel, global_kernel, reduce_kernel, freq_kernel, expand_kernel = weights
    spec_gain, spec_bias, freq_gain, freq_bias, out_gain, out_bias = gains
    narrow = local_kernel.shape[2]
    rounded = values.astype(jnp.bfloat16)
    rows_local = rounded.shape[1]
    map_cols = rounded.shape[2]
    channels = rounded.shape[3]
    map_rows = rows_local * lax.axis_size("sp")
    padded = padded_input(rounded)
    patches = unfold(padded, rows_local, map_cols)
    patches_local = unfold(padded[..., :narrow], rows_local, map_cols)
    local_pre = project(patches, local_kernel.reshape(9 * channels, narrow))
    global_pre = project(patches_local, global_kernel.reshape(9 * narrow, channels - narrow))
    reduced = project(rounded[..., narrow:], reduce_kernel)
    normed_spec, inv_spec = normalize(reduced, position_count(reduced))
    act_spec = normed_spec * spec_gain + spec_bias
    hidden = jax.nn.gelu(act_spec)
    spectrum_low = forward_transform(hidden, map_cols, False).astype(jnp.bfloat16)
    mixed = project(spectrum_low, freq_kernel)
    freq_positions = freq_position_count(rounded.shape[0], map_rows, map_cols)
    normed_freq, inv_freq = normalize(mixed, freq_positions)
    act_freq = normed_freq * freq_gain + freq_bias
    returned = inverse_transform(jax.nn.gelu(act_freq), map_cols, True)
    summed_low = (hidden + returned).astype(jnp.bfloat16)
    both_pre = jnp.concatenate([local_pre, global_pre + project(summed_low, expand_kernel)], axis=3)
    normed_out, inv_out = normalize(both_pre, position_count(both_pre))
    act_out = normed_out * out_gain + out_bias
    kept = (
        padded,
        normed_spec,
        inv_spec,
        act_spec,
        spectrum_low,
        normed_freq,
        inv_freq,
        act_freq,
        summed_low,
        normed_out,
        inv_out,
        act_out,
    )
    return (jax.nn.gelu(act_out), kept)


def section_backward(grad_out, kept, weights, gains):
    (
        padded,
        normed_spec,
        inv_spec,
        act_spec,
        spectrum_low,
        normed_freq,
        inv_freq,
        act_freq,
        summed_low,
        normed_out,
        inv_out,
        act_out,
    ) = kept
    local_kernel, global_kernel, reduce_kernel, freq_kernel, expand_kernel = weights
    spec_gain, spec_bias, freq_gain, freq_bias, out_gain, out_bias = gains
    narrow = local_kernel.shape[2]
    rows_local = normed_out.shape[1]
    map_cols = normed_out.shape[2]
    channels = normed_out.shape[3]
    map_rows = rows_local * lax.axis_size("sp")
    grad_pre, out_gain_grad, out_bias_grad = norm_back(
        gelu_back(act_out, grad_out), normed_out, out_gain, inv_out, position_count(grad_out)
    )
    grad_low = grad_pre.astype(jnp.bfloat16)
    grad_local = grad_low[..., :narrow]
    grad_global = grad_low[..., narrow:]
    grad_padded = padded_grad(grad_low)
    back_local = jnp.transpose(local_kernel[::-1], (0, 2, 1)).reshape(9 * narrow, channels)
    back_global = jnp.transpose(global_kernel[::-1], (0, 2, 1)).reshape(
        9 * (channels - narrow), narrow
    )
    grad_input = project(unfold(grad_padded[..., :narrow], rows_local, map_cols), back_local)
    into_local = project(unfold(grad_padded[..., narrow:], rows_local, map_cols), back_global)
    patches = unfold(padded, rows_local, map_cols)
    patches_local = unfold(padded[..., :narrow], rows_local, map_cols)
    local_kernel_grad = outer_sum(patches, grad_local).reshape(9, channels, narrow)
    global_kernel_grad = outer_sum(patches_local, grad_global).reshape(9, narrow, channels - narrow)
    expand_grad = outer_sum(summed_low, grad_global)
    grad_summed = project_back(grad_global, expand_kernel)
    grad_spectrum = forward_transform(grad_summed, map_cols, True)
    freq_positions = freq_position_count(normed_out.shape[0], map_rows, map_cols)
    grad_mixed, freq_gain_grad, freq_bias_grad = norm_back(
        gelu_back(act_freq, grad_spectrum), normed_freq, freq_gain, inv_freq, freq_positions
    )
    grad_mixed_low = grad_mixed.astype(jnp.bfloat16)
    freq_grad = outer_sum(spectrum_low, grad_mixed_low)
    grad_freq_in = project_back(grad_mixed_low, freq_kernel)
    grad_hidden = grad_summed + inverse_transform(grad_freq_in, map_cols, False)
    grad_reduced, spec_gain_grad, spec_bias_grad = norm_back(
        gelu_back(act_spec, grad_hidden),
        normed_spec,
        spec_gain,
        inv_spec,
        position_count(grad_hidden),
    )
    grad_reduced_low = grad_reduced.astype(jnp.bfloat16)
    rounded = padded[:, 1 : rows_local + 1, 1 : map_cols + 1, :]
    reduce_grad = outer_sum(rounded[..., narrow:], grad_reduced_low)
    into_global = project_back(grad_reduced_low, reduce_kernel)
    grad_values = grad_input + jnp.concatenate([into_local, into_global], axis=3)
    weight_terms = (local_kernel_grad, global_kernel_grad, reduce_grad, freq_grad, expand_grad)
    gain_terms = (
        spec_gain_grad,
        spec_bias_grad,
        freq_gain_grad,
        freq_bias_grad,
        out_gain_grad,
        out_bias_grad,
    )
    return (grad_values, weight_terms, gain_terms)


def per_device(
    land,
    port,
    to_local,
    to_global,
    reduce_weight,
    freq_weight,
    expand_weight,
    spec_gain,
    spec_bias,
    freq_gain,
    freq_bias,
    out_gain,
    out_bias,
    cot_land,
    cot_port,
):
    section_count = to_local.shape[0]
    gain_args = (spec_gain, spec_bias, freq_gain, freq_bias, out_gain, out_bias)
    states = [land, port]
    kept_all = []
    gathered = []
    for section_index in range(section_count):
        fetched = (
            lax.all_gather(to_local[section_index], ("fsdp", "sp"), axis=1, tiled=True),
            lax.all_gather(to_global[section_index], ("fsdp", "sp"), axis=2, tiled=True),
            lax.all_gather(reduce_weight[section_index], ("fsdp", "sp"), axis=0, tiled=True),
            lax.all_gather(freq_weight[section_index], ("fsdp", "sp"), axis=0, tiled=True),
            lax.all_gather(expand_weight[section_index], ("fsdp", "sp"), axis=1, tiled=True),
        )
        gathered.append(fetched)
        gains = tuple((item[section_index] for item in gain_args))
        kept_section = []
        for batch_index in range(2):
            states[batch_index], kept_one = section_forward(states[batch_index], fetched, gains)
            kept_section.append(kept_one)
        kept_all.append(kept_section)
    land_out = (land.astype(jnp.float32) + states[0]).astype(jnp.bfloat16)
    port_out = (port.astype(jnp.float32) + states[1]).astype(jnp.bfloat16)
    grads = [cot_land.astype(jnp.float32), cot_port.astype(jnp.float32)]
    weight_shares = [None] * section_count
    gain_grads = [None] * section_count
    for section_index in reversed(range(section_count)):
        fetched = (
            lax.all_gather(to_local[section_index], ("fsdp", "sp"), axis=1, tiled=True),
            lax.all_gather(to_global[section_index], ("fsdp", "sp"), axis=2, tiled=True),
            lax.all_gather(reduce_weight[section_index], ("fsdp", "sp"), axis=0, tiled=True),
            lax.all_gather(freq_weight[section_index], ("fsdp", "sp"), axis=0, tiled=True),
            lax.all_gather(expand_weight[section_index], ("fsdp", "sp"), axis=1, tiled=True),
        )
        gains = tuple((item[section_index] for item in gain_args))
        results = []
        for batch_index in range(2):
            grad_values, weight_terms, gain_terms = section_backward(
                grads[batch_index], kept_all[section_index][batch_index], fetched, gains
            )
            grads[batch_index] = grad_values
            results.append((weight_terms, gain_terms))
        totals = jax.tree.map(jnp.add, results[0][0], results[1][0])
        gain_grads[section_index] = jax.tree.map(jnp.add, results[0][1], results[1][1])
        weight_shares[section_index] = (
            lax.psum_scatter(totals[0], ("fsdp", "sp"), scatter_dimension=1, tiled=True),
            lax.psum_scatter(totals[1], ("fsdp", "sp"), scatter_dimension=2, tiled=True),
            lax.psum_scatter(totals[2], ("fsdp", "sp"), scatter_dimension=0, tiled=True),
            lax.psum_scatter(totals[3], ("fsdp", "sp"), scatter_dimension=0, tiled=True),
            lax.psum_scatter(totals[4], ("fsdp", "sp"), scatter_dimension=1, tiled=True),
        )
    land_grad = (cot_land.astype(jnp.float32) + grads[0]).astype(jnp.bfloat16)
    port_grad = (cot_port.astype(jnp.float32) + grads[1]).astype(jnp.bfloat16)
    stacked_weights = [
        jnp.stack([weight_shares[section_index][member] for section_index in range(section_count)])
        for member in range(5)
    ]
    stacked_gains = [
        jnp.stack([gain_grads[section_index][member] for section_index in range(section_count)])
        for member in range(6)
    ]
    return (
        land_out,
        port_out,
        land_grad,
        port_grad,
        stacked_weights[0],
        stacked_weights[1],
        stacked_weights[2],
        stacked_weights[3],
        stacked_weights[4],
        stacked_gains[0],
        stacked_gains[1],
        stacked_gains[2],
        stacked_gains[3],
        stacked_gains[4],
        stacked_gains[5],
    )


def solution(mesh):
    return jax.shard_map(
        per_device,
        mesh=mesh,
        in_specs=(
            P("fsdp", "sp", None, None),
            P("fsdp", "sp", None, None),
            P(None, None, ("fsdp", "sp"), None),
            P(None, None, None, ("fsdp", "sp")),
            P(None, ("fsdp", "sp"), None),
            P(None, ("fsdp", "sp"), None),
            P(None, None, ("fsdp", "sp")),
            P(),
            P(),
            P(),
            P(),
            P(),
            P(),
            P("fsdp", "sp", None, None),
            P("fsdp", "sp", None, None),
        ),
        out_specs=(
            P("fsdp", "sp", None, None),
            P("fsdp", "sp", None, None),
            P("fsdp", "sp", None, None),
            P("fsdp", "sp", None, None),
            P(None, None, ("fsdp", "sp"), None),
            P(None, None, None, ("fsdp", "sp")),
            P(None, ("fsdp", "sp"), None),
            P(None, ("fsdp", "sp"), None),
            P(None, None, ("fsdp", "sp")),
            P(),
            P(),
            P(),
            P(),
            P(),
            P(),
        ),
        check_vma=False,
    )
```

profile of v0, /device:TPU:0, one launch (start us, length us, event | category | flops | bytes accessed | tf_op | source)
XLA Modules:
  0.0 2579.7 jit_solution(93929330637560690)
XLA Ops:
  8.7 5.5 collective-permute-start.4
  25.2 71.7 %all-gather.2 = bf16[1,384,192]{2,0,1:T(2,128)(2,1)S(1)} all-gather(bf16[1,12,192]{2,0,1:T(2,128)(2,1)S(1)} %get-tuple-element.219), channel_id=4, replica_groups=mesh['fsdp'=8,'sp'=4] {'fsdp','sp'}, dimensions={1}, use_global_device_ids=true | all-gather | bytes 152064 | tf_op jit(solution)/shard_map/all_gather | solution.py:322
  98.2 36.9 %all-reduce.37 = (f32[192]{0:T(256)S(1)}, f32[192]{0:T(256)S(1)}) all-reduce(f32[192]{0:T(256)S(1)} %get-tuple-element.270, f32[192]{0:T(256)S(1)} %get-tuple-element.272), channel_id=1, replica_groups=mesh['fsdp'=8,'sp'=4] {'fsdp','sp'}, use_global_device_ids=true, to_apply=%region_1.2 | all-reduce | flops 384 | bytes 3072 | tf_op jit(solution)/shard_map/psum | solution.py:87
  135.3 41.6 %all-reduce.36 = (f32[192]{0:T(256)S(1)}, f32[192]{0:T(256)S(1)}) all-reduce(f32[192]{0:T(256)S(1)} %multiply_reduce_fusion.19, f32[192]{0:T(256)S(1)} %multiply_reduce_fusion.17), channel_id=1, replica_groups=mesh['fsdp'=8,'sp'=4] {'fsdp','sp'}, use_global_device_ids=true, to_apply=%region_3.4 | all-reduce | flops 384 | bytes 3072 | tf_op jit(solution)/shard_map/psum | solution.py:90
  188.7 75.4 %all-gather.9 = bf16[1,192,384]{1,0,2:T(2,128)(2,1)} all-gather(bf16[1,192,12]{1,0,2:T(2,128)(2,1)S(1)} %get-tuple-element.216), channel_id=11, replica_groups=mesh['fsdp'=8,'sp'=4] {'fsdp','sp'}, dimensions={2}, use_global_device_ids=true | all-gather | bytes 152064 | tf_op jit(solution)/shard_map/all_gather | solution.py:324
  264.0 71.6 %all-gather.7 = bf16[1,384,192]{2,0,1:T(2,128)(2,1)} all-gather(bf16[1,12,192]{2,0,1:T(2,128)(2,1)S(1)} %get-tuple-element.218), channel_id=9, replica_groups=mesh['fsdp'=8,'sp'=4] {'fsdp','sp'}, dimensions={1}, use_global_device_ids=true | all-gather | bytes 152064 | tf_op jit(solution)/shard_map/all_gather | solution.py:322
  336.7 75.1 %all-gather.8 = bf16[1,384,384]{2,0,1:T(2,128)(2,1)} all-gather(bf16[1,12,384]{2,0,1:T(2,128)(2,1)S(1)} %get-tuple-element.214), channel_id=10, replica_groups=mesh['fsdp'=8,'sp'=4] {'fsdp','sp'}, dimensions={1}, use_global_device_ids=true | all-gather | bytes 304128 | tf_op jit(solution)/shard_map/all_gather | solution.py:323
  411.7 73.8 %all-gather.3 = bf16[1,384,384]{2,0,1:T(2,128)(2,1)} all-gather(bf16[1,12,384]{2,0,1:T(2,128)(2,1)S(1)} %get-tuple-element.215), channel_id=5, replica_groups=mesh['fsdp'=8,'sp'=4] {'fsdp','sp'}, dimensions={1}, use_global_device_ids=true | all-gather | bytes 304128 | tf_op jit(solution)/shard_map/all_gather | solution.py:323
  485.5 85.8 %all-gather.6 = bf16[1,9,128,384]{2,1,0,3:T(8,128)(2,1)} all-gather(bf16[1,9,128,12]{2,1,0,3:T(8,128)(2,1)S(1)} %copy.517), channel_id=8, replica_groups=mesh['fsdp'=8,'sp'=4] {'fsdp','sp'}, dimensions={3}, use_global_device_ids=true | all-gather | bytes 912384 | tf_op jit(solution)/shard_map/all_gather | solution.py:321
  574.7 81.7 %all-gather.1 = bf16[1,9,128,384]{2,1,0,3:T(8,128)(2,1)} all-gather(bf16[1,9,128,12]{2,1,0,3:T(8,128)(2,1)S(1)} %copy.516), channel_id=3, replica_groups=mesh['fsdp'=8,'sp'=4] {'fsdp','sp'}, dimensions={3}, use_global_device_ids=true | all-gather | bytes 912384 | tf_op jit(solution)/shard_map/all_gather | solution.py:321
  662.0 73.1 %all-gather.4 = bf16[1,192,384]{1,0,2:T(2,128)(2,1)} all-gather(bf16[1,192,12]{1,0,2:T(2,128)(2,1)S(1)} %get-tuple-element.217), channel_id=6, replica_groups=mesh['fsdp'=8,'sp'=4] {'fsdp','sp'}, dimensions={2}, use_global_device_ids=true | all-gather | bytes 152064 | tf_op jit(solution)/shard_map/all_gather | solution.py:324
  769.7 5.4 all-to-all-done
  785.2 8.6 all-to-all-done.9
  804.3 9.5 all-to-all-done.1
  819.5 44.3 %all-reduce.35 = (f32[384]{0:T(512)}, f32[384]{0:T(512)}) all-reduce(f32[384]{0:T(512)S(1)} %get-tuple-element.274, f32[384]{0:T(512)S(1)} %get-tuple-element.276), channel_id=1, replica_groups=mesh['fsdp'=8,'sp'=4] {'fsdp','sp'}, use_global_device_ids=true, to_apply=%region_5.6 | all-reduce | flops 768 | bytes 6144 | tf_op jit(solution)/shard_map/psum | solution.py:87
  865.9 43.6 %all-reduce.34 = (f32[384]{0:T(512)}, f32[384]{0:T(512)}) all-reduce(f32[384]{0:T(512)} %multiply_reduce_fusion.23, f32[384]{0:T(512)} %multiply_reduce_fusion.11), channel_id=1, replica_groups=mesh['fsdp'=8,'sp'=4] {'fsdp','sp'}, use_global_device_ids=true, to_apply=%region_7.8 | all-reduce | flops 768 | bytes 6144 | tf_op jit(solution)/shard_map/psum | solution.py:90
  927.0 14.4 all-to-all-done.2
  955.5 9.7 all-to-all-done.10
  977.9 6.0 all-to-all-done.3
  1005.7 40.6 %all-reduce.33 = (f32[512]{0:T(512)S(1)}, f32[512]{0:T(512)S(1)}) all-reduce(f32[512]{0:T(512)S(1)} %fusion.190, f32[512]{0:T(512)S(1)} %fusion.189), channel_id=1, replica_groups=mesh['fsdp'=8,'sp'=4] {'fsdp','sp'}, use_global_device_ids=true, to_apply=%region_9.10 | all-reduce | flops 1024 | bytes 8192 | tf_op jit(solution)/shard_map/psum | solution.py:87
  1046.7 39.7 %all-reduce.32 = (f32[512]{0:T(512)S(1)}, f32[512]{0:T(512)S(1)}) all-reduce(f32[512]{0:T(512)S(1)} %multiply_reduce_fusion.7, f32[512]{0:T(512)S(1)} %multiply_reduce_fusion.5), channel_id=1, replica_groups=mesh['fsdp'=8,'sp'=4] {'fsdp','sp'}, use_global_device_ids=true, to_apply=%region_11.12 | all-reduce | flops 1024 | bytes 8192 | tf_op jit(solution)/shard_map/psum | solution.py:90
  1100.2 42.5 %all-reduce.31 = (f32[192]{0:T(256)S(1)}, f32[192]{0:T(256)S(1)}) all-reduce(f32[192]{0:T(256)S(1)} %get-tuple-element.278, f32[192]{0:T(256)S(1)} %get-tuple-element.280), channel_id=1, replica_groups=mesh['fsdp'=8,'sp'=4] {'fsdp','sp'}, use_global_device_ids=true, to_apply=%region_13.14 | all-reduce | flops 384 | bytes 3072 | tf_op jit(solution)/shard_map/psum | solution.py:87
  1142.9 40.3 %all-reduce.30 = (f32[192]{0:T(256)S(1)}, f32[192]{0:T(256)S(1)}) all-reduce(f32[192]{0:T(256)S(1)} %multiply_reduce_fusion.18, f32[192]{0:T(256)S(1)} %multiply_reduce_fusion.16), channel_id=1, replica_groups=mesh['fsdp'=8,'sp'=4] {'fsdp','sp'}, use_global_device_ids=true, to_apply=%region_15.16 | all-reduce | flops 384 | bytes 3072 | tf_op jit(solution)/shard_map/psum | solution.py:90
  1214.0 8.6 all-to-all-done.4
  1234.9 11.5 all-to-all-done.13
  1257.2 13.2 all-to-all-done.5
  1277.8 37.6 %all-reduce.29 = (f32[384]{0:T(512)S(1)}, f32[384]{0:T(512)S(1)}) all-reduce(f32[384]{0:T(512)S(1)} %get-tuple-element.282, f32[384]{0:T(512)S(1)} %get-tuple-element.284), channel_id=1, replica_groups=mesh['fsdp'=8,'sp'=4] {'fsdp','sp'}, use_global_device_ids=true, to_apply=%region_17.18 | all-reduce | flops 768 | bytes 6144 | tf_op jit(solution)/shard_map/psum | solution.py:87
  1317.7 42.9 %all-reduce.28 = (f32[384]{0:T(512)S(1)}, f32[384]{0:T(512)S(1)}) all-reduce(f32[384]{0:T(512)S(1)} %multiply_reduce_fusion.22, f32[384]{0:T(512)S(1)} %multiply_reduce_fusion.10), channel_id=1, replica_groups=mesh['fsdp'=8,'sp'=4] {'fsdp','sp'}, use_global_device_ids=true, to_apply=%region_19.20 | all-reduce | flops 768 | bytes 6144 | tf_op jit(solution)/shard_map/psum | solution.py:90
  1378.1 13.1 all-to-all-done.6
  1406.0 9.1 all-to-all-done.14
  1423.8 9.5 all-to-all-done.7
  1442.1 8.5 all-to-all-done.15
  1454.8 38.0 %all-reduce.27 = (f32[512]{0:T(512)}, f32[512]{0:T(512)}) all-reduce(f32[512]{0:T(512)} %fusion.400, f32[512]{0:T(512)} %fusion.399), channel_id=1, replica_groups=mesh['fsdp'=8,'sp'=4] {'fsdp','sp'}, use_global_device_ids=true, to_apply=%region_21.22 | all-reduce | flops 1024 | bytes 8192 | tf_op jit(solution)/shard_map/psum | solution.py:87
  1497.1 41.6 %all-reduce.26 = (f32[512]{0:T(512)}, f32[512]{0:T(512)}) all-reduce(f32[512]{0:T(512)} %multiply_reduce_fusion.6, f32[512]{0:T(512)} %multiply_reduce_fusion.4), channel_id=1, replica_groups=mesh['fsdp'=8,'sp'=4] {'fsdp','sp'}, use_global_device_ids=true, to_apply=%region_23.24 | all-reduce | flops 1024 | bytes 8192 | tf_op jit(solution)/shard_map/psum | solution.py:90
  1546.6 40.1 %all-reduce.25 = (f32[512]{0:T(512)}, f32[512]{0:T(512)S(1)}, f32[512]{0:T(512)}, f32[512]{0:T(512)S(1)}) all-reduce(f32[512]{0:T(512)S(1)} %get-tuple-element.97, f32[512]{0:T(512)S(1)} %get-tuple-element.96, f32[512]{0:T(512)S(1)} %copy-done.242, f32[512]{0:T(512)S(1)} %copy-done.241), channel_id=1, replica_groups=mesh['fsdp'=8,'sp'=4] {'fsdp','sp'}, use_global_device_ids=true, to_apply=%region_51.52 | all-reduce | flops 2048 | bytes 16384 | tf_op jit(solution)/shard_map/psum | solution.py:96
  1607.0 5.3 bitcast_add_fusion
  1613.5 5.2 collective-permute-start.8
  1652.2 16.7 all-to-all-done.24
  1681.6 17.7 all-to-all-done.17
  1699.2 5.3 all-to-all-start.25
  1712.4 19.4 all-to-all-done.25
  1739.5 38.5 %all-reduce.24 = (f32[384]{0:T(512)S(1)}, f32[384]{0:T(512)S(1)}, f32[384]{0:T(512)S(1)}, f32[384]{0:T(512)S(1)}) all-reduce(f32[384]{0:T(512)S(1)} %get-tuple-element.113, f32[384]{0:T(512)S(1)} %get-tuple-element.112, f32[384]{0:T(512)S(1)} %get-tuple-element.101, ...), channel_id=1, replica_groups=mesh['fsdp'=8,'sp'=4] {'fsdp','sp'}, use_global_device_ids=true, to_apply=%region_55.56 | all-reduce | flops 1536 | bytes 12288 | tf_op jit(solution)/shard_map/psum | solution.py:96
  1796.4 13.5 all-to-all-done.26
  1823.6 10.5 all-to-all-done.18
  1843.3 9.0 all-to-all-done.27
  1862.8 7.6 all-to-all-done.19
  1872.9 37.9 %all-reduce.23 = (f32[192]{0:T(256)S(1)}, f32[192]{0:T(256)S(1)}, f32[192]{0:T(256)S(1)}, f32[192]{0:T(256)S(1)}) all-reduce(f32[192]{0:T(256)S(1)} %get-tuple-element.109, f32[192]{0:T(256)S(1)} %get-tuple-element.108, f32[192]{0:T(256)S(1)} %get-tuple-element.105, ...), channel_id=1, replica_groups=mesh['fsdp'=8,'sp'=4] {'fsdp','sp'}, use_global_device_ids=true, to_apply=%region_59.60 | all-reduce | flops 768 | bytes 6144 | tf_op jit(solution)/shard_map/psum | solution.py:96
  1924.9 41.0 %all-reduce.22 = (f32[512]{0:T(512)S(1)}, f32[512]{0:T(512)S(1)}, f32[512]{0:T(512)S(1)}, f32[512]{0:T(512)S(1)}) all-reduce(f32[512]{0:T(512)S(1)} %get-tuple-element.95, f32[512]{0:T(512)S(1)} %get-tuple-element.94, f32[512]{0:T(512)S(1)} %get-tuple-element.91, ...), channel_id=1, replica_groups=mesh['fsdp'=8,'sp'=4] {'fsdp','sp'}, use_global_device_ids=true, to_apply=%region_63.64 | all-reduce | flops 2048 | bytes 16384 | tf_op jit(solution)/shard_map/psum | solution.py:96
  1974.6 5.1 collective-permute-start.10
  1998.7 5.2 bitcast_add_fusion.1
  2029.2 11.9 all-to-all-done.28
  2052.4 18.6 all-to-all-done.21
  2080.4 22.2 all-to-all-done.29
  2109.6 40.4 %all-reduce.21 = (f32[384]{0:T(512)S(1)}, f32[384]{0:T(512)S(1)}, f32[384]{0:T(512)S(1)}, f32[384]{0:T(512)S(1)}) all-reduce(f32[384]{0:T(512)S(1)} %get-tuple-element.111, f32[384]{0:T(512)S(1)} %get-tuple-element.110, f32[384]{0:T(512)S(1)} %get-tuple-element.99, ...), channel_id=1, replica_groups=mesh['fsdp'=8,'sp'=4] {'fsdp','sp'}, use_global_device_ids=true, to_apply=%region_67.68 | all-reduce | flops 1536 | bytes 12288 | tf_op jit(solution)/shard_map/psum | solution.py:96
  2164.4 15.3 all-to-all-done.22
  2192.8 10.9 all-to-all-done.30
  2211.8 9.5 all-to-all-done.23
  2225.6 97.8 %fusion.1077 = (f32[16,384]{1,0:T(8,128)S(1)}, f32[16,384]{1,0:T(8,128)S(1)}, f32[192,16]{0,1:T(8,128)S(1)}, f32[192,16]{0,1:T(8,128)S(1)}) fusion(f32[384,384]{1,0:T(8,128)S(1)} %copy-done.123, f32[384,384]{1,0:T(8,128)S(1)} %fusion.76, f32[192,384]{0,1:T(8,128)S(1)} %copy-done.92, f32[192,384]{0,1:T(8,128)S(1)} %copy-done.93), kind=kCustom, calls=%all-reduce-scatter.4 | all-reduce-scatter fusion | flops 589825 | bytes 1843200
  2326.0 5.9 collective-permute-start.44
  2348.6 6.6 collective-permute-start.38
  2369.0 38.2 %all-reduce.20 = (f32[192]{0:T(256)S(1)}, f32[192]{0:T(256)S(1)}, f32[192]{0:T(256)S(1)}, f32[192]{0:T(256)S(1)}) all-reduce(f32[192]{0:T(256)S(1)} %get-tuple-element.107, f32[192]{0:T(256)S(1)} %get-tuple-element.106, f32[192]{0:T(256)S(1)} %get-tuple-element.103, ...), channel_id=1, replica_groups=mesh['fsdp'=8,'sp'=4] {'fsdp','sp'}, use_global_device_ids=true, to_apply=%region_71.72 | all-reduce | flops 768 | bytes 6144 | tf_op jit(solution)/shard_map/psum | solution.py:96
  2422.0 6.1 collective-permute-start.30
  2447.4 6.6 collective-permute-start.22
  2479.9 87.4 %all-reduce.42.cloned.1.call-done = (f32[9,128,384]{1,2,0:T(8,128)}, f32[9,128,384]{1,2,0:T(8,128)}, f32[384,192]{0,1:T(8,128)}, f32[384,192]{0,1:T(8,128)}) async-done(((f32[9,128,384]{1,2,0:T(8,128)}, f32[9,128,384]{1,2,0:T(8,128)}, f32[384,192]{0,1:T(8,128)}, f32[384,192]{0,1:T(8,128)}), (f32[9,128,384]{1,2,0:T(8,128)}, f32[9,128,384]{1,2,0:T(8,128)}, f32[384,192]{0,1:T(8,128)}, ...) | async-done | bytes 4128784
  (1246 shorter events, 674.2 us)
Async XLA Ops:
  7.2 962.6 %all-gather.13.cloned.1.call-start = ((), (), s32[]{:S(2)}) async-start(), calls=%async_computation.36 | async-start | bytes 1216512 | tf_op jit(solution)/shard_map/all_gather | solution.py:320
  8.7 739.6 %collective-permute-start.4 = (bf16[1,1,32,512]{3,2,1,0:T(8,128)(2,1)}, bf16[1,1,32,512]{3,2,1,0:T(8,128)(2,1)}, u32[]{:S(2)}, u32[]{:S(2)}) collective-permute-start(bf16[1,1,32,512]{3,2,1,0:T(8,128)(2,1)} %get-tuple-element.204), channel_id=1, source_target_pairs={{0,1},{1,2},{2,3},{4,5},{5,6},{6,7},{8,9},{9,10},{10,11},{12,13},{... | collective-permute-start | bytes 98312 | tf_op jit(solution)/shard_map/ppermute | solution.py:17
  14.2 734.1 %collective-permute-start.5 = (bf16[1,1,32,512]{3,2,1,0:T(8,128)(2,1)}, bf16[1,1,32,512]{3,2,1,0:T(8,128)(2,1)}, u32[]{:S(2)}, u32[]{:S(2)}) collective-permute-start(bf16[1,1,32,512]{3,2,1,0:T(8,128)(2,1)} %get-tuple-element.205), channel_id=1, source_target_pairs={{1,0},{2,1},{3,2},{5,4},{6,5},{7,6},{9,8},{10,9},{11,10},{13,12},{... | collective-permute-start | bytes 98312 | tf_op jit(solution)/shard_map/ppermute | solution.py:20
  18.5 735.7 %collective-permute-start = (bf16[1,1,64,512]{3,2,1,0:T(8,128)(2,1)}, bf16[1,1,64,512]{3,2,1,0:T(8,128)(2,1)S(1)}, u32[]{:S(2)}, u32[]{:S(2)}) collective-permute-start(bf16[1,1,64,512]{3,2,1,0:T(8,128)(2,1)} %get-tuple-element.208), channel_id=1, source_target_pairs={{0,1},{1,2},{2,3},{4,5},{5,6},{6,7},{8,9},{9,10},{10,11},{12,13},{... | collective-permute-start | bytes 196616 | tf_op jit(solution)/shard_map/ppermute | solution.py:17
  23.0 731.3 %collective-permute-start.1 = (bf16[1,1,64,512]{3,2,1,0:T(8,128)(2,1)}, bf16[1,1,64,512]{3,2,1,0:T(8,128)(2,1)S(1)}, u32[]{:S(2)}, u32[]{:S(2)}) collective-permute-start(bf16[1,1,64,512]{3,2,1,0:T(8,128)(2,1)} %get-tuple-element.209), channel_id=1, source_target_pairs={{1,0},{2,1},{3,2},{5,4},{6,5},{7,6},{9,8},{10,9},{11,10},{13,12},{... | collective-permute-start | bytes 196616 | tf_op jit(solution)/shard_map/ppermute | solution.py:20
  180.1 581.0 %all-to-all-start.8 = ((f32[1,16,32,192]{3,1,0,2:T(8,128)}), f32[1,16,32,192]{3,1,0,2:T(8,128)}, u32[]{:S(2)}, u32[]{:S(2)}) async-start(f32[1,16,32,192]{3,1,0,2:T(8,128)} %copy.386), calls=%async_computation.8 | async-start | bytes 1048576 | tf_op jit(solution)/shard_map/all_to_all | solution.py:115
  184.2 812.1 %all-gather.15.cloned.1.call-start = ((), (), s32[]{:S(2)}) async-start(), calls=%async_computation.37 | async-start | bytes 1216512 | tf_op jit(solution)/shard_map/all_gather | solution.py:320
  775.0 18.7 all-to-all-start.9
  793.7 20.0 all-to-all-start.1
  917.2 24.2 all-to-all-start.2
  941.4 23.9 all-to-all-start.10
  965.3 18.6 all-to-all-start.3
  983.9 18.9 all-to-all-start.11
  1090.6 100.3 %collective-permute-start.6 = (bf16[1,1,32,512]{3,2,1,0:T(8,128)(2,1)}, bf16[1,1,32,512]{3,2,1,0:T(8,128)(2,1)S(1)}, u32[]{:S(2)}, u32[]{:S(2)}) collective-permute-start(bf16[1,1,32,512]{3,2,1,0:T(8,128)(2,1)} %get-tuple-element.198), channel_id=1, source_target_pairs={{0,1},{1,2},{2,3},{4,5},{5,6},{6,7},{8,9},{9,10},{10,11},{12,13},{... | collective-permute-start | bytes 98312 | tf_op jit(solution)/shard_map/ppermute | solution.py:17
  1093.0 97.8 %collective-permute-start.7 = (bf16[1,1,32,512]{3,2,1,0:T(8,128)(2,1)S(1)}, bf16[1,1,32,512]{3,2,1,0:T(8,128)(2,1)S(1)}, u32[]{:S(2)}, u32[]{:S(2)}) collective-permute-start(bf16[1,1,32,512]{3,2,1,0:T(8,128)(2,1)S(1)} %get-tuple-element.199), channel_id=1, source_target_pairs={{1,0},{2,1},{3,2},{5,4},{6,5},{7,6},{9,8},{10,9},{11,10},{13,12},{... | collective-permute-start | bytes 98312 | tf_op jit(solution)/shard_map/ppermute | solution.py:20
  1094.3 103.0 %collective-permute-start.2 = (bf16[1,1,64,512]{3,2,1,0:T(8,128)(2,1)}, bf16[1,1,64,512]{3,2,1,0:T(8,128)(2,1)S(1)}, u32[]{:S(2)}, u32[]{:S(2)}) collective-permute-start(bf16[1,1,64,512]{3,2,1,0:T(8,128)(2,1)} %get-tuple-element.200), channel_id=1, source_target_pairs={{0,1},{1,2},{2,3},{4,5},{5,6},{6,7},{8,9},{9,10},{10,11},{12,13},{... | collective-permute-start | bytes 196616 | tf_op jit(solution)/shard_map/ppermute | solution.py:17
  1098.9 99.1 %collective-permute-start.3 = (bf16[1,1,64,512]{3,2,1,0:T(8,128)(2,1)S(1)}, bf16[1,1,64,512]{3,2,1,0:T(8,128)(2,1)}, u32[]{:S(2)}, u32[]{:S(2)}) collective-permute-start(bf16[1,1,64,512]{3,2,1,0:T(8,128)(2,1)S(1)} %get-tuple-element.201), channel_id=1, source_target_pairs={{1,0},{2,1},{3,2},{5,4},{6,5},{7,6},{9,8},{10,9},{11,10},{13,12},{... | collective-permute-start | bytes 196616 | tf_op jit(solution)/shard_map/ppermute | solution.py:20
  1185.2 18.9 all-to-all-start.12
  1204.1 18.6 all-to-all-start.4
  1222.6 23.8 all-to-all-start.13
  1246.4 24.1 all-to-all-start.5
  1366.9 24.2 all-to-all-start.6
  1391.2 23.9 all-to-all-start.14
  1415.1 18.2 all-to-all-start.7
  1436.7 1041.6 %reduce-scatter.17.cloned.1.call-start = ((), (), s32[]{:S(2)}) async-start(), calls=%async_computation.35 | async-start | bytes 2433024 | tf_op jit(solution)/shard_map/reduce_scatter | solution.py:357
  1597.8 29.5 %collective-permute-start.12 = (bf16[1,1,32,512]{3,2,1,0:T(8,128)(2,1)}, bf16[1,1,32,512]{3,2,1,0:T(8,128)(2,1)}, u32[]{:S(2)}, u32[]{:S(2)}) collective-permute-start(bf16[1,1,32,512]{3,2,1,0:T(8,128)(2,1)} %get-tuple-element.194), channel_id=1, source_target_pairs={{0,1},{1,2},{2,3},{4,5},{5,6},{6,7},{8,9},{9,10},{10,11},{12,13},{... | collective-permute-start | bytes 98312 | tf_op jit(solution)/shard_map/ppermute | solution.py:17
  1602.6 24.8 collective-permute-start.13
  1613.5 21.0 collective-permute-start.8
  1621.1 23.4 all-to-all-start.16
  1644.4 24.6 all-to-all-start.24
  1669.0 30.2 %all-to-all-start.17 = ((f32[1,32,16,384]{3,2,0,1:T(8,128)}), f32[1,32,16,384]{3,2,0,1:T(8,128)}, u32[]{:S(2)}, u32[]{:S(2)}) async-start(f32[1,32,16,384]{3,2,0,1:T(8,128)} %copy.413), calls=%async_computation.17 | async-start | bytes 1572864 | tf_op jit(solution)/shard_map/all_to_all | solution.py:119
  1699.2 32.6 %all-to-all-start.25 = ((f32[1,64,8,384]{3,2,0,1:T(8,128)}), f32[1,64,8,384]{3,2,0,1:T(8,128)}, u32[]{:S(2)}, u32[]{:S(2)}) async-start(f32[1,64,8,384]{3,2,0,1:T(8,128)} %copy.436), calls=%async_computation.25 | async-start | bytes 1572864 | tf_op jit(solution)/shard_map/all_to_all | solution.py:119
  1785.6 24.3 all-to-all-start.26
  1809.9 24.2 all-to-all-start.18
  1834.1 18.2 all-to-all-start.27
  1852.3 18.2 all-to-all-start.19
  1969.1 36.2 %collective-permute-start.14 = (bf16[1,1,32,512]{3,2,1,0:T(8,128)(2,1)}, bf16[1,1,32,512]{3,2,1,0:T(8,128)(2,1)}, u32[]{:S(2)}, u32[]{:S(2)}) collective-permute-start(bf16[1,1,32,512]{3,2,1,0:T(8,128)(2,1)} %get-tuple-element.190), channel_id=1, source_target_pairs={{0,1},{1,2},{2,3},{4,5},{5,6},{6,7},{8,9},{9,10},{10,11},{12,13},{... | collective-permute-start | bytes 98312 | tf_op jit(solution)/shard_map/ppermute | solution.py:17
  1971.7 33.7 %collective-permute-start.15 = (bf16[1,1,32,512]{3,2,1,0:T(8,128)(2,1)}, bf16[1,1,32,512]{3,2,1,0:T(8,128)(2,1)}, u32[]{:S(2)}, u32[]{:S(2)}) collective-permute-start(bf16[1,1,32,512]{3,2,1,0:T(8,128)(2,1)} %get-tuple-element.191), channel_id=1, source_target_pairs={{1,0},{2,1},{3,2},{5,4},{6,5},{7,6},{9,8},{10,9},{11,10},{13,12},{... | collective-permute-start | bytes 98312 | tf_op jit(solution)/shard_map/ppermute | solution.py:20
  1974.6 37.9 %collective-permute-start.10 = (bf16[1,1,64,512]{3,2,1,0:T(8,128)(2,1)}, bf16[1,1,64,512]{3,2,1,0:T(8,128)(2,1)}, u32[]{:S(2)}, u32[]{:S(2)}) collective-permute-start(bf16[1,1,64,512]{3,2,1,0:T(8,128)(2,1)} %get-tuple-element.192), channel_id=1, source_target_pairs={{0,1},{1,2},{2,3},{4,5},{5,6},{6,7},{8,9},{9,10},{10,11},{12,13},{... | collective-permute-start | bytes 196616 | tf_op jit(solution)/shard_map/ppermute | solution.py:17
  1979.8 32.7 %collective-permute-start.11 = (bf16[1,1,64,512]{3,2,1,0:T(8,128)(2,1)}, bf16[1,1,64,512]{3,2,1,0:T(8,128)(2,1)S(1)}, u32[]{:S(2)}, u32[]{:S(2)}) collective-permute-start(bf16[1,1,64,512]{3,2,1,0:T(8,128)(2,1)} %get-tuple-element.193), channel_id=1, source_target_pairs={{1,0},{2,1},{3,2},{5,4},{6,5},{7,6},{9,8},{10,9},{11,10},{13,12},{... | collective-permute-start | bytes 196616 | tf_op jit(solution)/shard_map/ppermute | solution.py:20
  1982.7 35.3 %all-to-all-start.20 = ((f32[1,8,64,192]{3,1,0,2:T(8,128)}), f32[1,8,64,192]{3,1,0,2:T(8,128)}, u32[]{:S(2)}, u32[]{:S(2)}) async-start(f32[1,8,64,192]{3,1,0,2:T(8,128)} %copy.422), calls=%async_computation.20 | async-start | bytes 1048576 | tf_op jit(solution)/shard_map/all_to_all | solution.py:115
  1987.8 490.6 %reduce-scatter.15.cloned.1.call-start = ((), (), s32[]{:S(2)}) async-start(), calls=%async_computation.34 | async-start | bytes 2433024 | tf_op jit(solution)/shard_map/reduce_scatter | solution.py:357
  2018.0 23.1 all-to-all-start.28
  2041.2 29.8 %all-to-all-start.21 = ((f32[1,32,16,384]{3,2,0,1:T(8,128)}), f32[1,32,16,384]{3,2,0,1:T(8,128)S(1)}, u32[]{:S(2)}, u32[]{:S(2)}) async-start(f32[1,32,16,384]{3,2,0,1:T(8,128)} %copy.426), calls=%async_computation.21 | async-start | bytes 1572864 | tf_op jit(solution)/shard_map/all_to_all | solution.py:119
  2071.0 31.6 %all-to-all-start.29 = ((f32[1,64,8,384]{3,2,0,1:T(8,128)}), f32[1,64,8,384]{3,2,0,1:T(8,128)}, u32[]{:S(2)}, u32[]{:S(2)}) async-start(f32[1,64,8,384]{3,2,0,1:T(8,128)} %copy.446), calls=%async_computation.29 | async-start | bytes 1572864 | tf_op jit(solution)/shard_map/all_to_all | solution.py:119
  2155.0 24.7 all-to-all-start.22
  2179.8 23.9 all-to-all-start.30
  2221.3 144.4 %all-to-all-start.31 = ((f32[1,64,8,192]{3,2,0,1:T(8,128)}), f32[1,64,8,192]{3,2,0,1:T(8,128)}, u32[]{:S(2)}, u32[]{:S(2)}) async-start(f32[1,64,8,192]{3,2,0,1:T(8,128)} %copy.450), calls=%async_computation.31 | async-start | bytes 1048576 | tf_op jit(solution)/shard_map/all_to_all | solution.py:157
  2225.5 341.9 %all-reduce.42.cloned.1.call-start = ((), (), s32[]{:S(2)}) async-start(), calls=%async_computation.38 | async-start | bytes 8257536
  2323.4 20.2 collective-permute-start.46
  2324.7 20.2 collective-permute-start.45
  2326.0 22.6 collective-permute-start.44
  2331.9 23.4 collective-permute-start.43
  2338.7 19.3 collective-permute-start.42
  2348.6 63.7 %collective-permute-start.38 = (f32[192,16]{0,1:T(8,128)S(1)}, f32[192,16]{0,1:T(8,128)S(1)}, u32[]{:S(2)}, u32[]{:S(2)}) collective-permute-start(f32[192,16]{0,1:T(8,128)S(1)} %get-tuple-element.177), channel_id=1, source_target_pairs={{0,7},{1,8},{2,9},{3,10},{4,11},{5,12},{6,13},{7,14},{8,15},{9,16}... | collective-permute-start | bytes 36872
  2355.2 59.0 %collective-permute-start.37 = (f32[192,16]{0,1:T(8,128)S(1)}, f32[192,16]{0,1:T(8,128)S(1)}, u32[]{:S(2)}, u32[]{:S(2)}) collective-permute-start(f32[192,16]{0,1:T(8,128)S(1)} %get-tuple-element.177), channel_id=1, source_target_pairs={{0,6},{1,7},{2,8},{3,9},{4,10},{5,11},{6,12},{7,13},{8,14},{9,15},... | collective-permute-start | bytes 36872
  2358.0 59.3 %collective-permute-start.36 = (f32[192,16]{0,1:T(8,128)S(1)}, f32[192,16]{0,1:T(8,128)S(1)}, u32[]{:S(2)}, u32[]{:S(2)}) collective-permute-start(f32[192,16]{0,1:T(8,128)S(1)} %get-tuple-element.177), channel_id=1, source_target_pairs={{0,5},{1,6},{2,7},{3,8},{4,9},{5,10},{6,11},{7,12},{8,13},{9,14},{... | collective-permute-start | bytes 36872
  2359.4 62.7 %collective-permute-start.35 = (f32[192,16]{0,1:T(8,128)S(1)}, f32[192,16]{0,1:T(8,128)S(1)}, u32[]{:S(2)}, u32[]{:S(2)}) collective-permute-start(f32[192,16]{0,1:T(8,128)S(1)} %get-tuple-element.177), channel_id=1, source_target_pairs={{0,4},{1,5},{2,6},{3,7},{4,8},{5,9},{6,10},{7,11},{8,12},{9,13},{1... | collective-permute-start | bytes 36872
  2362.0 46.8 %collective-permute-start.39 = (f32[192,12]{0,1:T(8,128)S(1)}, f32[192,12]{0,1:T(8,128)S(1)}, u32[]{:S(2)}, u32[]{:S(2)}) collective-permute-start(f32[192,12]{0,1:T(8,128)S(1)} %slice.1430), channel_id=1, source_target_pairs={{0,8},{1,9},{2,10},{3,11},{4,12},{5,13},{6,14},{7,15},{8,16},{9,17... | collective-permute-start | bytes 27656
  2408.9 19.3 collective-permute-start.34
  2414.3 18.4 collective-permute-start.32
  2422.0 20.9 collective-permute-start.30
  2432.7 21.3 collective-permute-start.27
  2438.0 18.9 collective-permute-start.26
  (299 other events, 8315.1 us)
Sparse Core Ops, SparseCore 0:
  17.1 56.3 all-gather.12
  188.5 55.3 all-gather.14
  1613.6 148.5 reduce-scatter.16
  2005.5 148.7 reduce-scatter.14
  2422.1 145.1 all-reduce.41
where the time goes:
time: 2600 us; the launch traced here: 2580 us
  blocking collectives  1430 us (55%)
  waiting for transfers between devices  403 us (16%)
  starting transfers between devices  278 us (11%)
  local copies, waits for them, and re-layouts  182 us (7%)
  matrix products  168 us (6%)
  other arithmetic  97.6 us (4%)
    psum x6, blocking collectives, normalize(): lax.psum(jnp.sum(squared, axis=(0, 1, 2)), ('fsdp', 'sp')) / positions  250 us
    psum x6, blocking collectives, normalize(): center = lax.psum(local_sum, ('fsdp', 'sp')) / positions  240 us
    psum x6, blocking collectives, norm_back(): lax.psum((jnp.sum(grad_out, axis=(0, 1, 2)), jnp.sum(grad_out * normed, a...  236 us
    all_gather x2, blocking collectives, per_device(): lax.all_gather(to_global[section_index], ('fsdp', 'sp'), axis=2, tiled=True)  168 us
    all_gather x2, blocking collectives, per_device(): lax.all_gather(freq_weight[section_index], ('fsdp', 'sp'), axis=0, tiled=...  149 us
    all_gather x2, blocking collectives, per_device(): lax.all_gather(expand_weight[section_index], ('fsdp', 'sp'), axis=1, tile...  148 us
    all_gather x2, blocking collectives, per_device(): lax.all_gather(reduce_weight[section_index], ('fsdp', 'sp'), axis=0, tile...  143 us
    all_to_all x8, waiting for transfers between devices, to_spectrum(): lax.all_to_all(columns, 'sp', split_axis=1, concat_axis=2, tiled=True)  121 us
  transfers between devices with their start and end apart: 85, of which 30 were waited for; matrix products, arithmetic and copies ran while one was open for 19% of the time, Pallas kernels for 0%

commit v1 on v0

v1 whole, which is shorter than its diff:
```python
import math

import jax
import jax.numpy as jnp
import numpy as np
from jax import lax
from jax.sharding import Mesh, PartitionSpec as P

EPS = 1e-05
LINE = ("c", "k", "z", "e")
KIND = ("g", "c", "z", "e")
PART = ("c", "e")
ALL = ("g", "c", "k", "z", "e")
f32 = jnp.float32
bf16 = jnp.bfloat16


def routes(e_n):
    s_n = 4 * e_n
    count = 2 * s_n
    edges = []
    for c in range(2):
        for s in range(s_n):
            src = c * s_n + s
            for half in range(2):
                target = half * s_n + (0 * 2 + c) * e_n + s // 4
                edges.append((src, half, target, s % 4))
            part = s // 2
            for half in range(2):
                target = (part // e_n) * s_n + (1 * 2 + c) * e_n + part % e_n
                edges.append((src, 2 + half, target, (s % 2) * 2 + half))
    rounds = []
    left = list(edges)
    for _ in range(4):
        owner = {}

        def augment(src, seen):
            for edge in left:
                if edge[0] == src and edge[2] not in seen:
                    seen.add(edge[2])
                    if edge[2] not in owner or augment(owner[edge[2]][0], seen):
                        owner[edge[2]] = edge
                        return True
            return False

        for src in range(count):
            assert augment(src, set())
        chosen = list(owner.values())
        for edge in chosen:
            left.remove(edge)
        pairs = [(edge[0], edge[2]) for edge in chosen]
        sent = np.zeros(count, np.int32)
        slot = np.zeros(count, np.int32)
        for edge in chosen:
            sent[edge[0]] = edge[1]
            slot[edge[2]] = edge[3]
        rounds.append((pairs, sent, slot))
    return rounds


def transform_tables(e_n, land_shape, port_shape):
    parts = 2 * e_n
    shapes = (land_shape, port_shape)
    most = max(rows * (cols // 2 + 1) for rows, cols in shapes)
    per_part = -(-most // (16 * parts)) * 16
    forward, inverse, weight, counts = [], [], [], []
    for kind, (rows, cols) in enumerate(shapes):
        half = cols // 2 + 1
        total = rows * half
        point = np.arange(per_part * parts)
        valid = point < total
        kr, f = point // half, point % half
        tiles = []
        for part in range(parts):
            c, e = part // e_n, part % e_n
            if kind == 0:
                h = np.arange(rows // e_n) + e * (rows // e_n)
                w = np.arange(cols // 2) + c * (cols // 2)
            else:
                h = np.arange(rows // parts) + part * (rows // parts)
                w = np.arange(cols)
            tiles.append((np.repeat(h, len(w)), np.tile(w, len(h))))
        cell_h = np.concatenate([tile[0] for tile in tiles])
        cell_w = np.concatenate([tile[1] for tile in tiles])
        size = rows * cols
        phase = (kr[:, None] * cell_h[None, :] * cols + f[:, None] * cell_w[None, :] * rows) % size
        angle = phase * (2.0 * math.pi / size)
        table = np.stack([np.cos(angle), -np.sin(angle)]) * valid[None, :, None]
        table = table.astype(np.float32).astype(jnp.bfloat16)
        cells = size // parts
        factor = np.where((f == 0) | (2 * f == cols), 1.0, 2.0) * valid
        counts.append([int(valid[p * per_part : (p + 1) * per_part].sum()) for p in range(parts)])
        for part in range(parts):
            order = [(part + step) % parts for step in range(parts)]
            own_points = slice(part * per_part, (part + 1) * per_part)
            own_cells = slice(part * cells, (part + 1) * cells)
            forward.append(
                np.concatenate([table[:, own_points, q * cells : (q + 1) * cells] for q in order], axis=2)
            )
            back = np.concatenate([table[:, q * per_part : (q + 1) * per_part, own_cells] for q in order], axis=1)
            inverse.append(np.ascontiguousarray(back.transpose(0, 2, 1)))
            weight.append(factor[own_points].astype(np.float32))
    return np.stack(forward), np.stack(inverse), np.stack(weight), np.asarray(counts, np.int32)


def pick(table, index):
    return lax.dynamic_index_in_dim(jnp.asarray(table), index, 0, keepdims=False)


def to_tile(land, port, rounds):
    rows = land.shape[1]
    wide = port.shape[2]
    units = jnp.stack([land[0, :, :wide], land[0, :, wide:], port[0, :rows], port[0, rows:]])
    me = lax.axis_index(LINE)
    got = []
    for pairs, sent, _ in rounds:
        got.append(lax.ppermute(pick(units, pick(sent, me)), LINE, pairs))
    got = jnp.stack(got)
    slots = np.stack([slot for _, _, slot in rounds], axis=1)
    order = pick(np.argsort(slots, axis=1).astype(np.int32), me)
    return jnp.concatenate([pick(got, order[i]) for i in range(4)], axis=0)


def from_tile(tile, rounds):
    rows = tile.shape[0] // 4
    units = tile.reshape((4, rows) + tile.shape[1:])
    me = lax.axis_index(LINE)
    got = []
    for pairs, _, slot in rounds:
        got.append(lax.ppermute(pick(units, pick(slot, me)), LINE, [(b, a) for a, b in pairs]))
    got = jnp.stack(got)
    sents = np.stack([sent for _, sent, _ in rounds], axis=1)
    order = pick(np.argsort(sents, axis=1).astype(np.int32), me)
    parts = [pick(got, order[i]) for i in range(4)]
    land = jnp.concatenate(parts[:2], axis=1)
    port = jnp.concatenate(parts[2:], axis=0)
    return land[None], port[None]


def share(block):
    parts = lax.axis_size(PART)
    pieces = [block]
    for step in range(1, parts):
        pieces.append(lax.ppermute(block, PART, [((p + step) % parts, p) for p in range(parts)]))
    return jnp.concatenate(pieces, axis=0)


def with_halo(tile):
    rows, cols, channels = tile.shape
    c, k = lax.axis_index("c"), lax.axis_index("k")
    e_n = lax.axis_size("e")
    swap = [(0, 1), (1, 0)]
    zero = jnp.zeros((), tile.dtype)
    col_edge = jnp.where(c == 0, tile[:, -1], tile[:, 0])
    if e_n == 1:
        row_edge = jnp.where(c == 0, tile[-1], tile[0])
        got = lax.ppermute(jnp.where(k == 0, col_edge, row_edge), "c", swap)
        left = jnp.where((k == 0) & (c == 1), got, zero)
        right = jnp.where((k == 0) & (c == 0), got, zero)
        top = jnp.where((k == 1) & (c == 1), got, zero)
        bottom = jnp.where((k == 1) & (c == 0), got, zero)
        top = jnp.pad(top, ((1, 1), (0, 0)))
        bottom = jnp.pad(bottom, ((1, 1), (0, 0)))
        wide = jnp.concatenate([left[:, None], tile, right[:, None]], axis=1)
    else:
        got = lax.ppermute(col_edge, "c", swap)
        left = jnp.where((k == 0) & (c == 1), got, zero)
        right = jnp.where((k == 0) & (c == 0), got, zero)
        wide = jnp.concatenate([left[:, None], tile, right[:, None]], axis=1)
        ahead = []
        for cc in range(2):
            for e in range(e_n):
                if e + 1 < e_n:
                    ahead.append(((cc * 2 + 0) * e_n + e, (cc * 2 + 0) * e_n + e + 1))
                p = cc * e_n + e + 1
                if p < 2 * e_n:
                    ahead.append(((cc * 2 + 1) * e_n + e, ((p // e_n) * 2 + 1) * e_n + p % e_n))
        axes = ("c", "k", "e")
        top = lax.ppermute(wide[-1], axes, ahead)
        bottom = lax.ppermute(wide[0], axes, [(b, a) for a, b in ahead])
    return jnp.concatenate([top[None], wide, bottom[None]], axis=0)


def spread(values, axes):
    count = lax.axis_size(axes)
    return lax.all_to_all(jnp.broadcast_to(values[None], (count,) + values.shape), axes, 0, 0, tiled=True)


def norm_stats(values, counts, mask=None):
    me = lax.axis_index(KIND)
    own = counts[me]
    local_sum = jnp.sum(values, axis=0)
    centered = values - local_sum / own
    if mask is not None:
        centered = centered * mask
    local_square = jnp.sum(centered * centered, axis=0)
    every = spread(jnp.stack([local_sum, local_square]), KIND)
    total = jnp.sum(counts)
    mean = jnp.sum(every[:, 0], axis=0) / total
    apart = every[:, 0] / counts[:, None] - mean
    square = jnp.sum(every[:, 1] + counts[:, None] * apart * apart, axis=0)
    return mean, lax.rsqrt(square / total + EPS)


def gelu(v):
    return 0.5 * v * (1.0 + jnp.tanh(math.sqrt(2.0 / math.pi) * (v + 0.044715 * v * v * v)))


def gelu_slope(v):
    k = math.sqrt(2.0 / math.pi)
    t = jnp.tanh(k * (v + 0.044715 * v * v * v))
    return 0.5 * (1.0 + t) + 0.5 * v * (1.0 - t * t) * (k * (1.0 + 3.0 * 0.044715 * v * v))


def norm_back(q, normed, gain, inv, total):
    every = spread(jnp.stack([jnp.sum(q, axis=0), jnp.sum(q * normed, axis=0)]), KIND)
    sums = jnp.sum(every, axis=0)
    return gain * inv * (q - sums[0] / total - normed * (sums[1] / total)), sums


def dot(a, b):
    return lax.dot_general(a, b, (((1,), (0,)), ((), ())), preferred_element_type=f32)


def dot_t(a, b):
    return lax.dot_general(a, b, (((1,), (1,)), ((), ())), preferred_element_type=f32)


def outer(a, b):
    return lax.dot_general(a, b, (((0,), (0,)), ((), ())), preferred_element_type=f32)


def unfold(padded):
    rows, cols, channels = padded.shape[0] - 2, padded.shape[1] - 2, padded.shape[2]
    return jnp.concatenate(
        [padded[t // 3 : t // 3 + rows, t % 3 : t % 3 + cols].reshape(rows * cols, channels) for t in range(9)],
        axis=1,
    )


def gather_rows(shard):
    return lax.all_gather(shard, ALL, tiled=True)


def per_device(plan, *args):
    (
        land,
        port,
        to_local,
        to_global,
        reduce_weight,
        freq_weight,
        expand_weight,
        spec_gain,
        spec_bias,
        freq_gain,
        freq_bias,
        out_gain,
        out_bias,
        cot_land,
        cot_port,
    ) = args
    rounds, forward_table, inverse_table, weight_table, point_counts, cells_of_kind = plan
    sections = to_local.shape[0]
    devices = lax.axis_size(ALL)
    own_in = to_local.shape[2]
    own_out = to_global.shape[3]
    narrow = to_local.shape[3]
    channels = own_in * devices
    broad = channels - narrow
    half = reduce_weight.shape[2]
    k, part = lax.axis_index("k"), lax.axis_index(PART)
    variant = k * lax.axis_size(PART) + part
    g_n, z_n, e_n = lax.axis_size("g"), lax.axis_size("z"), lax.axis_size("e")

    x = to_tile(land, port, rounds)
    rows, cols = x.shape[:2]
    cells = rows * cols
    size = cells * lax.axis_size(PART)
    scale = 1.0 / math.sqrt(size)
    maps = g_n * z_n

    small, kernels = [], []
    for s in range(sections):
        packed = jnp.concatenate(
            [freq_weight[s], reduce_weight[s], jnp.transpose(expand_weight[s])], axis=1
        )
        full = gather_rows(packed)
        wide = full.shape[1] - 2 * half
        small.append((full[:, wide : wide + half], full[:, :wide], full[:, wide + half :]))
    for s in range(sections):
        taps_local = jnp.reshape(to_local[s], (1, 9 * own_in, narrow))
        taps_global = jnp.transpose(to_global[s], (2, 0, 1)).reshape(1, own_out * 9, narrow)
        full = gather_rows(jnp.concatenate([taps_local, taps_global], axis=1))
        local_kernel = full[:, : 9 * own_in].reshape(devices, 9, own_in, narrow)
        local_kernel = jnp.transpose(local_kernel, (1, 0, 2, 3)).reshape(9, channels, narrow)
        global_kernel = full[:, 9 * own_in :].reshape(devices * own_out, 9 * narrow)
        kernels.append((local_kernel, global_kernel))
    cot = to_tile(cot_land, cot_port, rounds)

    forward = pick(forward_table, variant)
    inverse = pick(inverse_table, variant)
    factor = pick(weight_table, variant)[:, None]
    mask = jnp.where(factor > 0.0, 1.0, 0.0)
    cell_counts = jnp.full((maps * 2 * e_n,), cells, f32)
    by_part = pick(point_counts, k).astype(f32)
    freq_counts = jnp.broadcast_to(by_part.reshape(1, 2, 1, e_n), (g_n, 2, z_n, e_n)).reshape(-1)
    cell_total = float(maps * size)
    freq_total = jnp.sum(freq_counts)

    def to_spectrum(values):
        whole = share(values.astype(bf16))
        return dot(forward[0], whole) * scale, dot(forward[1], whole) * scale

    def from_spectrum(values):
        whole = share(values.astype(bf16))
        return (dot(inverse[0], whole[:, :half]) + dot(inverse[1], whole[:, half:])) * scale

    state = x
    kept = []
    for s in range(sections):
        reduce_kernel, freq_kernel, expand_t = small[s]
        local_kernel, global_t = kernels[s]
        low = state.astype(bf16)
        flat = low.reshape(cells, channels)
        padded = with_halo(low)
        reduced = dot(flat[:, narrow:], reduce_kernel)
        mean_1, inv_1 = norm_stats(reduced, cell_counts)
        normed_1 = (reduced - mean_1) * inv_1
        act_1 = normed_1 * spec_gain[s] + spec_bias[s]
        hidden = gelu(act_1)
        real, imag = to_spectrum(hidden)
        real, imag = real.astype(bf16), imag.astype(bf16)
        mixed = dot(real, freq_kernel[:half]) + dot(imag, freq_kernel[half:])
        mean_2, inv_2 = norm_stats(mixed, freq_counts, mask)
        normed_2 = (mixed - mean_2) * inv_2
        act_2 = normed_2 * freq_gain[s] + freq_bias[s]
        returned = from_spectrum(gelu(act_2) * factor)
        summed = (hidden + returned).astype(bf16)
        local_pre = dot(unfold(padded), local_kernel.reshape(9 * channels, narrow))
        global_pre = dot_t(unfold(padded[..., :narrow]), global_t)
        both = jnp.concatenate([local_pre, global_pre + dot_t(summed, expand_t)], axis=1)
        mean_3, inv_3 = norm_stats(both, cell_counts)
        normed_3 = (both - mean_3) * inv_3
        act_3 = normed_3 * out_gain[s] + out_bias[s]
        state = gelu(act_3).reshape(rows, cols, channels)
        kept.append(
            (padded, flat, normed_1, inv_1, act_1, real, imag, normed_2, inv_2, act_2, summed, normed_3, inv_3, act_3)
        )
    land_out, port_out = from_tile((x.astype(f32) + state).astype(bf16), rounds)

    grad = cot.astype(f32).reshape(cells, channels)
    weight_shares = [None] * sections
    norm_sums = [None] * sections
    for s in reversed(range(sections)):
        (padded, flat, normed_1, inv_1, act_1, real, imag, normed_2, inv_2, act_2, summed, normed_3, inv_3, act_3) = kept[s]
        reduce_kernel, freq_kernel, expand_t = small[s]
        local_kernel, global_t = kernels[s]
        grad_pre, sums_3 = norm_back(gelu_slope(act_3) * grad, normed_3, out_gain[s], inv_3, cell_total)
        grad_low = grad_pre.astype(bf16)
        grad_local, grad_global = grad_low[:, :narrow], grad_low[:, narrow:]
        grad_summed = dot(grad_global, expand_t)
        freq_real, freq_imag = to_spectrum(grad_summed)
        grad_freq = jnp.concatenate([freq_real, freq_imag], axis=1) * factor
        grad_mixed, sums_2 = norm_back(gelu_slope(act_2) * grad_freq, normed_2, freq_gain[s], inv_2, freq_total)
        mixed_low = grad_mixed.astype(bf16)
        grad_hidden = grad_summed + from_spectrum(dot_t(mixed_low, freq_kernel) * mask)
        grad_reduced, sums_1 = norm_back(gelu_slope(act_1) * grad_hidden, normed_1, spec_gain[s], inv_1, cell_total)
        reduced_low = grad_reduced.astype(bf16)
        into_global = dot_t(reduced_low, reduce_kernel)

        grad_padded = with_halo(grad_low.reshape(rows, cols, channels))
        back_local = jnp.transpose(local_kernel[::-1], (0, 2, 1)).reshape(9 * narrow, channels)
        taps_t = global_t.reshape(broad, 9, narrow)
        back_global = jnp.transpose(taps_t[:, ::-1], (1, 0, 2)).reshape(9 * broad, narrow)
        grad_input = dot(unfold(grad_padded[..., :narrow]), back_local)
        into_local = dot(unfold(grad_padded[..., narrow:]), back_global)
        grad = grad_input + jnp.concatenate([into_local, into_global], axis=1)

        local_grad = outer(unfold(padded), grad_local)
        global_grad = outer(grad_global, unfold(padded[..., :narrow]))
        expand_grad = outer(grad_global, summed)
        freq_grad = jnp.concatenate([outer(real, mixed_low), outer(imag, mixed_low)], axis=0)
        reduce_grad = outer(flat[:, narrow:], reduced_low)
        local_grad = jnp.transpose(local_grad.reshape(9, devices, own_in, narrow), (1, 0, 2, 3))
        local_grad = local_grad.reshape(devices, 9 * own_in, narrow)
        global_grad = global_grad.reshape(devices, own_out * 9, narrow)
        others = jnp.concatenate([freq_grad, reduce_grad, expand_grad], axis=1)
        others = others.reshape(devices, own_out, others.shape[1])
        owned_kernels = owned(jnp.concatenate([local_grad, global_grad], axis=1))
        owned_others = owned(others)
        weight_shares[s] = (
            owned_kernels[: 9 * own_in].reshape(9, own_in, narrow),
            jnp.transpose(owned_kernels[9 * own_in :].reshape(own_out, 9, narrow), (1, 2, 0)),
            owned_others[:, 2 * half : 3 * half],
            owned_others[:, : 2 * half],
            jnp.transpose(owned_others[:, 3 * half :]),
        )
        norm_sums[s] = (sums_1, sums_2, sums_3)
    land_grad, port_grad = from_tile(
        (cot.astype(f32) + grad.reshape(rows, cols, channels)).astype(bf16), rounds
    )
    flat_sums = jnp.concatenate([item.reshape(-1) for s in range(sections) for item in norm_sums[s]])
    flat_sums = flat_sums + lax.ppermute(flat_sums, "k", [(0, 1), (1, 0)])
    gains = [[] for _ in range(6)]
    offset = 0
    for s in range(sections):
        for index, width in enumerate((half, 2 * half, channels)):
            bias_sum = flat_sums[offset : offset + width]
            gain_sum = flat_sums[offset + width : offset + 2 * width]
            offset += 2 * width
            gains[2 * index].append(gain_sum)
            gains[2 * index + 1].append(bias_sum)
    stacked = [jnp.stack([weight_shares[s][i] for s in range(sections)]) for i in range(5)]
    return (land_out, port_out, land_grad, port_grad, *stacked, *[jnp.stack(item) for item in gains])


def owned(shares):
    shape = shares.shape[1:]
    g_n, c_n = lax.axis_size("g"), lax.axis_size("c")
    rest = lax.axis_size(("k", "z", "e"))
    low = shares.astype(bf16).reshape((g_n * c_n, rest) + shape)
    first = lax.all_to_all(low, ("g", "c"), 0, 0, tiled=True)
    first = jnp.sum(first.astype(f32), axis=0).astype(bf16)
    second = lax.all_to_all(first, ("k", "z", "e"), 0, 0, tiled=True)
    return jnp.sum(second.astype(f32), axis=0)


def solution(mesh):
    f_n, s_n = mesh.shape["fsdp"], mesh.shape["sp"]
    e_n = s_n // 4
    fine = Mesh(np.asarray(mesh.devices).reshape(f_n // 2, 2, 2, 2, e_n), ALL)
    maps = P(("g", "c"), ("k", "z", "e"), None, None)
    split = ALL

    def whole(*args):
        land, port = args[0], args[1]
        plan = (
            routes(e_n),
            *transform_tables(e_n, land.shape[1:3], port.shape[1:3]),
            land.shape[1] * land.shape[2],
        )
        weights = (
            P(None, None, split, None),
            P(None, None, None, split),
            P(None, split, None),
            P(None, split, None),
            P(None, None, split),
        )
        return jax.shard_map(
            lambda *local: per_device(plan, *local),
            mesh=fine,
            in_specs=(maps, maps, *weights, P(), P(), P(), P(), P(), P(), maps, maps),
            out_specs=(maps, maps, maps, maps, *weights, P(), P(), P(), P(), P(), P()),
            check_vma=False,
        )(*args)

    return whole
```

time: 2600 us -> 812 us (0.31)
  blocking collectives: 1430 us -> 153 us
  waiting for transfers between devices: 403 us -> 94.1 us
  starting transfers between devices: 278 us -> 135 us
  matrix products: 168 us -> 124 us
  between operations: 19.9 us -> 49.4 us
    psum x18 -> x0, blocking collectives: 725 us -> none  [the longest x6 250 us: normalize(): lax.psum(jnp.sum(squared, axis=(0, 1, 2)), ('fsdp', 'sp')) / positions]
    all_gather x8 -> x2, blocking collectives: 608 us -> 153 us  [gather_rows(): return lax.all_gather(shard, ALL, tiled=True)]
    all_to_all x32 -> x20, waiting for transfers between devices: 313 us -> 91.7 us  [the longest x4 33 us: owned(): second = lax.all_to_all(first, ('k', 'z', 'e'), 0, 0, tiled=True)]
    unnamed x1 -> x0, blocking collectives: 97.8 us -> none
    unnamed x33 -> x0, starting transfers between devices: 96.4 us -> none
    unnamed x38 -> x2, waiting for transfers between devices: 89.6 us -> 0.03 us
    all_to_all x32 -> x20, starting transfers between devices: 136 us -> 76.2 us  [the longest x12 47.3 us: spread(): lax.all_to_all(jnp.broadcast_to(values[None], (count,) + values.shape), a...]
    dot_general x156 -> x50, matrix products: 168 us -> 124 us  [the longest x30 82.3 us: dot(): lax.dot_general(a, b, (((1,), (0,)), ((), ())), preferred_element_type=f32)]
  transfers between devices with their start and end apart: 85 -> 51, of which waited for: 30 -> 16; matrix products, arithmetic and copies ran while one was open for 19% -> 34% of each run, Pallas kernels for 0% -> 0%
where the time goes in v1:
time: 812 us; the launch traced here: 802 us
  local copies, waits for them, and re-layouts  162 us (20%)
  blocking collectives  153 us (19%)
  starting transfers between devices  135 us (17%)
  matrix products  124 us (15%)
  waiting for transfers between devices  94.1 us (12%)
  other arithmetic  84.3 us (10%)
  between operations  49.4 us (6%)
    all_gather x2, blocking collectives, gather_rows(): return lax.all_gather(shard, ALL, tiled=True)  153 us
    dot_general x30, matrix products, dot(): lax.dot_general(a, b, (((1,), (0,)), ((), ())), preferred_element_type=f32)  82.3 us
    all_to_all x12, starting transfers between devices, spread(): lax.all_to_all(jnp.broadcast_to(values[None], (count,) + values.shape), a...  47.3 us
    unnamed x401, local copies, waits for them, and re-layouts  39.3 us
    all_to_all x4, waiting for transfers between devices, owned(): second = lax.all_to_all(first, ('k', 'z', 'e'), 0, 0, tiled=True)  33 us
    all_to_all x4, waiting for transfers between devices, owned(): first = lax.all_to_all(low, ('g', 'c'), 0, 0, tiled=True)  32.1 us
    ppermute x8, starting transfers between devices, from_tile(): lax.ppermute(pick(units, pick(slot, me)), LINE, [(b, a) for a, b in pairs])  29.7 us
    dot_general x12, matrix products, outer(): lax.dot_general(a, b, (((0,), (0,)), ((), ())), preferred_element_type=f32)  26.8 us
  transfers between devices with their start and end apart: 51, of which 16 were waited for; matrix products, arithmetic and copies ran while one was open for 34% of the time, Pallas kernels for 0%

profile of v1, /device:TPU:0, one launch (start us, length us, event | category | flops | bytes accessed | tf_op | source)
XLA Modules:
  0.0 801.8 jit_solution(4202646079535492780)
XLA Ops:
  24.1 6.1 collective-permute-start
  32.1 3.0 collective-permute-start.2
  37.8 5.0 collective-permute-start.14
  47.9 82.8 %all-gather = bf16[32,12,768]{2,1,0:T(8,128)(2,1)S(1)} all-gather(bf16[1,12,768]{2,1,0:T(8,128)(2,1)S(1)} %maximum_bitcast_fusion.4), channel_id=1, replica_groups=mesh['g'=4,'c'=2,'k'=2,'z'=2,'e'=1] {'g','c','k','z','e'}, dimensions={0}, use_global_device_ids=true | all-gather | bytes 608256 | tf_op jit(solution)/shard_map/all_gather | solution.py:242
  130.8 70.4 %all-gather.1 = bf16[32,12,768]{2,1,0:T(8,128)(2,1)S(1)} all-gather(bf16[1,12,768]{2,1,0:T(8,128)(2,1)S(1)} %maximum_bitcast_fusion.5), channel_id=1, replica_groups=mesh['g'=4,'c'=2,'k'=2,'z'=2,'e'=1] {'g','c','k','z','e'}, dimensions={0}, use_global_device_ids=true | all-gather | bytes 608256 | tf_op jit(solution)/shard_map/all_gather | solution.py:242
  247.8 3.7 all-to-all-start
  284.5 4.0 all-to-all-start.1
  290.2 3.9 all-to-all-done.1
  306.0 3.5 fusion.77
  313.6 3.5 fusion.286
  322.2 3.7 all-to-all-start.2
  333.9 3.0 reshape_reshape.15
  341.9 2.9 reshape_reshape.14
  344.9 4.9 rev.15
  352.4 4.9 rev.13
  365.4 2.9 pad_maximum_fusion.5
  379.1 4.2 all-to-all-start.3
  391.2 7.1 fusion.287
  413.2 4.9 all-to-all-start.4
  418.8 4.8 all-to-all-done.4
  427.4 3.1 fusion.288
  439.0 3.5 all-to-all-start.5
  449.5 4.1 fusion.237
  454.2 4.4 all-to-all-start.6
  458.7 3.3 fusion.28
  463.0 6.9 collective-permute-start.10
  472.1 4.5 collective-permute-start.12
  476.6 3.8 collective-permute-start.11
  480.5 3.2 fusion.51
  483.7 6.7 convolution_convert_fusion
  490.5 3.9 convolution_convert_fusion.2
  506.4 2.9 copy.827
  521.7 3.1 pad_maximum_fusion.10
  532.9 3.7 all-to-all-start.7
  538.9 3.4 all-to-all-done.7
  550.2 4.0 fusion.241
  554.9 3.7 all-to-all-start.8
  559.5 4.6 all-to-all-done.8
  570.6 6.9 fusion.236
  578.1 3.5 all-to-all-start.9
  587.1 4.2 all-to-all-start.18
  594.0 6.4 convolution_convert_fusion.1
  600.4 3.9 convolution_convert_fusion.3
  611.3 2.9 copy.824
  633.5 4.2 all-to-all-start.10
  643.3 3.3 all-to-all-start.19
  647.3 5.2 all-to-all-done.19
  652.5 3.6 all-to-all-start.14
  665.5 4.0 fusion.240
  669.6 12.8 %all-to-all-done.14 = bf16[8,4,252,128]{3,1,2,0:T(4,128)(2,1)S(1)} async-done(((bf16[8,4,252,128]{3,1,2,0:T(4,128)(2,1)}), bf16[8,4,252,128]{3,1,2,0:T(4,128)(2,1)S(1)}, u32[]{:S(2)}, u32[]{:S(2)}) %all-to-all-start.14) | async-done | bytes 2064416 | tf_op jit(solution)/shard_map/all_to_all | solution.py:423
  683.0 3.7 all-to-all-start.11
  689.3 2.9 all-to-all-done.11
  698.1 3.5 all-to-all-start.16
  701.7 3.6 maximum_add_fusion.1
  706.7 4.2 collective-permute-start.24
  713.4 4.3 collective-permute-start.26
  719.8 3.4 all-to-all-start.15
  724.2 17.2 %all-to-all-done.15 = bf16[4,252,128]{2,1,0:T(8,128)(2,1)S(1)} async-done(((bf16[4,252,128]{2,1,0:T(8,128)(2,1)}), bf16[4,252,128]{2,1,0:T(8,128)(2,1)S(1)}, u32[]{:S(2)}, u32[]{:S(2)}) %all-to-all-start.15) | async-done | bytes 258080 | tf_op jit(solution)/shard_map/all_to_all | solution.py:425
  741.4 3.3 all-to-all-start.17
  745.3 5.2 all-to-all-done.17
  750.5 4.1 all-to-all-start.12
  761.6 19.3 %all-to-all-done.12 = bf16[8,4,252,128]{3,1,2,0:T(4,128)(2,1)S(1)} async-done(((bf16[8,4,252,128]{3,1,2,0:T(4,128)(2,1)}), bf16[8,4,252,128]{3,1,2,0:T(4,128)(2,1)S(1)}, u32[]{:S(2)}, u32[]{:S(2)}) %all-to-all-start.12) | async-done | bytes 2064416 | tf_op jit(solution)/shard_map/all_to_all | solution.py:423
  782.8 3.4 all-to-all-start.13
  787.5 5.4 all-to-all-done.13
  (823 shorter events, 305.7 us)
Async XLA Ops:
  7.2 302.4 %all-gather.5.cloned.1.call-start = ((), (), s32[]{:S(2)}) async-start(), calls=%async_computation.20 | async-start | bytes 2162688 | tf_op jit(solution)/shard_map/all_gather | solution.py:242
  9.7 317.7 %all-gather.7.cloned.1.call-start = ((), (), s32[]{:S(2)}) async-start(), calls=%async_computation.21 | async-start | bytes 2162688 | tf_op jit(solution)/shard_map/all_gather | solution.py:242
  24.1 210.3 %collective-permute-start = (bf16[8,32,512]{2,1,0:T(8,128)(2,1)S(1)}, bf16[8,32,512]{2,1,0:T(8,128)(2,1)S(1)}, u32[]{:S(2)}, u32[]{:S(2)}) collective-permute-start(bf16[8,32,512]{2,1,0:T(8,128)(2,1)S(1)} %get-tuple-element.287), channel_id=1, source_target_pairs={{3,0},{1,4},{0,2},{2,6},{7,1},{5,5},{4,3},{6,7},{11,8},{9,12},{8,1... | collective-permute-start | bytes 786440 | tf_op jit(solution)/shard_map/ppermute | solution.py:117
  30.2 206.1 %collective-permute-start.3 = (bf16[8,32,512]{2,1,0:T(8,128)(2,1)S(1)}, bf16[8,32,512]{2,1,0:T(8,128)(2,1)}, u32[]{:S(2)}, u32[]{:S(2)}) collective-permute-start(bf16[8,32,512]{2,1,0:T(8,128)(2,1)S(1)} %get-tuple-element.288), channel_id=1, source_target_pairs={{0,2},{1,0},{2,4},{3,6},{4,3},{5,1},{6,5},{7,7},{8,10},{9,8},{10,1... | collective-permute-start | bytes 786440 | tf_op jit(solution)/shard_map/ppermute | solution.py:117
  32.1 206.4 %collective-permute-start.2 = (bf16[8,32,512]{2,1,0:T(8,128)(2,1)S(1)}, bf16[8,32,512]{2,1,0:T(8,128)(2,1)}, u32[]{:S(2)}, u32[]{:S(2)}) collective-permute-start(bf16[8,32,512]{2,1,0:T(8,128)(2,1)S(1)} %get-tuple-element.289), channel_id=1, source_target_pairs={{0,4},{2,0},{1,2},{3,6},{4,5},{6,1},{5,3},{7,7},{8,12},{10,8},{9,1... | collective-permute-start | bytes 786440 | tf_op jit(solution)/shard_map/ppermute | solution.py:117
  35.2 204.8 %collective-permute-start.1 = (bf16[8,32,512]{2,1,0:T(8,128)(2,1)S(1)}, bf16[8,32,512]{2,1,0:T(8,128)(2,1)}, u32[]{:S(2)}, u32[]{:S(2)}) collective-permute-start(bf16[8,32,512]{2,1,0:T(8,128)(2,1)S(1)} %get-tuple-element.290), channel_id=1, source_target_pairs={{0,0},{3,4},{1,2},{2,6},{4,1},{7,5},{5,3},{6,7},{8,8},{11,12},{9,1... | collective-permute-start | bytes 786440 | tf_op jit(solution)/shard_map/ppermute | solution.py:117
  36.9 185.4 %copy-start.138 = (f32[2,192]{1,0:T(2,128)S(1)}, f32[2,192]{1,0:T(2,128)}, u32[]{:S(2)}) copy-start(f32[2,192]{1,0:T(2,128)} %param.38) | copy-start | bytes 4612
  36.9 185.9 %copy-start.129 = (f32[2,512]{1,0:T(2,128)S(1)}, f32[2,512]{1,0:T(2,128)}, u32[]{:S(2)}) copy-start(f32[2,512]{1,0:T(2,128)} %param.42) | copy-start | bytes 12292
  37.8 213.7 %collective-permute-start.14 = (bf16[8,32,512]{2,1,0:T(8,128)(2,1)}, bf16[8,32,512]{2,1,0:T(8,128)(2,1)}, u32[]{:S(2)}, u32[]{:S(2)}) collective-permute-start(bf16[8,32,512]{2,1,0:T(8,128)(2,1)} %get-tuple-element.260), channel_id=1, source_target_pairs={{3,0},{1,4},{0,2},{2,6},{7,1},{5,5},{4,3},{6,7},{11,8},{9,12},{8,1... | collective-permute-start | bytes 786440 | tf_op jit(solution)/shard_map/ppermute | solution.py:117
  45.7 250.1 %copy-start.108 = (f32[384]{0:T(512)}, f32[384]{0:T(512)S(1)}, u32[]{:S(2)}) copy-start(f32[384]{0:T(512)S(1)} %slice_reduce_fusion.3) | copy-start | bytes 4612
  47.0 236.5 %copy-start.92 = (f32[544]{0:T(1024)}, f32[544]{0:T(1024)S(1)}, u32[]{:S(2)}) copy-start(f32[544]{0:T(1024)S(1)} %compare_select_fusion) | copy-start | bytes 6532
  130.7 103.1 %copy-start.152 = (f32[2,512]{1,0:T(2,128)S(1)}, f32[2,512]{1,0:T(2,128)}, u32[]{:S(2)}) copy-start(f32[2,512]{1,0:T(2,128)} %param.43) | copy-start | bytes 12292
  223.5 71.4 %copy-start.136 = (f32[16]{0:T(128)}, f32[16]{0:T(128)S(1)}, u32[]{:S(2)}) copy-start(f32[16]{0:T(128)S(1)} %broadcast_in_dim.102) | copy-start | bytes 196
  234.4 17.1 %collective-permute-start.17 = (bf16[8,32,512]{2,1,0:T(8,128)(2,1)}, bf16[8,32,512]{2,1,0:T(8,128)(2,1)}, u32[]{:S(2)}, u32[]{:S(2)}) collective-permute-start(bf16[8,32,512]{2,1,0:T(8,128)(2,1)} %get-tuple-element.261), channel_id=1, source_target_pairs={{0,2},{1,0},{2,4},{3,6},{4,3},{5,1},{6,5},{7,7},{8,10},{9,8},{10,1... | collective-permute-start | bytes 786440 | tf_op jit(solution)/shard_map/ppermute | solution.py:117
  236.3 17.4 %collective-permute-start.16 = (bf16[8,32,512]{2,1,0:T(8,128)(2,1)S(1)}, bf16[8,32,512]{2,1,0:T(8,128)(2,1)}, u32[]{:S(2)}, u32[]{:S(2)}) collective-permute-start(bf16[8,32,512]{2,1,0:T(8,128)(2,1)S(1)} %get-tuple-element.262), channel_id=1, source_target_pairs={{0,4},{2,0},{1,2},{3,6},{4,5},{6,1},{5,3},{7,7},{8,12},{10,8},{9,1... | collective-permute-start | bytes 786440 | tf_op jit(solution)/shard_map/ppermute | solution.py:117
  238.6 15.2 %collective-permute-start.15 = (bf16[8,32,512]{2,1,0:T(8,128)(2,1)S(1)}, bf16[8,32,512]{2,1,0:T(8,128)(2,1)}, u32[]{:S(2)}, u32[]{:S(2)}) collective-permute-start(bf16[8,32,512]{2,1,0:T(8,128)(2,1)S(1)} %get-tuple-element.263), channel_id=1, source_target_pairs={{0,0},{3,4},{1,2},{2,6},{4,1},{7,5},{5,3},{6,7},{8,8},{11,12},{9,1... | collective-permute-start | bytes 786440 | tf_op jit(solution)/shard_map/ppermute | solution.py:117
  242.5 13.6 %collective-permute-start.4 = (bf16[32,512]{1,0:T(8,128)(2,1)S(1)}, bf16[32,512]{1,0:T(8,128)(2,1)S(1)}, u32[]{:S(2)}, u32[]{:S(2)}) collective-permute-start(bf16[32,512]{1,0:T(8,128)(2,1)S(1)} %fusion.176), channel_id=1, source_target_pairs={{0,4},{4,0},{1,5},{5,1},{2,6},{6,2},{3,7},{7,3},{8,12},{12,8},{9,1... | collective-permute-start | bytes 98312 | tf_op jit(solution)/shard_map/ppermute | solution.py:157
  246.8 59.1 %copy-start.11 = (f32[1024,192]{0,1:T(8,128)}, f32[1024,192]{0,1:T(8,128)S(1)}, u32[]{:S(2)}) copy-start(f32[1024,192]{0,1:T(8,128)S(1)} %get-tuple-element.386) | copy-start | bytes 2359300
  247.8 24.8 %all-to-all-start = ((f32[16,2,192]{2,1,0:T(2,128)}), f32[16,2,192]{2,1,0:T(2,128)S(1)}, u32[]{:S(2)}, u32[]{:S(2)}) async-start(f32[16,2,192]{2,1,0:T(2,128)} %broadcast_in_dim.100), calls=%async_computation | async-start | bytes 65536 | tf_op jit(solution)/shard_map/all_to_all | solution.py:186
  272.6 33.4 %copy-start.116 = (f32[192]{0:T(256)}, f32[192]{0:T(256)S(1)}, u32[]{:S(2)}) copy-start(f32[192]{0:T(256)S(1)} %broadcast_multiply_fusion.5) | copy-start | bytes 2308
  272.7 33.3 %copy-start.118 = (f32[192]{0:T(256)}, f32[192]{0:T(256)S(1)}, u32[]{:S(2)}) copy-start(f32[192]{0:T(256)S(1)} %add_rsqrt_fusion.5) | copy-start | bytes 2308
  273.2 2.9 collective-permute-start.5
  284.5 9.6 %all-to-all-start.1 = ((f32[16,2,384]{2,1,0:T(2,128)}), f32[16,2,384]{2,1,0:T(2,128)S(1)}, u32[]{:S(2)}, u32[]{:S(2)}) async-start(f32[16,2,384]{2,1,0:T(2,128)} %broadcast_in_dim.105), calls=%async_computation.1 | async-start | bytes 98304 | tf_op jit(solution)/shard_map/all_to_all | solution.py:186
  296.4 7.0 collective-permute-start.6
  321.0 52.5 %copy-start.9 = (f32[1024,128]{1,0:T(8,128)}, f32[1024,128]{1,0:T(8,128)S(1)}, u32[]{:S(2)}) copy-start(f32[1024,128]{1,0:T(8,128)S(1)} %fusion.285) | copy-start | bytes 1572868
  322.2 9.2 %all-to-all-start.2 = ((f32[16,2,512]{2,1,0:T(2,128)}), f32[16,2,512]{2,1,0:T(2,128)S(1)}, u32[]{:S(2)}, u32[]{:S(2)}) async-start(f32[16,2,512]{2,1,0:T(2,128)} %broadcast_in_dim.106), calls=%async_computation.2 | async-start | bytes 131072 | tf_op jit(solution)/shard_map/all_to_all | solution.py:186
  332.6 29.7 %collective-permute-start.7 = (bf16[32,512]{1,0:T(8,128)(2,1)S(1)}, bf16[32,512]{1,0:T(8,128)(2,1)S(1)}, u32[]{:S(2)}, u32[]{:S(2)}) collective-permute-start(bf16[32,512]{1,0:T(8,128)(2,1)S(1)} %fusion.174), channel_id=1, source_target_pairs={{0,4},{4,0},{1,5},{5,1},{2,6},{6,2},{3,7},{7,3},{8,12},{12,8},{9,1... | collective-permute-start | bytes 98312 | tf_op jit(solution)/shard_map/ppermute | solution.py:157
  379.1 20.0 %all-to-all-start.3 = ((f32[16,2,192]{2,1,0:T(2,128)}), f32[16,2,192]{2,1,0:T(2,128)S(1)}, u32[]{:S(2)}, u32[]{:S(2)}) async-start(f32[16,2,192]{2,1,0:T(2,128)} %broadcast_in_dim.111), calls=%async_computation.3 | async-start | bytes 65536 | tf_op jit(solution)/shard_map/all_to_all | solution.py:186
  399.2 34.1 %copy-start.121 = (f32[192]{0:T(256)}, f32[192]{0:T(256)S(1)}, u32[]{:S(2)}) copy-start(f32[192]{0:T(256)S(1)} %broadcast_multiply_fusion.4) | copy-start | bytes 2308
  399.2 34.1 %copy-start.123 = (f32[192]{0:T(256)}, f32[192]{0:T(256)S(1)}, u32[]{:S(2)}) copy-start(f32[192]{0:T(256)S(1)} %add_rsqrt_fusion.4) | copy-start | bytes 2308
  399.9 33.5 %copy-start.141 = (f32[1,192]{1,0:T(1,128)}, f32[1,192]{1,0:T(1,128)S(1)}, u32[]{:S(2)}) copy-start(f32[1,192]{1,0:T(1,128)S(1)} %get-tuple-element.370) | copy-start | bytes 2308
  401.5 3.0 collective-permute-start.8
  413.2 10.4 %all-to-all-start.4 = ((f32[16,2,384]{2,1,0:T(2,128)}), f32[16,2,384]{2,1,0:T(2,128)S(1)}, u32[]{:S(2)}, u32[]{:S(2)}) async-start(f32[16,2,384]{2,1,0:T(2,128)} %broadcast_in_dim.112), calls=%async_computation.4 | async-start | bytes 98304 | tf_op jit(solution)/shard_map/all_to_all | solution.py:186
  426.4 4.2 collective-permute-start.9
  439.0 9.0 %all-to-all-start.5 = ((f32[16,2,512]{2,1,0:T(2,128)}), f32[16,2,512]{2,1,0:T(2,128)S(1)}, u32[]{:S(2)}, u32[]{:S(2)}) async-start(f32[16,2,512]{2,1,0:T(2,128)} %broadcast_in_dim.113), calls=%async_computation.5 | async-start | bytes 131072 | tf_op jit(solution)/shard_map/all_to_all | solution.py:186
  454.2 26.2 %all-to-all-start.6 = ((f32[16,2,512]{2,1,0:T(2,128)}), f32[16,2,512]{2,1,0:T(2,128)S(1)}, u32[]{:S(2)}, u32[]{:S(2)}) async-start(f32[16,2,512]{2,1,0:T(2,128)} %broadcast_in_dim.116), calls=%async_computation.6 | async-start | bytes 131072 | tf_op jit(solution)/shard_map/all_to_all | solution.py:186
  463.0 58.6 %collective-permute-start.10 = (bf16[8,32,512]{2,1,0:T(8,128)(2,1)}, bf16[8,32,512]{2,1,0:T(8,128)(2,1)}, u32[]{:S(2)}, u32[]{:S(2)}) collective-permute-start(bf16[8,32,512]{2,1,0:T(8,128)(2,1)} %get-tuple-element.268), channel_id=1, source_target_pairs={{0,3},{4,1},{2,0},{6,2},{1,7},{5,5},{3,4},{7,6},{8,11},{12,9},{10,... | collective-permute-start | bytes 786440 | tf_op jit(solution)/shard_map/ppermute | solution.py:130
  469.9 51.8 %collective-permute-start.13 = (bf16[8,32,512]{2,1,0:T(8,128)(2,1)}, bf16[8,32,512]{2,1,0:T(8,128)(2,1)}, u32[]{:S(2)}, u32[]{:S(2)}) collective-permute-start(bf16[8,32,512]{2,1,0:T(8,128)(2,1)} %get-tuple-element.269), channel_id=1, source_target_pairs={{2,0},{0,1},{4,2},{6,3},{3,4},{1,5},{5,6},{7,7},{10,8},{8,9},{12,1... | collective-permute-start | bytes 786440 | tf_op jit(solution)/shard_map/ppermute | solution.py:130
  472.1 49.5 %collective-permute-start.12 = (bf16[8,32,512]{2,1,0:T(8,128)(2,1)}, bf16[8,32,512]{2,1,0:T(8,128)(2,1)}, u32[]{:S(2)}, u32[]{:S(2)}) collective-permute-start(bf16[8,32,512]{2,1,0:T(8,128)(2,1)} %get-tuple-element.270), channel_id=1, source_target_pairs={{4,0},{0,2},{2,1},{6,3},{5,4},{1,6},{3,5},{7,7},{12,8},{8,10},{10,... | collective-permute-start | bytes 786440 | tf_op jit(solution)/shard_map/ppermute | solution.py:130
  476.6 45.0 %collective-permute-start.11 = (bf16[8,32,512]{2,1,0:T(8,128)(2,1)}, bf16[8,32,512]{2,1,0:T(8,128)(2,1)}, u32[]{:S(2)}, u32[]{:S(2)}) collective-permute-start(bf16[8,32,512]{2,1,0:T(8,128)(2,1)} %get-tuple-element.271), channel_id=1, source_target_pairs={{0,0},{4,3},{2,1},{6,2},{1,4},{5,7},{3,5},{7,6},{8,8},{12,11},{10,... | collective-permute-start | bytes 786440 | tf_op jit(solution)/shard_map/ppermute | solution.py:130
  504.2 6.0 collective-permute-start.18
  510.2 14.6 %collective-permute-start.19 = (bf16[1024,192]{0,1:T(8,128)(2,1)S(1)}, bf16[1024,192]{0,1:T(8,128)(2,1)S(1)}, u32[]{:S(2)}, u32[]{:S(2)}) collective-permute-start(bf16[1024,192]{0,1:T(8,128)(2,1)S(1)} %copy-done.76), channel_id=1, source_target_pairs={{4,0},{0,4},{5,1},{1,5},{6,2},{2,6},{7,3},{3,7},{12,8},{8,12},{13,... | collective-permute-start | bytes 1179656 | tf_op jit(solution)/shard_map/ppermute | solution.py:144
  532.9 9.3 %all-to-all-start.7 = ((f32[16,2,384]{2,1,0:T(2,128)}), f32[16,2,384]{2,1,0:T(2,128)S(1)}, u32[]{:S(2)}, u32[]{:S(2)}) async-start(f32[16,2,384]{2,1,0:T(2,128)} %broadcast_in_dim.235), calls=%async_computation.7 | async-start | bytes 98304 | tf_op jit(solution)/shard_map/all_to_all | solution.py:186
  545.1 2.3 collective-permute-start.20
  554.9 9.2 %all-to-all-start.8 = ((f32[16,2,192]{2,1,0:T(2,128)}), f32[16,2,192]{2,1,0:T(2,128)S(1)}, u32[]{:S(2)}, u32[]{:S(2)}) async-start(f32[16,2,192]{2,1,0:T(2,128)} %broadcast_in_dim.236), calls=%async_computation.8 | async-start | bytes 65536 | tf_op jit(solution)/shard_map/all_to_all | solution.py:186
  578.1 9.0 %all-to-all-start.9 = ((f32[16,2,512]{2,1,0:T(2,128)}), f32[16,2,512]{2,1,0:T(2,128)S(1)}, u32[]{:S(2)}, u32[]{:S(2)}) async-start(f32[16,2,512]{2,1,0:T(2,128)} %broadcast_in_dim.237), calls=%async_computation.9 | async-start | bytes 131072 | tf_op jit(solution)/shard_map/all_to_all | solution.py:186
  587.1 45.7 %all-to-all-start.18 = ((bf16[8,4,12,768]{3,1,2,0:T(4,128)(2,1)}), bf16[8,4,12,768]{3,1,2,0:T(4,128)(2,1)}, u32[]{:S(2)}, u32[]{:S(2)}) async-start(bf16[8,4,12,768]{3,1,2,0:T(4,128)(2,1)} %copy.837), calls=%async_computation.18 | async-start | bytes 1179648 | tf_op jit(solution)/shard_map/all_to_all | solution.py:423
  609.6 5.0 collective-permute-start.21
  614.3 11.0 %collective-permute-start.22 = (bf16[1024,192]{0,1:T(8,128)(2,1)}, bf16[1024,192]{0,1:T(8,128)(2,1)S(1)}, u32[]{:S(2)}, u32[]{:S(2)}) collective-permute-start(bf16[1024,192]{0,1:T(8,128)(2,1)} %get-tuple-element.397), channel_id=1, source_target_pairs={{4,0},{0,4},{5,1},{1,5},{6,2},{2,6},{7,3},{3,7},{12,8},{8,12},{13,... | collective-permute-start | bytes 1179656 | tf_op jit(solution)/shard_map/ppermute | solution.py:144
  633.5 9.8 %all-to-all-start.10 = ((f32[16,2,384]{2,1,0:T(2,128)}), f32[16,2,384]{2,1,0:T(2,128)S(1)}, u32[]{:S(2)}, u32[]{:S(2)}) async-start(f32[16,2,384]{2,1,0:T(2,128)} %broadcast_in_dim.242), calls=%async_computation.10 | async-start | bytes 98304 | tf_op jit(solution)/shard_map/all_to_all | solution.py:186
  643.3 9.3 %all-to-all-start.19 = ((bf16[4,12,768]{2,1,0:T(8,128)(2,1)}), bf16[4,12,768]{2,1,0:T(8,128)(2,1)S(1)}, u32[]{:S(2)}, u32[]{:S(2)}) async-start(bf16[4,12,768]{2,1,0:T(8,128)(2,1)} %copy.838), calls=%async_computation.19 | async-start | bytes 196608 | tf_op jit(solution)/shard_map/all_to_all | solution.py:425
  652.5 29.8 %all-to-all-start.14 = ((bf16[8,4,252,128]{3,1,2,0:T(4,128)(2,1)}), bf16[8,4,252,128]{3,1,2,0:T(4,128)(2,1)S(1)}, u32[]{:S(2)}, u32[]{:S(2)}) async-start(bf16[8,4,252,128]{3,1,2,0:T(4,128)(2,1)} %copy.827), calls=%async_computation.14 | async-start | bytes 4128768 | tf_op jit(solution)/shard_map/all_to_all | solution.py:423
  659.1 3.6 collective-permute-start.23
  683.0 9.3 %all-to-all-start.11 = ((f32[16,2,192]{2,1,0:T(2,128)}), f32[16,2,192]{2,1,0:T(2,128)S(1)}, u32[]{:S(2)}, u32[]{:S(2)}) async-start(f32[16,2,192]{2,1,0:T(2,128)} %broadcast_in_dim.243), calls=%async_computation.11 | async-start | bytes 65536 | tf_op jit(solution)/shard_map/all_to_all | solution.py:186
  695.8 23.2 %collective-permute-start.28 = (f32[4352]{0:T(1024)S(1)}, f32[4352]{0:T(1024)}, u32[]{:S(2)}, u32[]{:S(2)}) collective-permute-start(f32[4352]{0:T(1024)S(1)} %constant_dynamic-update-slice_fusion.76), channel_id=1, source_target_pairs={{0,2},{2,0},{1,3},{3,1},{4,6},{6,4},{5,7},{7,5},{8,10},{10,8},{9,1... | collective-permute-start | bytes 52232 | tf_op jit(solution)/shard_map/ppermute | solution.py:404
  698.1 21.6 %all-to-all-start.16 = ((bf16[8,4,12,768]{3,1,2,0:T(4,128)(2,1)}), bf16[8,4,12,768]{3,1,2,0:T(4,128)(2,1)S(1)}, u32[]{:S(2)}, u32[]{:S(2)}) async-start(bf16[8,4,12,768]{3,1,2,0:T(4,128)(2,1)} %copy.833), calls=%async_computation.16 | async-start | bytes 1179648 | tf_op jit(solution)/shard_map/all_to_all | solution.py:423
  706.7 51.0 %collective-permute-start.24 = (bf16[8,32,512]{2,1,0:T(8,128)(2,1)}, bf16[8,32,512]{2,1,0:T(8,128)(2,1)}, u32[]{:S(2)}, u32[]{:S(2)}) collective-permute-start(bf16[8,32,512]{2,1,0:T(8,128)(2,1)} %get-tuple-element.236), channel_id=1, source_target_pairs={{0,3},{4,1},{2,0},{6,2},{1,7},{5,5},{3,4},{7,6},{8,11},{12,9},{10,... | collective-permute-start | bytes 786440 | tf_op jit(solution)/shard_map/ppermute | solution.py:130
  710.9 46.8 %collective-permute-start.27 = (bf16[8,32,512]{2,1,0:T(8,128)(2,1)S(1)}, bf16[8,32,512]{2,1,0:T(8,128)(2,1)}, u32[]{:S(2)}, u32[]{:S(2)}) collective-permute-start(bf16[8,32,512]{2,1,0:T(8,128)(2,1)S(1)} %get-tuple-element.237), channel_id=1, source_target_pairs={{2,0},{0,1},{4,2},{6,3},{3,4},{1,5},{5,6},{7,7},{10,8},{8,9},{12,1... | collective-permute-start | bytes 786440 | tf_op jit(solution)/shard_map/ppermute | solution.py:130
  713.4 44.4 %collective-permute-start.26 = (bf16[8,32,512]{2,1,0:T(8,128)(2,1)S(1)}, bf16[8,32,512]{2,1,0:T(8,128)(2,1)}, u32[]{:S(2)}, u32[]{:S(2)}) collective-permute-start(bf16[8,32,512]{2,1,0:T(8,128)(2,1)S(1)} %get-tuple-element.238), channel_id=1, source_target_pairs={{4,0},{0,2},{2,1},{6,3},{5,4},{1,6},{3,5},{7,7},{12,8},{8,10},{10,... | collective-permute-start | bytes 786440 | tf_op jit(solution)/shard_map/ppermute | solution.py:130
  717.7 40.1 %collective-permute-start.25 = (bf16[8,32,512]{2,1,0:T(8,128)(2,1)S(1)}, bf16[8,32,512]{2,1,0:T(8,128)(2,1)}, u32[]{:S(2)}, u32[]{:S(2)}) collective-permute-start(bf16[8,32,512]{2,1,0:T(8,128)(2,1)S(1)} %get-tuple-element.239), channel_id=1, source_target_pairs={{0,0},{4,3},{2,1},{6,2},{1,4},{5,7},{3,5},{7,6},{8,8},{12,11},{10,... | collective-permute-start | bytes 786440 | tf_op jit(solution)/shard_map/ppermute | solution.py:130
  719.8 21.7 %all-to-all-start.15 = ((bf16[4,252,128]{2,1,0:T(8,128)(2,1)}), bf16[4,252,128]{2,1,0:T(8,128)(2,1)S(1)}, u32[]{:S(2)}, u32[]{:S(2)}) async-start(bf16[4,252,128]{2,1,0:T(8,128)(2,1)} %copy.828), calls=%async_computation.15 | async-start | bytes 524288 | tf_op jit(solution)/shard_map/all_to_all | solution.py:425
  741.4 9.1 %all-to-all-start.17 = ((bf16[4,12,768]{2,1,0:T(8,128)(2,1)}), bf16[4,12,768]{2,1,0:T(8,128)(2,1)S(1)}, u32[]{:S(2)}, u32[]{:S(2)}) async-start(bf16[4,12,768]{2,1,0:T(8,128)(2,1)} %copy.834), calls=%async_computation.17 | async-start | bytes 196608 | tf_op jit(solution)/shard_map/all_to_all | solution.py:425
  750.5 30.4 %all-to-all-start.12 = ((bf16[8,4,252,128]{3,1,2,0:T(4,128)(2,1)}), bf16[8,4,252,128]{3,1,2,0:T(4,128)(2,1)S(1)}, u32[]{:S(2)}, u32[]{:S(2)}) async-start(bf16[8,4,252,128]{3,1,2,0:T(4,128)(2,1)} %copy.824), calls=%async_computation.12 | async-start | bytes 4128768 | tf_op jit(solution)/shard_map/all_to_all | solution.py:423
  782.8 10.2 %all-to-all-start.13 = ((bf16[4,252,128]{2,1,0:T(8,128)(2,1)}), bf16[4,252,128]{2,1,0:T(8,128)(2,1)S(1)}, u32[]{:S(2)}, u32[]{:S(2)}) async-start(bf16[4,252,128]{2,1,0:T(8,128)(2,1)} %copy.825), calls=%async_computation.13 | async-start | bytes 524288 | tf_op jit(solution)/shard_map/all_to_all | solution.py:425
  (148 other events, 815.3 us)
Sparse Core Ops, SparseCore 0:
  11.5 73.3 all-gather.4
  88.5 56.3 all-gather.6

commit v2 on v1

v2 whole, which is shorter than its diff:
```python
import math

import jax
import jax.numpy as jnp
import numpy as np
from jax import lax
from jax.experimental import pallas as pl
from jax.experimental.pallas import tpu as pltpu
from jax.sharding import Mesh, PartitionSpec as P

EPS = 1e-05
LINE = ("c", "k", "z", "e")
KIND = ("g", "c", "z", "e")
PART = ("c", "e")
ALL = ("g", "c", "k", "z", "e")
f32 = jnp.float32
bf16 = jnp.bfloat16


def routes(e_n):
    s_n = 4 * e_n
    count = 2 * s_n
    edges = []
    for c in range(2):
        for s in range(s_n):
            src = c * s_n + s
            for half in range(2):
                target = half * s_n + (0 * 2 + c) * e_n + s // 4
                edges.append((src, half, target, s % 4))
            part = s // 2
            for half in range(2):
                target = (part // e_n) * s_n + (1 * 2 + c) * e_n + part % e_n
                edges.append((src, 2 + half, target, (s % 2) * 2 + half))
    rounds = []
    left = list(edges)
    for _ in range(4):
        owner = {}

        def augment(src, seen):
            for edge in left:
                if edge[0] == src and edge[2] not in seen:
                    seen.add(edge[2])
                    if edge[2] not in owner or augment(owner[edge[2]][0], seen):
                        owner[edge[2]] = edge
                        return True
            return False

        for src in range(count):
            assert augment(src, set())
        chosen = list(owner.values())
        for edge in chosen:
            left.remove(edge)
        pairs = [(edge[0], edge[2]) for edge in chosen]
        sent = np.zeros(count, np.int32)
        slot = np.zeros(count, np.int32)
        for edge in chosen:
            sent[edge[0]] = edge[1]
            slot[edge[2]] = edge[3]
        rounds.append((pairs, sent, slot))
    return rounds


def transform_tables(e_n, land_shape, port_shape):
    parts = 2 * e_n
    shapes = (land_shape, port_shape)
    most = max(rows * (cols // 2 + 1) for rows, cols in shapes)
    per_part = -(-most // (16 * parts)) * 16
    forward, inverse, weight, counts = [], [], [], []
    for kind, (rows, cols) in enumerate(shapes):
        half = cols // 2 + 1
        total = rows * half
        point = np.arange(per_part * parts)
        valid = point < total
        kr, f = point // half, point % half
        tiles = []
        for part in range(parts):
            c, e = part // e_n, part % e_n
            if kind == 0:
                h = np.arange(rows // e_n) + e * (rows // e_n)
                w = np.arange(cols // 2) + c * (cols // 2)
            else:
                h = np.arange(rows // parts) + part * (rows // parts)
                w = np.arange(cols)
            tiles.append((np.repeat(h, len(w)), np.tile(w, len(h))))
        cell_h = np.concatenate([tile[0] for tile in tiles])
        cell_w = np.concatenate([tile[1] for tile in tiles])
        size = rows * cols
        phase = (kr[:, None] * cell_h[None, :] * cols + f[:, None] * cell_w[None, :] * rows) % size
        angle = phase * (2.0 * math.pi / size)
        table = np.stack([np.cos(angle), -np.sin(angle)]) * valid[None, :, None]
        table = table.astype(np.float32).astype(jnp.bfloat16)
        cells = size // parts
        factor = np.where((f == 0) | (2 * f == cols), 1.0, 2.0) * valid
        counts.append([int(valid[p * per_part : (p + 1) * per_part].sum()) for p in range(parts)])
        for part in range(parts):
            order = [(part + step) % parts for step in range(parts)]
            own_points = slice(part * per_part, (part + 1) * per_part)
            own_cells = slice(part * cells, (part + 1) * cells)
            forward.append(
                np.concatenate([table[:, own_points, q * cells : (q + 1) * cells] for q in order], axis=2)
            )
            back = np.concatenate([table[:, q * per_part : (q + 1) * per_part, own_cells] for q in order], axis=1)
            inverse.append(np.ascontiguousarray(back.transpose(0, 2, 1)))
            weight.append(factor[own_points].astype(np.float32))
    return np.stack(forward), np.stack(inverse), np.stack(weight), np.asarray(counts, np.int32)


def pick(table, index):
    return lax.dynamic_index_in_dim(jnp.asarray(table), index, 0, keepdims=False)


def to_tile(land, port, rounds):
    rows = land.shape[1]
    wide = port.shape[2]
    units = jnp.stack([land[0, :, :wide], land[0, :, wide:], port[0, :rows], port[0, rows:]])
    me = lax.axis_index(LINE)
    got = []
    for pairs, sent, _ in rounds:
        got.append(lax.ppermute(pick(units, pick(sent, me)), LINE, pairs))
    got = jnp.stack(got)
    slots = np.stack([slot for _, _, slot in rounds], axis=1)
    order = pick(np.argsort(slots, axis=1).astype(np.int32), me)
    return jnp.concatenate([pick(got, order[i]) for i in range(4)], axis=0)


def from_tile(tile, rounds):
    rows = tile.shape[0] // 4
    units = tile.reshape((4, rows) + tile.shape[1:])
    me = lax.axis_index(LINE)
    got = []
    for pairs, _, slot in rounds:
        got.append(lax.ppermute(pick(units, pick(slot, me)), LINE, [(b, a) for a, b in pairs]))
    got = jnp.stack(got)
    sents = np.stack([sent for _, sent, _ in rounds], axis=1)
    order = pick(np.argsort(sents, axis=1).astype(np.int32), me)
    parts = [pick(got, order[i]) for i in range(4)]
    land = jnp.concatenate(parts[:2], axis=1)
    port = jnp.concatenate(parts[2:], axis=0)
    return land[None], port[None]


def shared(block):
    parts = lax.axis_size(PART)
    pieces = [
        lax.ppermute(block, PART, [((p + step) % parts, p) for p in range(parts)]) for step in range(1, parts)
    ]
    return pieces[0] if parts == 2 else jnp.concatenate(pieces, axis=0)


def edges(tile):
    rows, cols, channels = tile.shape
    c, k = lax.axis_index("c"), lax.axis_index("k")
    e_n = lax.axis_size("e")
    swap = [(0, 1), (1, 0)]
    zero = jnp.zeros((), tile.dtype)
    col_edge = jnp.where(c == 0, tile[:, -1], tile[:, 0])
    if e_n == 1:
        row_edge = jnp.where(c == 0, tile[-1], tile[0])
        got = lax.ppermute(jnp.where(k == 0, col_edge, row_edge), "c", swap)
        left = jnp.pad(jnp.where((k == 0) & (c == 1), got, zero), ((1, 1), (0, 0)))
        right = jnp.pad(jnp.where((k == 0) & (c == 0), got, zero), ((1, 1), (0, 0)))
        top = jnp.where((k == 1) & (c == 1), got, zero)
        bottom = jnp.where((k == 1) & (c == 0), got, zero)
        return top, bottom, left, right
    got = lax.ppermute(col_edge, "c", swap)
    left = jnp.where((k == 0) & (c == 1), got, zero)
    right = jnp.where((k == 0) & (c == 0), got, zero)
    wide = jnp.concatenate([left[:, None], tile, right[:, None]], axis=1)
    ahead = []
    for cc in range(2):
        for e in range(e_n):
            if e + 1 < e_n:
                ahead.append(((cc * 2 + 0) * e_n + e, (cc * 2 + 0) * e_n + e + 1))
            p = cc * e_n + e + 1
            if p < 2 * e_n:
                ahead.append(((cc * 2 + 1) * e_n + e, ((p // e_n) * 2 + 1) * e_n + p % e_n))
    axes = ("c", "k", "e")
    top = lax.ppermute(wide[-1], axes, ahead)
    bottom = lax.ppermute(wide[0], axes, [(b, a) for a, b in ahead])
    left = jnp.concatenate([top[:1], left, bottom[:1]], axis=0)
    right = jnp.concatenate([top[-1:], right, bottom[-1:]], axis=0)
    return top[1:-1], bottom[1:-1], left, right


def spread(values, axes):
    count = lax.axis_size(axes)
    return lax.all_to_all(jnp.broadcast_to(values[None], (count,) + values.shape), axes, 0, 0, tiled=True)


def gelu_parts(v):
    k = math.sqrt(2.0 / math.pi)
    square = v * v
    t = jnp.tanh(k * v * (1.0 + 0.044715 * square))
    half = 0.5 * (1.0 + t)
    return v * half, half + 0.5 * v * (1.0 - t * t) * (k * (1.0 + 3.0 * 0.044715 * square))


def gelu(v):
    return 0.5 * v * (1.0 + jnp.tanh(math.sqrt(2.0 / math.pi) * v * (1.0 + 0.044715 * (v * v))))


def dot(a, b):
    return lax.dot_general(a, b, (((1,), (0,)), ((), ())), preferred_element_type=f32)


def dot_t(a, b):
    return lax.dot_general(a, b, (((1,), (1,)), ((), ())), preferred_element_type=f32)


def outer(a, b):
    return lax.dot_general(a, b, (((0,), (0,)), ((), ())), preferred_element_type=f32)


def moments(every, counts):
    sums, squares = every[:, 0, :], every[:, 1, :]
    total = jnp.sum(counts)
    mean = jnp.sum(sums, axis=0, keepdims=True) / total
    apart = sums / counts - mean
    square = jnp.sum(squares + counts * apart * apart, axis=0, keepdims=True)
    return mean, lax.rsqrt(square / total + EPS)


def emit(out_ref, first, second):
    both = jnp.concatenate([first, second], axis=0)
    out_ref[...] = jnp.broadcast_to(both[None], out_ref.shape)


def emit_moments(out_ref, values, count, mask=None):
    local_sum = jnp.sum(values, axis=0, keepdims=True)
    centered = values - local_sum / count
    if mask is not None:
        centered = centered * mask
    emit(out_ref, local_sum, jnp.sum(centered * centered, axis=0, keepdims=True))


def emit_sums(out_ref, q, normed):
    emit(out_ref, jnp.sum(q, axis=0, keepdims=True), jnp.sum(q * normed, axis=0, keepdims=True))


def back_terms(every_ref, total):
    sums = jnp.sum(every_ref[...], axis=0)
    return sums, sums[0:1] / total, sums[1:2] / total


def run(body, outs, ins, name):
    return pl.pallas_call(
        body,
        out_shape=outs,
        compiler_params=pltpu.CompilerParams(vmem_limit_bytes=40 * 1024 * 1024),
        name=name,
    )(*ins)


def shape(dims, kind=f32):
    return jax.ShapeDtypeStruct(tuple(dims), kind)


def row_block(rows, most):
    block = rows
    while block > most or rows % block or block % 16:
        block -= 1
    return block


def whole_spec(array):
    zeros = (0,) * array.ndim
    return pl.BlockSpec(array.shape, lambda i, v: zeros)


def run_table(body, table, block, variant, outs, ins, name):
    rows = table.shape[2]
    spec = pl.BlockSpec((1, 2, block, table.shape[3]), lambda i, v: (v[0], 0, i, 0))
    return pl.pallas_call(
        body,
        out_shape=outs,
        grid_spec=pltpu.PrefetchScalarGridSpec(
            num_scalar_prefetch=1,
            grid=(rows // block,),
            in_specs=[spec] + [whole_spec(item) for item in ins],
            out_specs=[whole_spec(item) for item in outs],
        ),
        compiler_params=pltpu.CompilerParams(vmem_limit_bytes=40 * 1024 * 1024),
        name=name,
    )(variant, table, *ins)


def reduce_first(x, reduce_kernel, width, narrow):
    cells, channels = x.shape
    half = reduce_kernel.shape[1]

    def body(x_ref, r_ref, reduced_ref, stats_ref):
        reduced = dot(x_ref[:, narrow:], r_ref[...])
        reduced_ref[...] = reduced
        emit_moments(stats_ref, reduced, float(cells))

    return run(body, [shape((cells, half)), shape((width, 2, half))], (x, reduce_kernel), "reduce_first")


def reduce_next(both, every, counts, gain, bias, s, reduce_kernel, narrow):
    cells, channels = both.shape
    half = reduce_kernel.shape[1]
    width = every.shape[0]

    def body(both_ref, every_ref, counts_ref, g_ref, b_ref, r_ref, low_ref, reduced_ref, stats_ref, mi_ref):
        mean, inv = moments(every_ref[...], counts_ref[...])
        mi_ref[...] = jnp.concatenate([mean, inv], axis=0)
        state = gelu((both_ref[...] - mean) * inv * g_ref[s : s + 1] + b_ref[s : s + 1])
        low = state.astype(bf16)
        low_ref[...] = low
        reduced = dot(low[:, narrow:], r_ref[...])
        reduced_ref[...] = reduced
        emit_moments(stats_ref, reduced, float(cells))

    outs = [shape((cells, channels), bf16), shape((cells, half)), shape((width, 2, half)), shape((2, channels))]
    return run(body, outs, (both, every, counts, gain, bias, reduce_kernel), "reduce_next")


def activate(values, every, counts, gain, bias, s, factor, keep, name):
    rows, channels = values.shape

    def body(v_ref, every_ref, counts_ref, g_ref, b_ref, factor_ref, *out_refs):
        mean, inv = moments(every_ref[...], counts_ref[...])
        out_refs[0][...] = jnp.concatenate([mean, inv], axis=0)
        act = gelu((v_ref[...] - mean) * inv * g_ref[s : s + 1] + b_ref[s : s + 1])
        if keep:
            out_refs[2][...] = act
        else:
            act = act * factor_ref[...]
        out_refs[1][...] = act.astype(bf16)

    outs = [shape((2, channels)), shape((rows, channels), bf16)]
    if keep:
        outs.append(shape((rows, channels)))
    return run(body, outs, (values, every, counts, gain, bias, factor), name)


def spectrum_forward(table, variant, own, others, freq_kernel, factor, scale, width):
    points = table.shape[2]
    half = own.shape[1]
    wide = freq_kernel.shape[1]
    block = row_block(points, 272)
    cells = own.shape[0]

    def body(v_ref, t_ref, own_ref, others_ref, w_ref, factor_ref, real_ref, imag_ref, mixed_ref, stats_ref):
        i = pl.program_id(0)
        t = t_ref[0].reshape(2 * block, t_ref.shape[3])
        z = (dot(t[:, :cells], own_ref[...]) + dot(t[:, cells:], others_ref[...])) * scale
        real, imag = z[:block].astype(bf16), z[block:].astype(bf16)
        rows = pl.ds(pl.multiple_of(i * block, block), block)
        real_ref[rows] = real
        imag_ref[rows] = imag
        mixed_ref[rows] = dot(real, w_ref[:half]) + dot(imag, w_ref[half:])

        @pl.when(i == pl.num_programs(0) - 1)
        def _():
            mask = jnp.where(factor_ref[...] > 0.0, 1.0, 0.0)
            emit_moments(stats_ref, mixed_ref[...], jnp.sum(mask), mask)

    outs = [shape((points, half), bf16), shape((points, half), bf16), shape((points, wide)), shape((width, 2, wide))]
    return run_table(body, table, block, variant, outs, (own, others, freq_kernel, factor), "spectrum_forward")


def inverse_forward(table, variant, own, others, hidden, pre, expand_t, scale, width):
    cells = table.shape[2]
    half = hidden.shape[1]
    channels = pre.shape[1]
    narrow = channels - expand_t.shape[0]
    block = row_block(cells, 256)

    def body(v_ref, t_ref, own_ref, others_ref, hidden_ref, pre_ref, e_ref, summed_ref, both_ref, stats_ref):
        i = pl.program_id(0)
        rows = pl.ds(pl.multiple_of(i * block, block), block)
        freq = jnp.concatenate([own_ref[...], others_ref[...]], axis=0)
        returned = (dot(t_ref[0, 0], freq[:, :half]) + dot(t_ref[0, 1], freq[:, half:])) * scale
        summed = (hidden_ref[rows] + returned).astype(bf16)
        summed_ref[rows] = summed
        both_ref[rows, :narrow] = pre_ref[rows, :narrow]
        both_ref[rows, narrow:] = pre_ref[rows, narrow:] + dot_t(summed, e_ref[...])

        @pl.when(i == pl.num_programs(0) - 1)
        def _():
            emit_moments(stats_ref, both_ref[...], float(cells))

    outs = [shape((cells, half), bf16), shape((cells, channels)), shape((width, 2, channels))]
    return run_table(body, table, block, variant, outs, (own, others, hidden, pre, expand_t), "inverse_forward")


def turn(both, every, counts, gain, bias, s, x, cot, width):
    cells, channels = both.shape

    def body(both_ref, every_ref, counts_ref, g_ref, b_ref, x_ref, cot_ref, out_ref, q_ref, sums_ref, mi_ref):
        mean, inv = moments(every_ref[...], counts_ref[...])
        mi_ref[...] = jnp.concatenate([mean, inv], axis=0)
        normed = (both_ref[...] - mean) * inv
        state, slope = gelu_parts(normed * g_ref[s : s + 1] + b_ref[s : s + 1])
        out_ref[...] = (x_ref[...].astype(f32) + state).astype(bf16)
        q = slope * cot_ref[...].astype(f32)
        q_ref[...] = q
        emit_sums(sums_ref, q, normed)

    outs = [shape((cells, channels), bf16), shape((cells, channels)), shape((width, 2, channels)), shape((2, channels))]
    return run(body, outs, (both, every, counts, gain, bias, x, cot), "turn")


def grad_pre(q, both, mi, every, gain, s, expand_t, total):
    cells, channels = both.shape
    broad, half = expand_t.shape
    narrow = channels - broad

    def body(q_ref, both_ref, mi_ref, every_ref, g_ref, e_ref, low_ref, summed_ref, summed_low_ref, sums_ref):
        sums, bias_term, gain_term = back_terms(every_ref, total)
        sums_ref[...] = sums
        inv = mi_ref[1:2]
        normed = (both_ref[...] - mi_ref[0:1]) * inv
        low = (g_ref[s : s + 1] * inv * (q_ref[...] - bias_term - normed * gain_term)).astype(bf16)
        low_ref[...] = low
        summed = dot(low[:, narrow:], e_ref[...])
        summed_ref[...] = summed
        summed_low_ref[...] = summed.astype(bf16)

    outs = [shape((cells, channels), bf16), shape((cells, half)), shape((cells, half), bf16), shape((2, channels))]
    return run(body, outs, (q, both, mi, every, gain, expand_t), "grad_pre")


def spectrum_backward(table, variant, own, others, mixed, mi, gain, bias, s, factor, scale, width):
    points, wide = mixed.shape
    block = row_block(points, 272)
    cells = own.shape[0]

    def body(v_ref, t_ref, own_ref, others_ref, mixed_ref, mi_ref, g_ref, b_ref, factor_ref, q_ref, sums_ref, n_ref):
        i = pl.program_id(0)
        t = t_ref[0].reshape(2 * block, t_ref.shape[3])
        z = dot(t[:, :cells], own_ref[...]) + dot(t[:, cells:], others_ref[...])
        rows = pl.ds(pl.multiple_of(i * block, block), block)
        grad = jnp.concatenate([z[:block], z[block:]], axis=1) * (factor_ref[rows] * scale)
        normed = (mixed_ref[rows] - mi_ref[0:1]) * mi_ref[1:2]
        _, slope = gelu_parts(normed * g_ref[s : s + 1] + b_ref[s : s + 1])
        q_ref[rows] = slope * grad
        n_ref[rows] = normed

        @pl.when(i == pl.num_programs(0) - 1)
        def _():
            emit_sums(sums_ref, q_ref[...], n_ref[...])

    outs = [shape((points, wide)), shape((width, 2, wide)), shape((points, wide))]
    ins = (own, others, mixed, mi, gain, bias, factor)
    return run_table(body, table, block, variant, outs, ins, "spectrum_backward")


def grad_mixed(q, normed, mi, every, gain, s, freq_kernel, counts):
    points, wide = q.shape

    def body(q_ref, n_ref, mi_ref, every_ref, g_ref, w_ref, counts_ref, low_ref, back_ref, sums_ref):
        sums, bias_term, gain_term = back_terms(every_ref, jnp.sum(counts_ref[...]))
        sums_ref[...] = sums
        low = (g_ref[s : s + 1] * mi_ref[1:2] * (q_ref[...] - bias_term - n_ref[...] * gain_term)).astype(bf16)
        low_ref[...] = low
        back_ref[...] = dot_t(low, w_ref[...]).astype(bf16)

    outs = [shape((points, wide), bf16), shape((points, wide), bf16), shape((2, wide))]
    return run(body, outs, (q, normed, mi, every, gain, freq_kernel, counts), "grad_mixed")


def inverse_backward(table, variant, own, others, summed, reduced, mi, gain, bias, s, scale, width):
    cells = table.shape[2]
    half = summed.shape[1]
    block = row_block(cells, 256)

    def body(v_ref, t_ref, own_ref, others_ref, summed_ref, reduced_ref, mi_ref, g_ref, b_ref, q_ref, sums_ref, n_ref):
        i = pl.program_id(0)
        rows = pl.ds(pl.multiple_of(i * block, block), block)
        freq = jnp.concatenate([own_ref[...], others_ref[...]], axis=0)
        back = (dot(t_ref[0, 0], freq[:, :half]) + dot(t_ref[0, 1], freq[:, half:])) * scale
        normed = (reduced_ref[rows] - mi_ref[0:1]) * mi_ref[1:2]
        _, slope = gelu_parts(normed * g_ref[s : s + 1] + b_ref[s : s + 1])
        q_ref[rows] = slope * (summed_ref[rows] + back)
        n_ref[rows] = normed

        @pl.when(i == pl.num_programs(0) - 1)
        def _():
            emit_sums(sums_ref, q_ref[...], n_ref[...])

    outs = [shape((cells, half)), shape((width, 2, half)), shape((cells, half))]
    ins = (own, others, summed, reduced, mi, gain, bias)
    return run_table(body, table, block, variant, outs, ins, "inverse_backward")


def grad_reduced(q, normed, mi, every, gain, s, reduce_kernel, total, conv_back, both, mi_3, gain_3, bias_3, width):
    cells, half = q.shape
    channels = both.shape[1]
    narrow = channels - reduce_kernel.shape[0]

    def body(q_ref, n_ref, mi_ref, every_ref, g_ref, r_ref, conv_ref, both_ref, mi3_ref, g3_ref, b3_ref, low_ref, out_ref, sums3_ref, sums_ref):
        sums, bias_term, gain_term = back_terms(every_ref, total)
        sums_ref[...] = sums
        low = (g_ref[s : s + 1] * mi_ref[1:2] * (q_ref[...] - bias_term - n_ref[...] * gain_term)).astype(bf16)
        low_ref[...] = low
        grad = conv_ref[...]
        grad = jnp.concatenate([grad[:, :narrow], grad[:, narrow:] + dot_t(low, r_ref[...])], axis=1)
        normed_3 = (both_ref[...] - mi3_ref[0:1]) * mi3_ref[1:2]
        _, slope = gelu_parts(normed_3 * g3_ref[s - 1 : s] + b3_ref[s - 1 : s])
        grad = grad * slope
        out_ref[...] = grad
        emit_sums(sums3_ref, grad, normed_3)

    outs = [shape((cells, half), bf16), shape((cells, channels)), shape((width, 2, channels)), shape((2, half))]
    ins = (q, normed, mi, every, gain, reduce_kernel, conv_back, both, mi_3, gain_3, bias_3)
    return run(body, outs, ins, "grad_reduced")


def grad_input(q, normed, mi, every, gain, s, reduce_kernel, total, conv_back, cot):
    cells, half = q.shape
    channels = cot.shape[1]
    narrow = channels - reduce_kernel.shape[0]

    def body(q_ref, n_ref, mi_ref, every_ref, g_ref, r_ref, conv_ref, cot_ref, low_ref, out_ref, sums_ref):
        sums, bias_term, gain_term = back_terms(every_ref, total)
        sums_ref[...] = sums
        low = (g_ref[s : s + 1] * mi_ref[1:2] * (q_ref[...] - bias_term - n_ref[...] * gain_term)).astype(bf16)
        low_ref[...] = low
        grad = conv_ref[...] + cot_ref[...].astype(f32)
        out_ref[:, :narrow] = grad[:, :narrow].astype(bf16)
        out_ref[:, narrow:] = (grad[:, narrow:] + dot_t(low, r_ref[...])).astype(bf16)

    outs = [shape((cells, half), bf16), shape((cells, channels), bf16), shape((2, half))]
    return run(body, outs, (q, normed, mi, every, gain, reduce_kernel, conv_back, cot), "grad_input")


def padded_columns(tile_ref, top_ref, bottom_ref, left_ref, right_ref, out_ref, cols, lanes):
    wide = jnp.concatenate([top_ref[:, lanes], tile_ref[:, lanes], bottom_ref[:, lanes]], axis=0)
    rows = wide.shape[0] // cols
    out_ref[1] = wide
    wide = wide.astype(f32)
    column = lax.broadcasted_iota(jnp.int32, (rows, cols, 1), 1)
    for j, edge_ref, at in ((0, left_ref, 0), (2, right_ref, cols - 1)):
        moved = pltpu.roll(wide, 1 if j == 0 else wide.shape[0] - 1, 0).reshape(rows, cols, wide.shape[1])
        edge = edge_ref[:, lanes].astype(f32)[:, None, :]
        moved = jnp.where(column == at, edge, moved)
        out_ref[j] = moved.reshape(rows * cols, wide.shape[1]).astype(bf16)


def conv_forward(low, sides, cols, local_kernel, global_t):
    cells, channels = low.shape
    narrow = local_kernel.shape[2]
    padded = cells + 2 * cols

    def body(x_ref, top_ref, bottom_ref, left_ref, right_ref, l_ref, g_ref, pre_ref, cols_ref, wide_ref):
        padded_columns(x_ref, top_ref, bottom_ref, left_ref, right_ref, wide_ref, cols, slice(None))
        cols_ref[...] = wide_ref[:, :, :narrow]
        local = jnp.zeros((cells, narrow), f32)
        for t in range(9):
            i, j = t // 3, t % 3
            local = local + dot(wide_ref[j, i * cols : i * cols + cells], l_ref[t])
        pre_ref[:, :narrow] = local
        patches = jnp.concatenate([wide_ref[t % 3, t // 3 * cols : t // 3 * cols + cells, :narrow] for t in range(9)], axis=1)
        pre_ref[:, narrow:] = dot_t(patches, g_ref[...])

    return pl.pallas_call(
        body,
        out_shape=[shape((cells, channels)), shape((3, padded, narrow), bf16)],
        scratch_shapes=[pltpu.VMEM((3, padded, channels), bf16)],
        compiler_params=pltpu.CompilerParams(vmem_limit_bytes=40 * 1024 * 1024),
        name="conv_forward",
    )(low, *sides, local_kernel, global_t)


def conv_backward(low, sides, cols, local_kernel, global_t):
    cells, channels = low.shape
    narrow = local_kernel.shape[2]
    broad = channels - narrow
    padded = cells + 2 * cols

    def body(x_ref, top_ref, bottom_ref, left_ref, right_ref, l_ref, g_ref, grad_ref, patches_ref, wide_ref):
        padded_columns(x_ref, top_ref, bottom_ref, left_ref, right_ref, wide_ref, cols, slice(None))
        grad = jnp.zeros((cells, channels), f32)
        into = jnp.zeros((cells, narrow), f32)
        for t in range(9):
            i, j = 2 - t // 3, 2 - t % 3
            rows = slice(i * cols, i * cols + cells)
            patches_ref[:, t * narrow : (t + 1) * narrow] = wide_ref[j, rows, :narrow]
            grad = grad + dot_t(wide_ref[j, rows, :narrow], l_ref[t])
            into = into + dot(wide_ref[j, rows, narrow:], g_ref[:, t * narrow : (t + 1) * narrow])
        grad_ref[:, :narrow] = grad[:, :narrow] + into
        grad_ref[:, narrow:] = grad[:, narrow:]

    return pl.pallas_call(
        body,
        out_shape=[shape((cells, channels)), shape((cells, 9 * narrow), bf16)],
        scratch_shapes=[pltpu.VMEM((3, padded, channels), bf16)],
        compiler_params=pltpu.CompilerParams(vmem_limit_bytes=40 * 1024 * 1024),
        name="conv_backward",
    )(low, *sides, local_kernel, global_t)


def gathered(shard):
    line = ("k", "z", "e")
    block = spread(shard, line)
    block = spread(block, "g")
    other = lax.ppermute(block, "c", [(0, 1), (1, 0)])
    first = jnp.where(lax.axis_index("c") == 0, block, other)
    second = jnp.where(lax.axis_index("c") == 0, other, block)
    both = jnp.stack([first, second], axis=1)
    return both.reshape((-1,) + shard.shape)


def per_device(plan, *args):
    (
        land,
        port,
        to_local,
        to_global,
        reduce_weight,
        freq_weight,
        expand_weight,
        spec_gain,
        spec_bias,
        freq_gain,
        freq_bias,
        out_gain,
        out_bias,
        cot_land,
        cot_port,
    ) = args
    rounds, forward_table, inverse_table, weight_table, point_counts = plan
    sections = to_local.shape[0]
    devices = lax.axis_size(ALL)
    own_in = to_local.shape[2]
    own_out = to_global.shape[3]
    narrow = to_local.shape[3]
    channels = own_in * devices
    broad = channels - narrow
    half = reduce_weight.shape[2]
    k, part = lax.axis_index("k"), lax.axis_index(PART)
    variant = k * lax.axis_size(PART) + part
    g_n, z_n, e_n = lax.axis_size("g"), lax.axis_size("z"), lax.axis_size("e")
    width = lax.axis_size(KIND)

    packed = jnp.concatenate([freq_weight, reduce_weight, jnp.transpose(expand_weight, (0, 2, 1))], axis=2)
    small = gathered(packed)
    x = to_tile(land, port, rounds)
    rows, cols = x.shape[:2]
    cells = rows * cols
    x = x.reshape(cells, channels)
    size = cells * lax.axis_size(PART)
    scale = 1.0 / math.sqrt(size)
    maps = g_n * z_n
    taps_local = jnp.reshape(to_local, (sections, 9 * own_in, narrow))
    taps_global = jnp.transpose(to_global, (0, 3, 1, 2)).reshape(sections, own_out * 9, narrow)
    kernels = gathered(jnp.concatenate([taps_local, taps_global], axis=1))
    weights = []
    for s in range(sections):
        full = small[:, s].reshape(broad, -1)
        wide = full.shape[1] - 2 * half
        local_kernel = kernels[:, s, : 9 * own_in].reshape(devices, 9, own_in, narrow)
        local_kernel = jnp.transpose(local_kernel, (1, 0, 2, 3)).reshape(9, channels, narrow)
        global_t = kernels[:, s, 9 * own_in :].reshape(broad, 9 * narrow)
        weights.append((full[:, wide : wide + half], full[:, :wide], full[:, wide + half :], local_kernel, global_t))
    cot = to_tile(cot_land, cot_port, rounds).reshape(cells, channels)

    factor = pick(weight_table, variant)[:, None]
    cell_counts = jnp.full((width, 1), cells, f32)
    by_part = pick(point_counts, k).astype(f32)
    freq_counts = jnp.broadcast_to(by_part.reshape(1, 2, 1, e_n), (g_n, 2, z_n, e_n)).reshape(width, 1)
    cell_total = float(maps * size)
    variant = variant.reshape(1)
    forward_table, inverse_table = jnp.asarray(forward_table), jnp.asarray(inverse_table)

    def exchange(stats):
        return lax.all_to_all(stats, KIND, 0, 0, tiled=True)

    kept = []
    both = every_3 = None
    for s in range(sections):
        reduce_kernel, freq_kernel, expand_t, local_kernel, global_t = weights[s]
        if s == 0:
            low = x
            reduced, stats = reduce_first(x, reduce_kernel, width, narrow)
        else:
            low, reduced, stats, mi_3 = reduce_next(both, every_3, cell_counts, out_gain, out_bias, s - 1, reduce_kernel, narrow)
            kept[-1]["mi_3"] = mi_3
        every_1 = exchange(stats)
        sides = edges(low.reshape(rows, cols, channels))
        pre, shifted = conv_forward(low, sides, cols, local_kernel, global_t)
        mi_1, hidden_low, hidden = activate(reduced, every_1, cell_counts, spec_gain, spec_bias, s, factor, True, "hidden")
        real, imag, mixed, stats = spectrum_forward(
            forward_table, variant, hidden_low, shared(hidden_low), freq_kernel, factor, scale, width
        )
        every_2 = exchange(stats)
        mi_2, freq_act = activate(mixed, every_2, freq_counts, freq_gain, freq_bias, s, factor, False, "freq_act")
        summed, both, stats = inverse_forward(
            inverse_table, variant, freq_act, shared(freq_act), hidden, pre, expand_t, scale, width
        )
        every_3 = exchange(stats)
        kept.append(
            dict(low=low, shifted=shifted, reduced=reduced, mi_1=mi_1, real=real, imag=imag, mixed=mixed, mi_2=mi_2, summed=summed, both=both)
        )
    out, q_3, sums, mi_3 = turn(both, every_3, cell_counts, out_gain, out_bias, sections - 1, x, cot, width)
    kept[-1]["mi_3"] = mi_3
    land_out, port_out = from_tile(out.reshape(rows, cols, channels), rounds)

    weight_shares = [None] * sections
    norm_sums = [None] * sections
    for s in reversed(range(sections)):
        reduce_kernel, freq_kernel, expand_t, local_kernel, global_t = weights[s]
        item = kept[s]
        every = exchange(sums)
        low, summed, summed_low, sums_3 = grad_pre(q_3, item["both"], item["mi_3"], every, out_gain, s, expand_t, cell_total)
        q, sums, normed = spectrum_backward(
            forward_table, variant, summed_low, shared(summed_low), item["mixed"], item["mi_2"], freq_gain, freq_bias, s, factor, scale, width
        )
        every = exchange(sums)
        sides = edges(low.reshape(rows, cols, channels))
        conv_back, patches = conv_backward(low, sides, cols, local_kernel, global_t)
        mixed_low, back, sums_2 = grad_mixed(q, normed, item["mi_2"], every, freq_gain, s, freq_kernel, freq_counts)
        q, sums, normed = inverse_backward(
            inverse_table, variant, back, shared(back), summed, item["reduced"], item["mi_1"], spec_gain, spec_bias, s, scale, width
        )
        every = exchange(sums)
        if s > 0:
            below = kept[s - 1]
            reduced_low, q_3, sums, sums_1 = grad_reduced(
                q, normed, item["mi_1"], every, spec_gain, s, reduce_kernel, cell_total,
                conv_back, below["both"], below["mi_3"], out_gain, out_bias, width,
            )
        else:
            reduced_low, grad, sums_1 = grad_input(
                q, normed, item["mi_1"], every, spec_gain, s, reduce_kernel, cell_total, conv_back, cot
            )
            land_grad, port_grad = from_tile(grad.reshape(rows, cols, channels), rounds)
        grad_global = low[:, narrow:]
        local_grad = outer(item["low"], patches)
        taps = jnp.concatenate(
            [item["shifted"][t % 3, t // 3 * cols : t // 3 * cols + cells] for t in range(9)], axis=1
        )
        global_grad = outer(grad_global, taps)
        expand_grad = outer(grad_global, item["summed"])
        freq_grad = jnp.concatenate([outer(item["real"], mixed_low), outer(item["imag"], mixed_low)], axis=0)
        reduce_grad = outer(item["low"][:, narrow:], reduced_low)
        local_grad = jnp.transpose(local_grad.reshape(devices, own_in, 9, narrow), (0, 2, 1, 3))
        local_grad = local_grad.reshape(devices, 9 * own_in, narrow)
        global_grad = global_grad.reshape(devices, own_out * 9, narrow)
        others = jnp.concatenate([freq_grad, reduce_grad, expand_grad], axis=1)
        others = others.reshape(devices, own_out, others.shape[1])
        owned_kernels = owned(jnp.concatenate([local_grad, global_grad], axis=1))
        owned_others = owned(others)
        weight_shares[s] = (
            owned_kernels[: 9 * own_in].reshape(9, own_in, narrow),
            jnp.transpose(owned_kernels[9 * own_in :].reshape(own_out, 9, narrow), (1, 2, 0)),
            owned_others[:, 2 * half : 3 * half],
            owned_others[:, : 2 * half],
            jnp.transpose(owned_others[:, 3 * half :]),
        )
        norm_sums[s] = (sums_1, sums_2, sums_3)
    flat_sums = jnp.concatenate([item for s in range(sections) for item in norm_sums[s]], axis=1)
    flat_sums = flat_sums + lax.ppermute(flat_sums, "k", [(0, 1), (1, 0)])
    gains = [[] for _ in range(6)]
    offset = 0
    for s in range(sections):
        for index, wide in enumerate((half, 2 * half, channels)):
            gains[2 * index].append(flat_sums[1, offset : offset + wide])
            gains[2 * index + 1].append(flat_sums[0, offset : offset + wide])
            offset += wide
    stacked = [jnp.stack([weight_shares[s][i] for s in range(sections)]) for i in range(5)]
    return (land_out, port_out, land_grad, port_grad, *stacked, *[jnp.stack(item) for item in gains])


def owned(shares):
    shape = shares.shape[1:]
    g_n, c_n = lax.axis_size("g"), lax.axis_size("c")
    rest = lax.axis_size(("k", "z", "e"))
    low = shares.astype(bf16).reshape((g_n * c_n, rest) + shape)
    first = lax.all_to_all(low, ("g", "c"), 0, 0, tiled=True)
    first = jnp.sum(first.astype(f32), axis=0).astype(bf16)
    second = lax.all_to_all(first, ("k", "z", "e"), 0, 0, tiled=True)
    return jnp.sum(second.astype(f32), axis=0)


def solution(mesh):
    f_n, s_n = mesh.shape["fsdp"], mesh.shape["sp"]
    e_n = s_n // 4
    fine = Mesh(np.asarray(mesh.devices).reshape(f_n // 2, 2, 2, 2, e_n), ALL)
    maps = P(("g", "c"), ("k", "z", "e"), None, None)
    split = ALL

    def whole(*args):
        land, port = args[0], args[1]
        plan = (
            routes(e_n),
            *transform_tables(e_n, land.shape[1:3], port.shape[1:3]),
        )
        weights = (
            P(None, None, split, None),
            P(None, None, None, split),
            P(None, split, None),
            P(None, split, None),
            P(None, None, split),
        )
        return jax.shard_map(
            lambda *local: per_device(plan, *local),
            mesh=fine,
            in_specs=(maps, maps, *weights, P(), P(), P(), P(), P(), P(), maps, maps),
            out_specs=(maps, maps, maps, maps, *weights, P(), P(), P(), P(), P(), P()),
            check_vma=False,
        )(*args)

    return whole
```

time: 812 us -> 619 us (0.76)
  blocking collectives: 153 us -> 0 us
  matrix products: 124 us -> 22.9 us
  Pallas kernels: 0 us -> 77.1 us
  other arithmetic: 84.3 us -> 40.8 us
  starting transfers between devices: 135 us -> 167 us
  local copies, waits for them, and re-layouts: 162 us -> 187 us
  waiting for transfers between devices: 94.1 us -> 78 us
  between operations: 49.4 us -> 33.7 us
    all_gather x2 -> x0, blocking collectives: 153 us -> none  [gather_rows(): return lax.all_gather(shard, ALL, tiled=True)]
    dot_general x38 -> x0, matrix products: 96.8 us -> none  [the longest x30 82.3 us: dot(): lax.dot_general(a, b, (((1,), (0,)), ((), ())), preferred_element_type=f32)]
    pallas_call x0 -> x25, Pallas kernels: none -> 77.1 us  [the longest x8 39.3 us: run_table(): pl.pallas_call(body, out_shape=outs, grid_spec=pltpu.PrefetchScalarGridSp...]
    unnamed x401 -> x333, local copies, waits for them, and re-layouts: 39.3 us -> 100 us
    all_to_all x0 -> x12, starting transfers between devices: none -> 52.9 us  [exchange(): return lax.all_to_all(stats, KIND, 0, 0, tiled=True)]
    all_to_all x12 -> x4, starting transfers between devices: 47.3 us -> 19.7 us  [spread(): lax.all_to_all(jnp.broadcast_to(values[None], (count,) + values.shape), a...]
    all_to_all x12 -> x4, waiting for transfers between devices: 26.6 us -> 1.93 us  [spread(): lax.all_to_all(jnp.broadcast_to(values[None], (count,) + values.shape), a...]
    convert_element_type x15 -> x0, other arithmetic: 22.3 us -> none  [the longest x3 6.82 us: per_device(): grad_low = grad_pre.astype(bf16)]
  transfers between devices with their start and end apart: 51 -> 55, of which waited for: 16 -> 17; matrix products, arithmetic and copies ran while one was open for 34% -> 28% of each run, Pallas kernels for 0% -> 7%
where the time goes in v2:
time: 619 us; the launch traced here: 607 us
  local copies, waits for them, and re-layouts  187 us (30%)
  starting transfers between devices  167 us (27%)
  waiting for transfers between devices  78 us (13%)
  Pallas kernels  77.1 us (12%)
  other arithmetic  40.8 us (7%)
  between operations  33.7 us (5%)
  matrix products  22.9 us (4%)
    unnamed x333, local copies, waits for them, and re-layouts  100 us
    all_to_all x12, starting transfers between devices, exchange(): return lax.all_to_all(stats, KIND, 0, 0, tiled=True)  52.9 us
    pallas_call x8, Pallas kernels, run_table(): pl.pallas_call(body, out_shape=outs, grid_spec=pltpu.PrefetchScalarGridSp...  39.3 us
    ppermute x8, starting transfers between devices, to_tile(): got.append(lax.ppermute(pick(units, pick(sent, me)), LINE, pairs))  31 us
    all_to_all x4, waiting for transfers between devices, owned(): second = lax.all_to_all(first, ('k', 'z', 'e'), 0, 0, tiled=True)  27.8 us
    all_to_all x4, waiting for transfers between devices, owned(): first = lax.all_to_all(low, ('g', 'c'), 0, 0, tiled=True)  25.3 us
    ppermute x8, starting transfers between devices, from_tile(): lax.ppermute(pick(units, pick(slot, me)), LINE, [(b, a) for a, b in pairs])  25.1 us
    dot_general x12, matrix products, outer(): lax.dot_general(a, b, (((0,), (0,)), ((), ())), preferred_element_type=f32)  22.9 us
  transfers between devices with their start and end apart: 55, of which 17 were waited for; matrix products, arithmetic and copies ran while one was open for 28% of the time, Pallas kernels for 7%

profile of v2, /device:TPU:0, one launch (start us, length us, event | category | flops | bytes accessed | tf_op | source)
XLA Modules:
  0.0 607.1 jit_solution(7046721002864424753)
XLA Ops:
  2.3 6.3 %all-to-all-start = ((bf16[4,2,12,768]{3,1,2,0:T(2,128)(2,1)}), bf16[4,2,12,768]{3,1,2,0:T(2,128)(2,1)S(1)}, u32[]{:S(2)}, u32[]{:S(2)}) async-start(bf16[4,2,12,768]{3,1,2,0:T(2,128)(2,1)} %broadcast_in_dim.65), calls=%async_computation | async-start | bytes 294912 | tf_op jit(solution)/shard_map/all_to_all | solution.py:187
  24.5 5.1 all-to-all-start.4
  30.7 4.8 collective-permute-start.3
  38.5 3.6 collective-permute-start.1
  45.6 3.7 all-to-all-start.1
  50.4 5.4 collective-permute-start.15
  61.0 4.6 all-to-all-start.5
  92.7 6.1 %collective-permute-start.14 = (bf16[8,32,512]{2,1,0:T(8,128)(2,1)}, bf16[8,32,512]{2,1,0:T(8,128)(2,1)}, u32[]{:S(2)}, u32[]{:S(2)}) collective-permute-start(bf16[8,32,512]{2,1,0:T(8,128)(2,1)} %get-tuple-element.306), channel_id=1, source_target_pairs={{0,4},{2,0},{1,2},{3,6},{4,5},{6,1},{5,3},{7,7},{8,12},{10,8},{9,1... | collective-permute-start | bytes 786440 | tf_op jit(solution)/shard_map/ppermute | solution.py:119
  98.8 3.6 collective-permute-start.13
  112.2 5.8 slice_reduce_fusion
  120.9 7.0 %all-to-all-start.2 = ((f32[16,2,192]{2,1,0:T(2,128)}), f32[16,2,192]{2,1,0:T(2,128)S(1)}, u32[]{:S(2)}, u32[]{:S(2)}) async-start(f32[16,2,192]{2,1,0:T(2,128)} %get-tuple-element.91), calls=%async_computation.2 | async-start | bytes 65536 | tf_op jit(solution)/shard_map/all_to_all | solution.py:669
  142.5 4.5 spectrum_forward.2
  149.0 3.7 all-to-all-start.3
  161.1 3.3 select_bitcast_fusion.1
  173.8 4.1 conv_forward.2
  178.8 5.8 inverse_forward.2
  186.1 3.8 all-to-all-start.6
  212.9 4.9 all-to-all-start.7
  222.4 4.1 conv_forward.3
  236.3 4.5 spectrum_forward.3
  243.8 5.0 all-to-all-start.8
  250.6 3.8 all-to-all-done.8.every_ref
  261.9 5.6 inverse_forward.3
  270.3 3.9 all-to-all-start.9
  275.9 3.8 all-to-all-done.9.every_ref
  282.6 4.0 turn.1
  289.6 3.5 all-to-all-start.10
  295.3 3.7 collective-permute-start.19
  299.0 3.0 collective-permute-start.18
  302.1 3.6 collective-permute-start.17
  313.5 3.8 convolution_convert_fusion.1
  326.8 3.9 spectrum_backward.2
  333.1 5.5 all-to-all-start.11
  343.1 4.8 conv_backward.2
  356.5 4.6 convolution_convert_fusion
  361.1 3.6 reshape.193
  370.0 5.1 inverse_backward.2
  377.8 5.1 all-to-all-start.12
  385.2 3.2 all-to-all-done.12.every_ref
  398.6 3.5 all-to-all-start.13
  404.2 3.4 all-to-all-done.13.every_ref
  415.8 4.4 spectrum_backward.3
  422.0 3.5 all-to-all-start.14
  431.0 4.2 all-to-all-start.22
  439.6 6.1 %all-to-all-done.22 = bf16[8,4,12,768]{3,1,2,0:T(4,128)(2,1)} async-done(((bf16[8,4,12,768]{3,1,2,0:T(4,128)(2,1)}), bf16[8,4,12,768]{3,1,2,0:T(4,128)(2,1)}, u32[]{:S(2)}, u32[]{:S(2)}) %all-to-all-start.22) | async-done | bytes 589856 | tf_op jit(solution)/shard_map/all_to_all | solution.py:772
  447.7 3.3 all-to-all-start.23
  452.4 5.7 inverse_backward.3
  460.1 3.5 all-to-all-start.15
  463.6 3.8 convolution_convert_fusion.2
  469.0 4.8 all-to-all-start.18
  481.8 4.8 conv_backward.3
  489.4 4.6 copy.337
  494.0 3.2 convolution_convert_fusion.3
  507.5 4.2 all-to-all-start.20
  521.6 4.3 collective-permute-start.28
  525.9 3.6 collective-permute-start.27
  531.4 4.2 all-to-all-start.19
  536.7 17.1 %all-to-all-done.19 = bf16[4,252,128]{2,1,0:T(8,128)(2,1)S(1)} async-done(((bf16[4,252,128]{2,1,0:T(8,128)(2,1)}), bf16[4,252,128]{2,1,0:T(8,128)(2,1)S(1)}, u32[]{:S(2)}, u32[]{:S(2)}) %all-to-all-start.19) | async-done | bytes 258080 | tf_op jit(solution)/shard_map/all_to_all | solution.py:774
  553.8 3.3 all-to-all-start.21
  557.7 5.2 all-to-all-done.21
  562.9 4.2 all-to-all-start.16
  574.2 19.3 %all-to-all-done.16 = bf16[8,4,252,128]{3,1,2,0:T(4,128)(2,1)S(1)} async-done(((bf16[8,4,252,128]{3,1,2,0:T(4,128)(2,1)}), bf16[8,4,252,128]{3,1,2,0:T(4,128)(2,1)S(1)}, u32[]{:S(2)}, u32[]{:S(2)}) %all-to-all-start.16) | async-done | bytes 2064416 | tf_op jit(solution)/shard_map/all_to_all | solution.py:772
  595.3 3.4 all-to-all-start.17
  600.0 5.4 all-to-all-done.17
  (568 shorter events, 266.4 us)
Async XLA Ops:
  0.6 28.9 %copy-start.143 = (bf16[1,8,64,512]{3,2,1,0:T(8,128)(2,1)S(1)}, bf16[1,8,64,512]{3,2,1,0:T(8,128)(2,1)}, u32[]{:S(2)}) copy-start(bf16[1,8,64,512]{3,2,1,0:T(8,128)(2,1)} %param.31) | copy-start | bytes 1572868
  0.7 28.9 %copy-start.144 = (bf16[1,16,32,512]{3,2,1,0:T(8,128)(2,1)S(1)}, bf16[1,16,32,512]{3,2,1,0:T(8,128)(2,1)}, u32[]{:S(2)}) copy-start(bf16[1,16,32,512]{3,2,1,0:T(8,128)(2,1)} %param.32) | copy-start | bytes 1572868
  2.3 21.1 %all-to-all-start = ((bf16[4,2,12,768]{3,1,2,0:T(2,128)(2,1)}), bf16[4,2,12,768]{3,1,2,0:T(2,128)(2,1)S(1)}, u32[]{:S(2)}, u32[]{:S(2)}) async-start(bf16[4,2,12,768]{3,1,2,0:T(2,128)(2,1)} %broadcast_in_dim.65), calls=%async_computation | async-start | bytes 294912 | tf_op jit(solution)/shard_map/all_to_all | solution.py:187
  24.5 20.1 %all-to-all-start.4 = ((bf16[4,2,252,128]{3,1,2,0:T(2,128)(2,1)}), bf16[4,2,252,128]{3,1,2,0:T(2,128)(2,1)S(1)}, u32[]{:S(2)}, u32[]{:S(2)}) async-start(bf16[4,2,252,128]{3,1,2,0:T(2,128)(2,1)} %broadcast_in_dim.71), calls=%async_computation.4 | async-start | bytes 1032192 | tf_op jit(solution)/shard_map/all_to_all | solution.py:187
  30.7 62.0 %collective-permute-start.3 = (bf16[8,32,512]{2,1,0:T(8,128)(2,1)}, bf16[8,32,512]{2,1,0:T(8,128)(2,1)}, u32[]{:S(2)}, u32[]{:S(2)}) collective-permute-start(bf16[8,32,512]{2,1,0:T(8,128)(2,1)} %get-tuple-element.315), channel_id=1, source_target_pairs={{0,2},{1,0},{2,4},{3,6},{4,3},{5,1},{6,5},{7,7},{8,10},{9,8},{10,1... | collective-permute-start | bytes 786440 | tf_op jit(solution)/shard_map/ppermute | solution.py:119
  35.5 63.3 %collective-permute-start.2 = (bf16[8,32,512]{2,1,0:T(8,128)(2,1)}, bf16[8,32,512]{2,1,0:T(8,128)(2,1)}, u32[]{:S(2)}, u32[]{:S(2)}) collective-permute-start(bf16[8,32,512]{2,1,0:T(8,128)(2,1)} %get-tuple-element.316), channel_id=1, source_target_pairs={{0,4},{2,0},{1,2},{3,6},{4,5},{6,1},{5,3},{7,7},{8,12},{10,8},{9,1... | collective-permute-start | bytes 786440 | tf_op jit(solution)/shard_map/ppermute | solution.py:119
  38.5 63.9 %collective-permute-start.1 = (bf16[8,32,512]{2,1,0:T(8,128)(2,1)}, bf16[8,32,512]{2,1,0:T(8,128)(2,1)}, u32[]{:S(2)}, u32[]{:S(2)}) collective-permute-start(bf16[8,32,512]{2,1,0:T(8,128)(2,1)} %get-tuple-element.317), channel_id=1, source_target_pairs={{0,0},{3,4},{1,2},{2,6},{4,1},{7,5},{5,3},{6,7},{8,8},{11,12},{9,1... | collective-permute-start | bytes 786440 | tf_op jit(solution)/shard_map/ppermute | solution.py:119
  42.1 60.3 %collective-permute-start = (bf16[8,32,512]{2,1,0:T(8,128)(2,1)S(1)}, bf16[8,32,512]{2,1,0:T(8,128)(2,1)}, u32[]{:S(2)}, u32[]{:S(2)}) collective-permute-start(bf16[8,32,512]{2,1,0:T(8,128)(2,1)S(1)} %get-tuple-element.314), channel_id=1, source_target_pairs={{3,0},{1,4},{0,2},{2,6},{7,1},{5,5},{4,3},{6,7},{11,8},{9,12},{8,1... | collective-permute-start | bytes 786440 | tf_op jit(solution)/shard_map/ppermute | solution.py:119
  45.6 13.6 %all-to-all-start.1 = ((bf16[4,4,2,12,768]{4,1,3,2,0:T(4,128)(2,1)}), bf16[4,4,2,12,768]{4,1,3,2,0:T(4,128)(2,1)S(1)}, u32[]{:S(2)}, u32[]{:S(2)}) async-start(bf16[4,4,2,12,768]{4,1,3,2,0:T(4,128)(2,1)} %broadcast_in_dim.66), calls=%async_computation.1 | async-start | bytes 1179648 | tf_op jit(solution)/shard_map/all_to_all | solution.py:187
  50.4 77.6 %collective-permute-start.15 = (bf16[8,32,512]{2,1,0:T(8,128)(2,1)}, bf16[8,32,512]{2,1,0:T(8,128)(2,1)}, u32[]{:S(2)}, u32[]{:S(2)}) collective-permute-start(bf16[8,32,512]{2,1,0:T(8,128)(2,1)} %get-tuple-element.305), channel_id=1, source_target_pairs={{0,2},{1,0},{2,4},{3,6},{4,3},{5,1},{6,5},{7,7},{8,10},{9,8},{10,1... | collective-permute-start | bytes 786440 | tf_op jit(solution)/shard_map/ppermute | solution.py:119
  61.0 23.8 %copy-start.150 = (s32[2,2]{1,0:T(2,128)S(1)}, s32[2,2]{1,0:T(2,128)}, u32[]{:S(2)}) copy-start(s32[2,2]{1,0:T(2,128)} %constant.184.clone) | copy-start | bytes 52
  61.0 43.5 %all-to-all-start.5 = ((bf16[4,4,2,252,128]{4,1,3,2,0:T(4,128)(2,1)}), bf16[4,4,2,252,128]{4,1,3,2,0:T(4,128)(2,1)}, u32[]{:S(2)}, u32[]{:S(2)}) async-start(bf16[4,4,2,252,128]{4,1,3,2,0:T(4,128)(2,1)} %broadcast_in_dim.72), calls=%async_computation.5 | async-start | bytes 4128768 | tf_op jit(solution)/shard_map/all_to_all | solution.py:187
  92.7 35.7 %collective-permute-start.14 = (bf16[8,32,512]{2,1,0:T(8,128)(2,1)}, bf16[8,32,512]{2,1,0:T(8,128)(2,1)}, u32[]{:S(2)}, u32[]{:S(2)}) collective-permute-start(bf16[8,32,512]{2,1,0:T(8,128)(2,1)} %get-tuple-element.306), channel_id=1, source_target_pairs={{0,4},{2,0},{1,2},{3,6},{4,5},{6,1},{5,3},{7,7},{8,12},{10,8},{9,1... | collective-permute-start | bytes 786440 | tf_op jit(solution)/shard_map/ppermute | solution.py:119
  98.8 29.6 %collective-permute-start.13 = (bf16[8,32,512]{2,1,0:T(8,128)(2,1)}, bf16[8,32,512]{2,1,0:T(8,128)(2,1)}, u32[]{:S(2)}, u32[]{:S(2)}) collective-permute-start(bf16[8,32,512]{2,1,0:T(8,128)(2,1)} %get-tuple-element.307), channel_id=1, source_target_pairs={{0,0},{3,4},{1,2},{2,6},{4,1},{7,5},{5,3},{6,7},{8,8},{11,12},{9,1... | collective-permute-start | bytes 786440 | tf_op jit(solution)/shard_map/ppermute | solution.py:119
  104.2 2.2 collective-permute-start.4
  104.6 56.5 %collective-permute-start.8 = (bf16[4,4,2,252,128]{4,1,3,2,0:T(4,128)(2,1)}, bf16[4,4,2,252,128]{4,1,3,2,0:T(4,128)(2,1)}, u32[]{:S(2)}, u32[]{:S(2)}) collective-permute-start(bf16[4,4,2,252,128]{4,1,3,2,0:T(4,128)(2,1)} %all-to-all-done.5), channel_id=1, source_target_pairs={{0,4},{4,0},{1,5},{5,1},{2,6},{6,2},{3,7},{7,3},{8,12},{12,8},{9,1... | collective-permute-start | bytes 6193160 | tf_op jit(solution)/shard_map/ppermute | solution.py:599
  106.4 22.1 %collective-permute-start.12 = (bf16[8,32,512]{2,1,0:T(8,128)(2,1)}, bf16[8,32,512]{2,1,0:T(8,128)(2,1)}, u32[]{:S(2)}, u32[]{:S(2)}) collective-permute-start(bf16[8,32,512]{2,1,0:T(8,128)(2,1)} %get-tuple-element.304), channel_id=1, source_target_pairs={{3,0},{1,4},{0,2},{2,6},{7,1},{5,5},{4,3},{6,7},{11,8},{9,12},{8,1... | collective-permute-start | bytes 786440 | tf_op jit(solution)/shard_map/ppermute | solution.py:119
  120.9 12.5 %all-to-all-start.2 = ((f32[16,2,192]{2,1,0:T(2,128)}), f32[16,2,192]{2,1,0:T(2,128)S(1)}, u32[]{:S(2)}, u32[]{:S(2)}) async-start(f32[16,2,192]{2,1,0:T(2,128)} %get-tuple-element.91), calls=%async_computation.2 | async-start | bytes 65536 | tf_op jit(solution)/shard_map/all_to_all | solution.py:669
  128.0 10.6 %collective-permute-start.7 = (bf16[32,512]{1,0:T(8,128)(2,1)S(1)}, bf16[32,512]{1,0:T(8,128)(2,1)S(1)}, u32[]{:S(2)}, u32[]{:S(2)}) collective-permute-start(bf16[32,512]{1,0:T(8,128)(2,1)S(1)} %fusion.7), channel_id=1, source_target_pairs={{0,4},{4,0},{1,5},{5,1},{2,6},{6,2},{3,7},{7,3},{8,12},{12,8},{9,1... | collective-permute-start | bytes 98312 | tf_op jit(solution)/shard_map/ppermute | solution.py:159
  134.5 8.0 %collective-permute-start.5 = (bf16[1024,192]{1,0:T(8,128)(2,1)S(1)}, bf16[1024,192]{1,0:T(8,128)(2,1)S(1)}, u32[]{:S(2)}, u32[]{:S(2)}) collective-permute-start(bf16[1024,192]{1,0:T(8,128)(2,1)S(1)} %get-tuple-element.92.own_ref), channel_id=1, source_target_pairs={{4,0},{0,4},{5,1},{1,5},{6,2},{2,6},{7,3},{3,7},{12,8},{8,12},{13,... | collective-permute-start | bytes 1179656 | tf_op jit(solution)/shard_map/ppermute | solution.py:145
  149.0 9.2 %all-to-all-start.3 = ((f32[16,2,384]{2,1,0:T(2,128)}), f32[16,2,384]{2,1,0:T(2,128)S(1)}, u32[]{:S(2)}, u32[]{:S(2)}) async-start(f32[16,2,384]{2,1,0:T(2,128)} %copy-done.98), calls=%async_computation.3 | async-start | bytes 98304 | tf_op jit(solution)/shard_map/all_to_all | solution.py:669
  161.0 17.8 %collective-permute-start.6 = (bf16[544,384]{1,0:T(8,128)(2,1)}, bf16[544,384]{1,0:T(8,128)(2,1)}, u32[]{:S(2)}, u32[]{:S(2)}) collective-permute-start(bf16[544,384]{1,0:T(8,128)(2,1)} %get-tuple-element.95.own_ref), channel_id=1, source_target_pairs={{4,0},{0,4},{5,1},{1,5},{6,2},{2,6},{7,3},{3,7},{12,8},{8,12},{13,... | collective-permute-start | bytes 1253384 | tf_op jit(solution)/shard_map/ppermute | solution.py:145
  186.1 14.8 %all-to-all-start.6 = ((f32[16,2,512]{2,1,0:T(2,128)}), f32[16,2,512]{2,1,0:T(2,128)S(1)}, u32[]{:S(2)}, u32[]{:S(2)}) async-start(f32[16,2,512]{2,1,0:T(2,128)} %copy-done.93), calls=%async_computation.6 | async-start | bytes 131072 | tf_op jit(solution)/shard_map/all_to_all | solution.py:669
  206.7 11.2 %collective-permute-start.11 = (bf16[32,512]{1,0:T(8,128)(2,1)}, bf16[32,512]{1,0:T(8,128)(2,1)}, u32[]{:S(2)}, u32[]{:S(2)}) collective-permute-start(bf16[32,512]{1,0:T(8,128)(2,1)} %fusion.14), channel_id=1, source_target_pairs={{0,4},{4,0},{1,5},{5,1},{2,6},{6,2},{3,7},{7,3},{8,12},{12,8},{9,1... | collective-permute-start | bytes 98312 | tf_op jit(solution)/shard_map/ppermute | solution.py:159
  212.9 17.3 %all-to-all-start.7 = ((f32[16,2,192]{2,1,0:T(2,128)}), f32[16,2,192]{2,1,0:T(2,128)S(1)}, u32[]{:S(2)}, u32[]{:S(2)}) async-start(f32[16,2,192]{2,1,0:T(2,128)} %get-tuple-element.101), calls=%async_computation.7 | async-start | bytes 65536 | tf_op jit(solution)/shard_map/all_to_all | solution.py:669
  232.4 3.9 collective-permute-start.9
  236.3 18.1 %copy-start.87 = (f32[2,384]{1,0:T(2,128)S(1)}, f32[2,384]{1,0:T(2,128)}, u32[]{:S(2)}) copy-start(f32[2,384]{1,0:T(2,128)} %g_ref.29) | copy-start | bytes 9220
  236.3 18.1 %copy-start.101 = (f32[2,384]{1,0:T(2,128)S(1)}, f32[2,384]{1,0:T(2,128)}, u32[]{:S(2)}) copy-start(f32[2,384]{1,0:T(2,128)} %b_ref.18) | copy-start | bytes 9220
  243.8 10.5 %all-to-all-start.8 = ((f32[16,2,384]{2,1,0:T(2,128)}), f32[16,2,384]{2,1,0:T(2,128)S(1)}, u32[]{:S(2)}, u32[]{:S(2)}) async-start(f32[16,2,384]{2,1,0:T(2,128)} %copy-done.99), calls=%async_computation.8 | async-start | bytes 98304 | tf_op jit(solution)/shard_map/all_to_all | solution.py:669
  256.2 3.6 collective-permute-start.10
  270.3 9.5 %all-to-all-start.9 = ((f32[16,2,512]{2,1,0:T(2,128)}), f32[16,2,512]{2,1,0:T(2,128)S(1)}, u32[]{:S(2)}, u32[]{:S(2)}) async-start(f32[16,2,512]{2,1,0:T(2,128)} %copy-done.96), calls=%async_computation.9 | async-start | bytes 131072 | tf_op jit(solution)/shard_map/all_to_all | solution.py:669
  289.6 16.1 %all-to-all-start.10 = ((f32[16,2,512]{2,1,0:T(2,128)}), f32[16,2,512]{2,1,0:T(2,128)S(1)}, u32[]{:S(2)}, u32[]{:S(2)}) async-start(f32[16,2,512]{2,1,0:T(2,128)} %copy-done.94), calls=%async_computation.10 | async-start | bytes 131072 | tf_op jit(solution)/shard_map/all_to_all | solution.py:669
  295.3 87.5 %collective-permute-start.19 = (bf16[8,32,512]{2,1,0:T(8,128)(2,1)}, bf16[8,32,512]{2,1,0:T(8,128)(2,1)}, u32[]{:S(2)}, u32[]{:S(2)}) collective-permute-start(bf16[8,32,512]{2,1,0:T(8,128)(2,1)} %get-tuple-element.297), channel_id=1, source_target_pairs={{2,0},{0,1},{4,2},{6,3},{3,4},{1,5},{5,6},{7,7},{10,8},{8,9},{12,1... | collective-permute-start | bytes 786440 | tf_op jit(solution)/shard_map/ppermute | solution.py:132
  299.0 83.9 %collective-permute-start.18 = (bf16[8,32,512]{2,1,0:T(8,128)(2,1)}, bf16[8,32,512]{2,1,0:T(8,128)(2,1)}, u32[]{:S(2)}, u32[]{:S(2)}) collective-permute-start(bf16[8,32,512]{2,1,0:T(8,128)(2,1)} %get-tuple-element.298), channel_id=1, source_target_pairs={{4,0},{0,2},{2,1},{6,3},{5,4},{1,6},{3,5},{7,7},{12,8},{8,10},{10,... | collective-permute-start | bytes 786440 | tf_op jit(solution)/shard_map/ppermute | solution.py:132
  302.1 80.8 %collective-permute-start.17 = (bf16[8,32,512]{2,1,0:T(8,128)(2,1)}, bf16[8,32,512]{2,1,0:T(8,128)(2,1)}, u32[]{:S(2)}, u32[]{:S(2)}) collective-permute-start(bf16[8,32,512]{2,1,0:T(8,128)(2,1)} %get-tuple-element.299), channel_id=1, source_target_pairs={{0,0},{4,3},{2,1},{6,2},{1,4},{5,7},{3,5},{7,6},{8,8},{12,11},{10,... | collective-permute-start | bytes 786440 | tf_op jit(solution)/shard_map/ppermute | solution.py:132
  312.3 10.7 %collective-permute-start.20 = (bf16[1024,192]{1,0:T(8,128)(2,1)}, bf16[1024,192]{1,0:T(8,128)(2,1)}, u32[]{:S(2)}, u32[]{:S(2)}) collective-permute-start(bf16[1024,192]{1,0:T(8,128)(2,1)} %get-tuple-element.115.own_ref), channel_id=1, source_target_pairs={{4,0},{0,4},{5,1},{1,5},{6,2},{2,6},{7,3},{3,7},{12,8},{8,12},{13,... | collective-permute-start | bytes 1179656 | tf_op jit(solution)/shard_map/ppermute | solution.py:145
  313.0 25.6 %collective-permute-start.22 = (bf16[32,512]{1,0:T(8,128)(2,1)}, bf16[32,512]{1,0:T(8,128)(2,1)}, u32[]{:S(2)}, u32[]{:S(2)}) collective-permute-start(bf16[32,512]{1,0:T(8,128)(2,1)} %fusion.12), channel_id=1, source_target_pairs={{0,4},{4,0},{1,5},{5,1},{2,6},{6,2},{3,7},{7,3},{8,12},{12,8},{9,1... | collective-permute-start | bytes 98312 | tf_op jit(solution)/shard_map/ppermute | solution.py:159
  323.0 59.9 %collective-permute-start.16 = (bf16[8,32,512]{2,1,0:T(8,128)(2,1)}, bf16[8,32,512]{2,1,0:T(8,128)(2,1)}, u32[]{:S(2)}, u32[]{:S(2)}) collective-permute-start(bf16[8,32,512]{2,1,0:T(8,128)(2,1)} %get-tuple-element.296), channel_id=1, source_target_pairs={{0,3},{4,1},{2,0},{6,2},{1,7},{5,5},{3,4},{7,6},{8,11},{12,9},{10,... | collective-permute-start | bytes 786440 | tf_op jit(solution)/shard_map/ppermute | solution.py:132
  333.1 17.6 %all-to-all-start.11 = ((f32[16,2,384]{2,1,0:T(2,128)}), f32[16,2,384]{2,1,0:T(2,128)S(1)}, u32[]{:S(2)}, u32[]{:S(2)}) async-start(f32[16,2,384]{2,1,0:T(2,128)} %copy-done.97), calls=%async_computation.11 | async-start | bytes 98304 | tf_op jit(solution)/shard_map/all_to_all | solution.py:669
  356.0 14.0 %collective-permute-start.21 = (bf16[544,384]{1,0:T(8,128)(2,1)}, bf16[544,384]{1,0:T(8,128)(2,1)}, u32[]{:S(2)}, u32[]{:S(2)}) collective-permute-start(bf16[544,384]{1,0:T(8,128)(2,1)} %get-tuple-element.120.own_ref), channel_id=1, source_target_pairs={{4,0},{0,4},{5,1},{1,5},{6,2},{2,6},{7,3},{3,7},{12,8},{8,12},{13,... | collective-permute-start | bytes 1253384 | tf_op jit(solution)/shard_map/ppermute | solution.py:145
  370.0 18.4 %copy-start.89 = (f32[2,512]{1,0:T(2,128)S(1)}, f32[2,512]{1,0:T(2,128)}, u32[]{:S(2)}) copy-start(f32[2,512]{1,0:T(2,128)} %g_ref.27) | copy-start | bytes 12292
  370.0 18.4 %copy-start.103 = (f32[2,512]{1,0:T(2,128)S(1)}, f32[2,512]{1,0:T(2,128)}, u32[]{:S(2)}) copy-start(f32[2,512]{1,0:T(2,128)} %b3_ref.1) | copy-start | bytes 12292
  370.0 18.4 %copy-start.109 = (f32[2,512]{1,0:T(2,128)S(1)}, f32[2,512]{1,0:T(2,128)}, u32[]{:S(2)}) copy-start(f32[2,512]{1,0:T(2,128)} %copy-done.108) | copy-start | bytes 12292
  377.8 10.6 %all-to-all-start.12 = ((f32[16,2,192]{2,1,0:T(2,128)}), f32[16,2,192]{2,1,0:T(2,128)S(1)}, u32[]{:S(2)}, u32[]{:S(2)}) async-start(f32[16,2,192]{2,1,0:T(2,128)} %copy-done.107), calls=%async_computation.12 | async-start | bytes 65536 | tf_op jit(solution)/shard_map/all_to_all | solution.py:669
  398.6 9.0 %all-to-all-start.13 = ((f32[16,2,512]{2,1,0:T(2,128)}), f32[16,2,512]{2,1,0:T(2,128)S(1)}, u32[]{:S(2)}, u32[]{:S(2)}) async-start(f32[16,2,512]{2,1,0:T(2,128)} %copy-done.95), calls=%async_computation.13 | async-start | bytes 131072 | tf_op jit(solution)/shard_map/all_to_all | solution.py:669
  413.7 2.1 collective-permute-start.23
  422.0 9.0 %all-to-all-start.14 = ((f32[16,2,384]{2,1,0:T(2,128)}), f32[16,2,384]{2,1,0:T(2,128)S(1)}, u32[]{:S(2)}, u32[]{:S(2)}) async-start(f32[16,2,384]{2,1,0:T(2,128)} %get-tuple-element.135), calls=%async_computation.14 | async-start | bytes 98304 | tf_op jit(solution)/shard_map/all_to_all | solution.py:669
  431.0 14.7 %all-to-all-start.22 = ((bf16[8,4,12,768]{3,1,2,0:T(4,128)(2,1)}), bf16[8,4,12,768]{3,1,2,0:T(4,128)(2,1)}, u32[]{:S(2)}, u32[]{:S(2)}) async-start(bf16[8,4,12,768]{3,1,2,0:T(4,128)(2,1)} %copy.352), calls=%async_computation.22 | async-start | bytes 1179648 | tf_op jit(solution)/shard_map/all_to_all | solution.py:772
  439.1 12.0 %collective-permute-start.24 = (bf16[544,384]{1,0:T(8,128)(2,1)}, bf16[544,384]{1,0:T(8,128)(2,1)}, u32[]{:S(2)}, u32[]{:S(2)}) collective-permute-start(bf16[544,384]{1,0:T(8,128)(2,1)} %get-tuple-element.136.own_ref), channel_id=1, source_target_pairs={{4,0},{0,4},{5,1},{1,5},{6,2},{2,6},{7,3},{3,7},{12,8},{8,12},{13,... | collective-permute-start | bytes 1253384 | tf_op jit(solution)/shard_map/ppermute | solution.py:145
  447.7 12.4 %all-to-all-start.23 = ((bf16[4,12,768]{2,1,0:T(8,128)(2,1)}), bf16[4,12,768]{2,1,0:T(8,128)(2,1)S(1)}, u32[]{:S(2)}, u32[]{:S(2)}) async-start(bf16[4,12,768]{2,1,0:T(8,128)(2,1)} %copy.353), calls=%async_computation.23 | async-start | bytes 196608 | tf_op jit(solution)/shard_map/all_to_all | solution.py:774
  451.0 29.5 %collective-permute-start.25 = (bf16[32,512]{1,0:T(8,128)(2,1)S(1)}, bf16[32,512]{1,0:T(8,128)(2,1)S(1)}, u32[]{:S(2)}, u32[]{:S(2)}) collective-permute-start(bf16[32,512]{1,0:T(8,128)(2,1)S(1)} %fusion.10), channel_id=1, source_target_pairs={{0,4},{4,0},{1,5},{5,1},{2,6},{6,2},{3,7},{7,3},{8,12},{12,8},{9,1... | collective-permute-start | bytes 98312 | tf_op jit(solution)/shard_map/ppermute | solution.py:159
  460.1 9.0 %all-to-all-start.15 = ((f32[16,2,192]{2,1,0:T(2,128)}), f32[16,2,192]{2,1,0:T(2,128)S(1)}, u32[]{:S(2)}, u32[]{:S(2)}) async-start(f32[16,2,192]{2,1,0:T(2,128)} %get-tuple-element.141), calls=%async_computation.15 | async-start | bytes 65536 | tf_op jit(solution)/shard_map/all_to_all | solution.py:669
  469.0 38.4 %all-to-all-start.18 = ((bf16[8,4,252,128]{3,1,2,0:T(4,128)(2,1)}), bf16[8,4,252,128]{3,1,2,0:T(4,128)(2,1)}, u32[]{:S(2)}, u32[]{:S(2)}) async-start(bf16[8,4,252,128]{3,1,2,0:T(4,128)(2,1)} %copy.342), calls=%async_computation.18 | async-start | bytes 4128768 | tf_op jit(solution)/shard_map/all_to_all | solution.py:772
  507.5 23.9 %all-to-all-start.20 = ((bf16[8,4,12,768]{3,1,2,0:T(4,128)(2,1)}), bf16[8,4,12,768]{3,1,2,0:T(4,128)(2,1)S(1)}, u32[]{:S(2)}, u32[]{:S(2)}) async-start(bf16[8,4,12,768]{3,1,2,0:T(4,128)(2,1)} %copy.348), calls=%async_computation.20 | async-start | bytes 1179648 | tf_op jit(solution)/shard_map/all_to_all | solution.py:772
  515.2 16.2 %collective-permute-start.30 = (f32[2,2176]{1,0:T(2,128)S(1)}, f32[2,2176]{1,0:T(2,128)S(1)}, u32[]{:S(2)}, u32[]{:S(2)}) collective-permute-start(f32[2,2176]{1,0:T(2,128)S(1)} %concatenate.87), channel_id=1, source_target_pairs={{0,2},{2,0},{1,3},{3,1},{4,6},{6,4},{5,7},{7,5},{8,10},{10,8},{9,1... | collective-permute-start | bytes 52232 | tf_op jit(solution)/shard_map/ppermute | solution.py:755
  519.1 51.1 %collective-permute-start.29 = (bf16[8,32,512]{2,1,0:T(8,128)(2,1)}, bf16[8,32,512]{2,1,0:T(8,128)(2,1)}, u32[]{:S(2)}, u32[]{:S(2)}) collective-permute-start(bf16[8,32,512]{2,1,0:T(8,128)(2,1)} %get-tuple-element.285), channel_id=1, source_target_pairs={{2,0},{0,1},{4,2},{6,3},{3,4},{1,5},{5,6},{7,7},{10,8},{8,9},{12,1... | collective-permute-start | bytes 786440 | tf_op jit(solution)/shard_map/ppermute | solution.py:132
  521.6 48.7 %collective-permute-start.28 = (bf16[8,32,512]{2,1,0:T(8,128)(2,1)}, bf16[8,32,512]{2,1,0:T(8,128)(2,1)}, u32[]{:S(2)}, u32[]{:S(2)}) collective-permute-start(bf16[8,32,512]{2,1,0:T(8,128)(2,1)} %get-tuple-element.286), channel_id=1, source_target_pairs={{4,0},{0,2},{2,1},{6,3},{5,4},{1,6},{3,5},{7,7},{12,8},{8,10},{10,... | collective-permute-start | bytes 786440 | tf_op jit(solution)/shard_map/ppermute | solution.py:132
  525.9 44.4 %collective-permute-start.27 = (bf16[8,32,512]{2,1,0:T(8,128)(2,1)}, bf16[8,32,512]{2,1,0:T(8,128)(2,1)}, u32[]{:S(2)}, u32[]{:S(2)}) collective-permute-start(bf16[8,32,512]{2,1,0:T(8,128)(2,1)} %get-tuple-element.287), channel_id=1, source_target_pairs={{0,0},{4,3},{2,1},{6,2},{1,4},{5,7},{3,5},{7,6},{8,8},{12,11},{10,... | collective-permute-start | bytes 786440 | tf_op jit(solution)/shard_map/ppermute | solution.py:132
  529.5 40.8 %collective-permute-start.26 = (bf16[8,32,512]{2,1,0:T(8,128)(2,1)}, bf16[8,32,512]{2,1,0:T(8,128)(2,1)}, u32[]{:S(2)}, u32[]{:S(2)}) collective-permute-start(bf16[8,32,512]{2,1,0:T(8,128)(2,1)} %get-tuple-element.284), channel_id=1, source_target_pairs={{0,3},{4,1},{2,0},{6,2},{1,7},{5,5},{3,4},{7,6},{8,11},{12,9},{10,... | collective-permute-start | bytes 786440 | tf_op jit(solution)/shard_map/ppermute | solution.py:132
  531.4 22.4 %all-to-all-start.19 = ((bf16[4,252,128]{2,1,0:T(8,128)(2,1)}), bf16[4,252,128]{2,1,0:T(8,128)(2,1)S(1)}, u32[]{:S(2)}, u32[]{:S(2)}) async-start(bf16[4,252,128]{2,1,0:T(8,128)(2,1)} %copy.343), calls=%async_computation.19 | async-start | bytes 524288 | tf_op jit(solution)/shard_map/all_to_all | solution.py:774
  553.8 9.1 %all-to-all-start.21 = ((bf16[4,12,768]{2,1,0:T(8,128)(2,1)}), bf16[4,12,768]{2,1,0:T(8,128)(2,1)S(1)}, u32[]{:S(2)}, u32[]{:S(2)}) async-start(bf16[4,12,768]{2,1,0:T(8,128)(2,1)} %copy.349), calls=%async_computation.21 | async-start | bytes 196608 | tf_op jit(solution)/shard_map/all_to_all | solution.py:774
  562.9 30.5 %all-to-all-start.16 = ((bf16[8,4,252,128]{3,1,2,0:T(4,128)(2,1)}), bf16[8,4,252,128]{3,1,2,0:T(4,128)(2,1)S(1)}, u32[]{:S(2)}, u32[]{:S(2)}) async-start(bf16[8,4,252,128]{3,1,2,0:T(4,128)(2,1)} %pad_maximum_fusion.2), calls=%async_computation.16 | async-start | bytes 4128768 | tf_op jit(solution)/shard_map/all_to_all | solution.py:772
  574.2 32.1 %slice-start = ((f32[252,128]{1,0:T(8,128)}), f32[144,128]{1,0:T(8,128)S(1)}, s32[]{:S(2)}) async-start(f32[252,128]{1,0:T(8,128)} %copy-done.142), calls=%async_computation.24 | async-start | bytes 147456 | tf_op jit(solution)/shard_map/slice | solution.py:747
  595.3 10.2 %all-to-all-start.17 = ((bf16[4,252,128]{2,1,0:T(8,128)(2,1)}), bf16[4,252,128]{2,1,0:T(8,128)(2,1)S(1)}, u32[]{:S(2)}, u32[]{:S(2)}) async-start(bf16[4,252,128]{2,1,0:T(8,128)(2,1)} %copy.340), calls=%async_computation.17 | async-start | bytes 524288 | tf_op jit(solution)/shard_map/all_to_all | solution.py:774
  (147 other events, 552.4 us)

commit v3 on v1

v3 whole, which is shorter than its diff:
```python
import math

import jax
import jax.numpy as jnp
import numpy as np
from jax import lax
from jax.experimental import pallas as pl
from jax.experimental.pallas import tpu as pltpu
from jax.sharding import Mesh, PartitionSpec as P

EPS = 1e-05
LINE = ("c", "k", "z", "e")
KIND = ("g", "c", "z", "e")
PART = ("c", "e")
ALL = ("g", "c", "k", "z", "e")
f32 = jnp.float32
bf16 = jnp.bfloat16


def routes(e_n):
    s_n = 4 * e_n
    count = 2 * s_n
    left = []
    for c in range(2):
        for s in range(s_n):
            for unit in range(4):
                kind, half = unit // 2, unit % 2
                left.append((c * s_n + s, unit, half * s_n + (kind * 2 + c) * e_n + s // 4, s % 4))
    rounds = []
    for _ in range(4):
        owner = {}

        def augment(src, seen):
            for edge in left:
                if edge[0] == src and edge[2] not in seen:
                    seen.add(edge[2])
                    if edge[2] not in owner or augment(owner[edge[2]][0], seen):
                        owner[edge[2]] = edge
                        return True
            return False

        for src in range(count):
            assert augment(src, set())
        chosen = list(owner.values())
        for edge in chosen:
            left.remove(edge)
        sent = np.zeros(count, np.int32)
        slot = np.zeros(count, np.int32)
        for edge in chosen:
            sent[edge[0]] = edge[1]
            slot[edge[2]] = edge[3]
        rounds.append(([(edge[0], edge[2]) for edge in chosen], sent, slot))
    return rounds


def transform_tables(e_n, land_shape, port_shape):
    parts = 2 * e_n
    shapes = (land_shape, port_shape)
    most = max(rows * (cols // 2 + 1) for rows, cols in shapes)
    per_part = -(-most // (16 * parts)) * 16
    forward, inverse, weight, counts = [], [], [], []
    for rows, cols in shapes:
        half = cols // 2 + 1
        point = np.arange(per_part * parts)
        valid = point < rows * half
        kr, f = point // half, point % half
        tiles = []
        for part in range(parts):
            c, e = part // e_n, part % e_n
            h = np.arange(rows // e_n) + e * (rows // e_n)
            w = np.arange(cols // 2) + c * (cols // 2)
            tiles.append((np.repeat(h, len(w)), np.tile(w, len(h))))
        cell_h = np.concatenate([tile[0] for tile in tiles])
        cell_w = np.concatenate([tile[1] for tile in tiles])
        size = rows * cols
        phase = (kr[:, None] * cell_h[None, :] * cols + f[:, None] * cell_w[None, :] * rows) % size
        angle = phase * (2.0 * math.pi / size)
        table = np.stack([np.cos(angle), -np.sin(angle)]) * valid[None, :, None]
        table = table.astype(np.float32).astype(jnp.bfloat16)
        cells = size // parts
        factor = np.where((f == 0) | (2 * f == cols), 1.0, 2.0) * valid
        counts.append([int(valid[p * per_part : (p + 1) * per_part].sum()) for p in range(parts)])
        for part in range(parts):
            order = [(part + step) % parts for step in range(parts)]
            own_points = slice(part * per_part, (part + 1) * per_part)
            own_cells = slice(part * cells, (part + 1) * cells)
            forward.append(
                np.concatenate([table[:, own_points, q * cells : (q + 1) * cells] for q in order], axis=2)
            )
            back = np.concatenate([table[:, q * per_part : (q + 1) * per_part, own_cells] for q in order], axis=1)
            inverse.append(np.ascontiguousarray(back.transpose(0, 2, 1)))
            weight.append(factor[own_points].astype(np.float32))
    return np.stack(forward), np.stack(inverse), np.stack(weight), np.asarray(counts, np.int32)


SWAP = [(0, 1), (1, 0)]


def pick(table, index):
    return lax.dynamic_index_in_dim(jnp.asarray(table), index, 0, keepdims=False)


def partners(pieces, axes, step):
    count = lax.axis_size(axes)
    return lax.ppermute(pieces, axes, [(i, i ^ step) for i in range(count)])


def split_halves(land, port, place):
    channels = land.shape[3]
    shapes = [maps.shape[1:3] for maps in (land, port)]
    cells = shapes[0][0] * shapes[0][1] // 2

    def body(land_ref, port_ref, place_ref, mine_ref, theirs_ref):
        c = place_ref[1]
        for kind, ref in enumerate((land_ref, port_ref)):
            half = shapes[kind][1] // 2
            for out_ref, core in ((mine_ref, c), (theirs_ref, 1 - c)):
                at = pl.ds(pl.multiple_of(core * half, half), half)
                out_ref[kind] = ref[0, :, at, :].reshape(cells, channels)

    outs = [shape((2, cells, channels), land.dtype)] * 2
    return run(body, outs, (land, port, place), "split_halves", scalars=1)


def join_halves(mine, theirs, like, place):
    def body(mine_ref, theirs_ref, place_ref, *out_refs):
        c = place_ref[1]
        for kind, out_ref in enumerate(out_refs):
            _, rows, cols, channels = out_ref.shape
            half = cols // 2
            for ref, core in ((mine_ref, c), (theirs_ref, 1 - c)):
                at = pl.ds(pl.multiple_of(core * half, half), half)
                out_ref[0, :, at, :] = ref[kind].reshape(rows, half, channels)

    return run(body, [shape(maps.shape, maps.dtype) for maps in like], (mine, theirs, place), "join_halves", scalars=1)


def to_slots(mine, theirs, place, lanes):
    channels = lanes.stop - lanes.start

    def body(mine_ref, theirs_ref, place_ref, *out_refs):
        here, c = place_ref[2], place_ref[1]
        for step, out_ref in enumerate(out_refs):
            there = here ^ step
            kind, core = there // 2, there % 2

            @pl.when(core == c)
            def _():
                out_ref[...] = mine_ref[kind, :, lanes]

            @pl.when(core != c)
            def _():
                out_ref[...] = theirs_ref[kind, :, lanes]

    outs = [shape((mine.shape[1], channels), mine.dtype)] * 4
    return run(body, outs, (mine, theirs, place), "to_slots", scalars=1)


def from_slots(pieces, place):
    def body(*refs):
        place_ref, mine_ref, theirs_ref = refs[-3:]
        here, c = place_ref[2], place_ref[1]
        for step in range(4):
            there = here ^ step
            kind, core = there // 2, there % 2

            @pl.when(core == c)
            def _():
                mine_ref[kind] = refs[step][...]

            @pl.when(core != c)
            def _():
                theirs_ref[kind] = refs[step][...]

    outs = [shape((2,) + pieces[0].shape, pieces[0].dtype)] * 2
    return run(body, outs, (*pieces, place), "from_slots", scalars=1)


def in_order(pieces, here):
    rows = pieces[0].shape[0]

    def body(*refs):
        here_ref, out_ref = refs[-2:]
        for step in range(len(pieces)):
            out_ref[here_ref[0] ^ step] = refs[step][...]

    outs = [shape((len(pieces),) + pieces[0].shape, pieces[0].dtype)]
    out = run(body, outs, (*pieces, here), "in_order", scalars=1)[0]
    return out.reshape((len(pieces) * rows,) + pieces[0].shape[1:])


def join_lanes(pieces, rest, here):
    rows, first = pieces[0].shape
    channels = first + rest.shape[1]
    count = len(pieces)

    def body(*refs):
        rest_ref, here_ref, out_ref = refs[count:]
        out_ref[:, first:] = rest_ref[...]
        for step in range(count):
            at = pl.ds(pl.multiple_of((here_ref[0] ^ step) * rows, 16), rows)
            out_ref[at, :first] = refs[step][...]

    return run(body, [shape((count * rows, channels), rest.dtype)], (*pieces, rest, here), "join_lanes", scalars=1)[0]


def for_partners(blocks, here, lanes):
    count, rows = blocks.shape[:2]

    def body(blocks_ref, here_ref, *out_refs):
        for step in range(count):
            out_refs[step][...] = blocks_ref[here_ref[0] ^ step, :, lanes]

    outs = [shape((rows, lanes.stop - lanes.start), blocks.dtype)] * count
    return run(body, outs, (blocks, here), "for_partners", scalars=1)


def advance(steps):
    return next(steps)


def finish(steps):
    while True:
        try:
            next(steps)
        except StopIteration as stop:
            return stop.value


def over_line(pieces):
    axes = ("k", "z", "e")
    return [pieces[0]] + [partners(pieces[step], axes, step) for step in range(1, lax.axis_size(axes))]


def over_plane(pieces):
    return [pieces[0]] + [partners(pieces[step], "g", step) for step in range(1, lax.axis_size("g"))]


def to_tile(land, port, rounds, place, here, narrow=0):
    channels = land.shape[3]
    if lax.axis_size("e") == 1:
        mine, theirs = split_halves(land, port, place)
        theirs = lax.ppermute(theirs, "c", SWAP)
        yield
        pieces = over_line(to_slots(mine, theirs, place, slice(narrow, channels)))
        if narrow:
            first = over_line(to_slots(mine, theirs, place, slice(0, narrow)))
        yield
        broad = in_order(pieces, here[0])
        if not narrow:
            return broad
        yield broad
        return join_lanes(first, broad, here[0])
    me = lax.axis_index(LINE)
    units = []
    for maps in (land, port):
        cols = maps.shape[2] // 2
        units += [maps[0, :, :cols].reshape(-1, channels), maps[0, :, cols:].reshape(-1, channels)]
    units = jnp.stack(units)
    got = [lax.ppermute(pick(units, pick(sent, me)), LINE, pairs) for pairs, sent, _ in rounds]
    yield
    slots = np.stack([slot for _, _, slot in rounds], axis=1)
    order = pick(np.argsort(slots, axis=1).astype(np.int32), me)
    yield
    tile = jnp.concatenate([pick(jnp.stack(got), order[i]) for i in range(4)], axis=0)
    if narrow:
        yield tile[:, narrow:]
    return tile


def from_tile(tile, rounds, place, here, lanes=None):
    lanes = lanes or slice(0, tile.shape[1])
    units = tile.reshape(4, -1, tile.shape[1])
    if lax.axis_size("e") == 1:
        pieces = over_line(for_partners(units, here[0], lanes))
        yield
        mine, theirs = from_slots(pieces, place)
        return mine, lax.ppermute(theirs, "c", SWAP)
    units = units[:, :, lanes]
    me = lax.axis_index(LINE)
    got = [lax.ppermute(pick(units, pick(slot, me)), LINE, [(b, a) for a, b in pairs]) for pairs, _, slot in rounds]
    yield
    sents = np.stack([sent for _, sent, _ in rounds], axis=1)
    order = pick(np.argsort(sents, axis=1).astype(np.int32), me)
    both = jnp.stack([pick(jnp.stack(got), order[i]) for i in range(4)]).reshape((2, 2) + units.shape[1:])
    c = lax.axis_index("c")
    return (
        lax.dynamic_index_in_dim(both, c, 1, keepdims=False),
        lax.dynamic_index_in_dim(both, 1 - c, 1, keepdims=False),
    )


def shared(block):
    parts = lax.axis_size(PART)
    pieces = [
        lax.ppermute(block, PART, [((p + step) % parts, p) for p in range(parts)]) for step in range(1, parts)
    ]
    return pieces[0] if parts == 2 else jnp.concatenate(pieces, axis=0)


def gelu_parts(v):
    k = math.sqrt(2.0 / math.pi)
    square = v * v
    t = jnp.tanh(k * v * (1.0 + 0.044715 * square))
    half = 0.5 * (1.0 + t)
    return v * half, half + 0.5 * v * (1.0 - t * t) * (k * (1.0 + 3.0 * 0.044715 * square))


def gelu(v):
    return 0.5 * v * (1.0 + jnp.tanh(math.sqrt(2.0 / math.pi) * v * (1.0 + 0.044715 * (v * v))))


def dot(a, b):
    return lax.dot_general(a, b, (((1,), (0,)), ((), ())), preferred_element_type=f32)


def dot_t(a, b):
    return lax.dot_general(a, b, (((1,), (1,)), ((), ())), preferred_element_type=f32)


def outer(a, b):
    return lax.dot_general(a, b, (((0,), (0,)), ((), ())), preferred_element_type=f32)


def device_counts(counts, kind, width, e_n, z_n):
    row = lax.broadcasted_iota(jnp.int32, (width, 1), 0)
    part = row // (e_n * z_n) % 2 * e_n + row % e_n
    out = jnp.zeros((width, 1), f32)
    for p in range(len(counts[0])):
        out = jnp.where(part == p, jnp.where(kind == 0, float(counts[0][p]), float(counts[1][p])), out)
    return out


def moments(every, counts, total):
    sums, squares = every[:, 0, :], every[:, 1, :]
    mean = jnp.sum(sums, axis=0, keepdims=True) / total
    apart = sums / counts - mean
    square = jnp.sum(squares + counts * apart * apart, axis=0, keepdims=True)
    return mean, lax.rsqrt(square / total + EPS)


def emit(out_ref, first, second):
    both = jnp.concatenate([first, second], axis=0)
    out_ref[...] = jnp.broadcast_to(both[None], out_ref.shape)


def row_step(rows):
    return next(step for step in (64, 32, 16, 8) if rows % step == 0)


def sweep(rows, body, carry=0, step=None):
    step = step or row_step(rows)
    if rows == step:
        return body(slice(0, rows), carry)
    return lax.fori_loop(0, rows // step, lambda i, carry: body(pl.ds(pl.multiple_of(i * step, step), step), carry), carry)


def folded(values):
    return jnp.sum(values.reshape(values.shape[0] // 8, 8, values.shape[1]), axis=0)


def column(values):
    return jnp.sum(values, axis=0, keepdims=True)


def emit_moments(out_ref, ref, count, factor_ref=None):
    rows, columns = ref.shape
    zero = jnp.zeros((8, columns), f32)
    local_sum = column(sweep(rows, lambda at, acc: acc + folded(ref[at, :]), zero))
    mean = local_sum / count

    def squares(at, acc):
        centered = ref[at, :] - mean
        if factor_ref is not None:
            centered = jnp.where(factor_ref[at, :] > 0.0, centered, 0.0)
        return acc + folded(centered * centered)

    emit(out_ref, local_sum, column(sweep(rows, squares, zero)))


def pair(columns):
    return jnp.zeros((8, columns), f32), jnp.zeros((8, columns), f32)


def add_sums(sums, q, normed):
    return sums[0] + folded(q), sums[1] + folded(q * normed)


def emit_sums(out_ref, sums):
    emit(out_ref, column(sums[0]), column(sums[1]))


def back_terms(every_ref, total):
    sums = jnp.sum(every_ref[...], axis=0)
    return sums, sums[0:1] / total, sums[1:2] / total


VMEM = pl.BlockSpec(memory_space=pltpu.VMEM)
SMEM = pl.BlockSpec(memory_space=pltpu.SMEM)
ANY = pl.BlockSpec(memory_space=pl.ANY)
HBM = pl.BlockSpec(memory_space=pltpu.HBM)


class Order:
    last = ()


def run(body, outs, ins, name, scratch=(), limit=8, scalars=0):
    vectors = len(ins) - scalars
    waits = len(Order.last)

    def ordered(*refs):
        body(*refs[:vectors], *refs[vectors + waits :])

    result = pl.pallas_call(
        ordered,
        out_shape=outs,
        in_specs=[HBM if item is None else VMEM for item in _spaces(ins[:vectors])] + [ANY] * waits + [SMEM] * scalars,
        out_specs=[VMEM] * len(outs),
        scratch_shapes=list(scratch),
        cost_estimate=pl.CostEstimate(flops=1, bytes_accessed=1, transcendentals=0),
        compiler_params=pltpu.CompilerParams(vmem_limit_bytes=limit * 1024 * 1024),
        name=name,
    )(*[item.array if isinstance(item, InPlace) else item for item in ins[:vectors]], *Order.last, *ins[vectors:])
    Order.last = (result[0],)
    return result


class InPlace:
    def __init__(self, array):
        self.array = array


def _spaces(items):
    return [None if isinstance(item, InPlace) else item for item in items]


def shape(dims, kind=f32):
    return jax.ShapeDtypeStruct(tuple(dims), kind)


def reduce_first(x, reduce_kernel, width):
    cells = x.shape[0]
    half = reduce_kernel.shape[1]

    def body(x_ref, r_ref, reduced_ref, stats_ref):
        reduced_ref[...] = dot(x_ref[...], r_ref[...])
        emit_moments(stats_ref, reduced_ref, float(cells))

    return run(body, [shape((cells, half)), shape((width, 2, half))], (x, reduce_kernel), "reduce_first")


def reduce_next(both, every, gain, bias, s, reduce_kernel, narrow):
    cells, channels = both.shape
    half = reduce_kernel.shape[1]
    width = every.shape[0]

    def body(both_ref, every_ref, g_ref, b_ref, r_ref, low_ref, reduced_ref, stats_ref, mi_ref):
        mean, inv = moments(every_ref[...], float(cells), float(cells * width))
        mi_ref[...] = jnp.concatenate([mean, inv], axis=0)
        gain_row, bias_row = g_ref[s : s + 1], b_ref[s : s + 1]

        def apply(at, carry):
            low_ref[at, :] = gelu((both_ref[at, :] - mean) * inv * gain_row + bias_row).astype(bf16)
            return carry

        sweep(cells, apply, step=32)
        reduced_ref[...] = dot(low_ref[:, narrow:], r_ref[...])
        emit_moments(stats_ref, reduced_ref, float(cells))

    outs = [shape((cells, channels), bf16), shape((cells, half)), shape((width, 2, half)), shape((2, channels))]
    return run(body, outs, (both, every, gain, bias, reduce_kernel), "reduce_next")


def hidden_act(reduced, every, gain, bias, s):
    cells, channels = reduced.shape
    width = every.shape[0]

    def body(v_ref, every_ref, g_ref, b_ref, low_ref, hidden_ref, mi_ref):
        mean, inv = moments(every_ref[...], float(cells), float(cells * width))
        mi_ref[...] = jnp.concatenate([mean, inv], axis=0)
        gain_row, bias_row = g_ref[s : s + 1], b_ref[s : s + 1]

        def apply(at, carry):
            act = gelu((v_ref[at, :] - mean) * inv * gain_row + bias_row)
            hidden_ref[at, :] = act
            low_ref[at, :] = act.astype(bf16)
            return carry

        sweep(cells, apply)

    outs = [shape((cells, channels), bf16), shape((cells, channels)), shape((2, channels))]
    return run(body, outs, (reduced, every, gain, bias), "hidden_act")


def freq_act(mixed, every, gain, bias, s, factor, place, counts, e_n, z_n):
    points, channels = mixed.shape
    width = every.shape[0]

    def body(v_ref, every_ref, g_ref, b_ref, factor_ref, place_ref, low_ref, mi_ref):
        by_device = device_counts(counts, place_ref[0], width, e_n, z_n)
        mean, inv = moments(every_ref[...], by_device, jnp.sum(by_device))
        mi_ref[...] = jnp.concatenate([mean, inv], axis=0)
        gain_row, bias_row = g_ref[s : s + 1], b_ref[s : s + 1]

        def apply(at, carry):
            act = gelu((v_ref[at, :] - mean) * inv * gain_row + bias_row)
            low_ref[at, :] = (act * factor_ref[at, :]).astype(bf16)
            return carry

        sweep(points, apply)

    outs = [shape((points, channels), bf16), shape((2, channels))]
    return run(body, outs, (mixed, every, gain, bias, factor, place), "freq_act", scalars=1)


def blocks_of(rows, most):
    count = -(-rows // most)
    while rows % (16 * count):
        count += 1
    return [slice(i * rows // count, (i + 1) * rows // count) for i in range(count)]


def spectrum_forward(table, own, others, freq_kernel, factor, scale, width):
    points = table.shape[1]
    cells, half = own.shape
    wide = freq_kernel.shape[1]

    def body(t_ref, own_ref, others_ref, w_ref, factor_ref, real_ref, imag_ref, mixed_ref, stats_ref):
        for side, out_ref in enumerate((real_ref, imag_ref)):
            for at in blocks_of(points, 272):
                z = dot(t_ref[side, at, :cells], own_ref[...]) + dot(t_ref[side, at, cells:], others_ref[...])
                out_ref[at, :] = (z * scale).astype(bf16)
        mixed_ref[...] = dot(real_ref[...], w_ref[:half]) + dot(imag_ref[...], w_ref[half:])
        count = jnp.sum(jnp.where(factor_ref[...] > 0.0, 1.0, 0.0))
        emit_moments(stats_ref, mixed_ref, count, factor_ref)

    outs = [shape((points, half), bf16), shape((points, half), bf16), shape((points, wide)), shape((width, 2, wide))]
    return run(body, outs, (table, own, others, freq_kernel, factor), "spectrum_forward")


def inverse_forward(table, own, others, hidden, pre, expand_t, scale, width):
    cells = table.shape[1]
    half = hidden.shape[1]
    channels = pre.shape[1]
    narrow = channels - expand_t.shape[0]

    def body(t_ref, own_ref, others_ref, hidden_ref, pre_ref, e_ref, summed_ref, both_ref, stats_ref):
        freq = jnp.concatenate([own_ref[...], others_ref[...]], axis=0)
        real, imag = freq[:, :half], freq[:, half:]
        for at in blocks_of(cells, 256):
            returned = dot(t_ref[0, at, :], real) + dot(t_ref[1, at, :], imag)
            summed_ref[at, :] = (hidden_ref[at, :] + returned * scale).astype(bf16)
        both_ref[:, :narrow] = pre_ref[:, :narrow]
        for at in blocks_of(cells, 256):
            both_ref[at, narrow:] = pre_ref[at, narrow:] + dot_t(summed_ref[at, :], e_ref[...])
        emit_moments(stats_ref, both_ref, float(cells))

    outs = [shape((cells, half), bf16), shape((cells, channels)), shape((width, 2, channels))]
    return run(body, outs, (table, own, others, hidden, pre, expand_t), "inverse_forward")


def turn(both, every, gain, bias, s, x, cot):
    cells, channels = both.shape

    width = every.shape[0]

    def body(both_ref, every_ref, g_ref, b_ref, x_ref, cot_ref, out_ref, q_ref, sums_ref, mi_ref):
        mean, inv = moments(every_ref[...], float(cells), float(cells * width))
        mi_ref[...] = jnp.concatenate([mean, inv], axis=0)
        gain_row, bias_row = g_ref[s : s + 1], b_ref[s : s + 1]

        def apply(at, sums):
            normed = (both_ref[at, :] - mean) * inv
            state, slope = gelu_parts(normed * gain_row + bias_row)
            out_ref[at, :] = (x_ref[at, :].astype(f32) + state).astype(bf16)
            q = slope * cot_ref[at, :].astype(f32)
            q_ref[at, :] = q
            return add_sums(sums, q, normed)

        emit_sums(sums_ref, sweep(cells, apply, pair(channels), step=32))

    outs = [shape((cells, channels), bf16), shape((cells, channels)), shape((width, 2, channels)), shape((2, channels))]
    return run(body, outs, (both, every, gain, bias, x, cot), "turn")


def grad_pre(q, both, mi, every, gain, s, expand_t, total):
    cells, channels = both.shape
    broad, half = expand_t.shape
    narrow = channels - broad

    def body(q_ref, both_ref, mi_ref, every_ref, g_ref, e_ref, *refs):
        low_ref, summed_ref, summed_low_ref, sums_ref = refs
        sums, bias_term, gain_term = back_terms(every_ref, total)
        sums_ref[...] = sums
        mean, inv = mi_ref[0:1], mi_ref[1:2]
        gain_row = g_ref[s : s + 1] * inv

        def apply(at, carry):
            normed = (both_ref[at, :] - mean) * inv
            low_ref[at, :] = (gain_row * (q_ref[at, :] - bias_term - normed * gain_term)).astype(bf16)
            return carry

        sweep(cells, apply, step=32)
        summed_ref[...] = dot(low_ref[:, narrow:], e_ref[...])
        summed_low_ref[...] = summed_ref[...].astype(bf16)

    outs = [shape((cells, channels), bf16), shape((cells, half)), shape((cells, half), bf16), shape((2, channels))]
    return run(body, outs, (q, both, mi, every, gain, expand_t), "grad_pre")


def spectrum_backward(table, own, others, mixed, mi, gain, bias, s, factor, scale, width):
    points, wide = mixed.shape
    cells, half = own.shape

    def body(t_ref, own_ref, others_ref, mixed_ref, mi_ref, g_ref, b_ref, factor_ref, *refs):
        q_ref, sums_ref, n_ref = refs
        mean, inv = mi_ref[0:1], mi_ref[1:2]
        gain_row, bias_row = g_ref[s : s + 1], b_ref[s : s + 1]
        for side in range(2):
            for at in blocks_of(points, 272):
                z = dot(t_ref[side, at, :cells], own_ref[...]) + dot(t_ref[side, at, cells:], others_ref[...])
                q_ref[at, side * half : (side + 1) * half] = z * (factor_ref[at, :] * scale)

        def apply(at, sums):
            normed = (mixed_ref[at, :] - mean) * inv
            q = gelu_parts(normed * gain_row + bias_row)[1] * q_ref[at, :]
            q_ref[at, :] = q
            n_ref[at, :] = normed
            return add_sums(sums, q, normed)

        emit_sums(sums_ref, sweep(points, apply, pair(wide)))

    outs = [shape((points, wide)), shape((width, 2, wide)), shape((points, wide))]
    return run(body, outs, (table, own, others, mixed, mi, gain, bias, factor), "spectrum_backward")


def norm_low(low_ref, q_ref, n_ref, mi_ref, gain_row, bias_term, gain_term):
    gain_row = gain_row * mi_ref[1:2]

    def apply(at, carry):
        low_ref[at, :] = (gain_row * (q_ref[at, :] - bias_term - n_ref[at, :] * gain_term)).astype(bf16)
        return carry

    sweep(q_ref.shape[0], apply)


def grad_mixed(q, normed, mi, every, gain, s, freq_kernel, place, totals):
    points, wide = q.shape

    def body(q_ref, n_ref, mi_ref, every_ref, g_ref, w_ref, place_ref, low_ref, back_ref, sums_ref):
        total = jnp.where(place_ref[0] == 0, float(totals[0]), float(totals[1]))
        sums, bias_term, gain_term = back_terms(every_ref, total)
        sums_ref[...] = sums
        norm_low(low_ref, q_ref, n_ref, mi_ref, g_ref[s : s + 1], bias_term, gain_term)
        back_ref[...] = dot_t(low_ref[...], w_ref[...]).astype(bf16)

    outs = [shape((points, wide), bf16), shape((points, wide), bf16), shape((2, wide))]
    return run(body, outs, (q, normed, mi, every, gain, freq_kernel, place), "grad_mixed", scalars=1)


def inverse_backward(table, own, others, summed, reduced, mi, gain, bias, s, scale, width):
    cells = table.shape[1]
    half = summed.shape[1]

    def body(t_ref, own_ref, others_ref, summed_ref, reduced_ref, mi_ref, g_ref, b_ref, *refs):
        q_ref, sums_ref, n_ref = refs
        mean, inv = mi_ref[0:1], mi_ref[1:2]
        gain_row, bias_row = g_ref[s : s + 1], b_ref[s : s + 1]
        freq = jnp.concatenate([own_ref[...], others_ref[...]], axis=0)
        real, imag = freq[:, :half], freq[:, half:]
        for at in blocks_of(cells, 256):
            back = dot(t_ref[0, at, :], real) + dot(t_ref[1, at, :], imag)
            q_ref[at, :] = summed_ref[at, :] + back * scale

        def apply(at, sums):
            normed = (reduced_ref[at, :] - mean) * inv
            q = gelu_parts(normed * gain_row + bias_row)[1] * q_ref[at, :]
            q_ref[at, :] = q
            n_ref[at, :] = normed
            return add_sums(sums, q, normed)

        emit_sums(sums_ref, sweep(cells, apply, pair(half)))

    outs = [shape((cells, half)), shape((width, 2, half)), shape((cells, half))]
    return run(body, outs, (table, own, others, summed, reduced, mi, gain, bias), "inverse_backward")


def grad_reduced(q, normed, mi, every, gain, s, reduce_kernel, total, conv_back, both, mi_3, gain_3, bias_3, width):
    cells, half = q.shape
    channels = both.shape[1]
    narrow = channels - reduce_kernel.shape[0]

    def body(q_ref, n_ref, mi_ref, every_ref, g_ref, r_ref, conv_ref, both_ref, mi3_ref, g3_ref, b3_ref, *refs):
        low_ref, out_ref, sums3_ref, sums_ref = refs
        sums, bias_term, gain_term = back_terms(every_ref, total)
        sums_ref[...] = sums
        norm_low(low_ref, q_ref, n_ref, mi_ref, g_ref[s : s + 1], bias_term, gain_term)
        out_ref[:, :narrow] = conv_ref[:, :narrow]
        for at in blocks_of(cells, 256):
            out_ref[at, narrow:] = conv_ref[at, narrow:] + dot_t(low_ref[at, :], r_ref[...])
        mean, inv = mi3_ref[0:1], mi3_ref[1:2]
        gain_row, bias_row = g3_ref[s - 1 : s], b3_ref[s - 1 : s]

        def apply(at, sums):
            normed_3 = (both_ref[at, :] - mean) * inv
            grad = gelu_parts(normed_3 * gain_row + bias_row)[1] * out_ref[at, :]
            out_ref[at, :] = grad
            return add_sums(sums, grad, normed_3)

        emit_sums(sums3_ref, sweep(cells, apply, pair(channels), step=32))

    outs = [shape((cells, half), bf16), shape((cells, channels)), shape((width, 2, channels)), shape((2, half))]
    ins = (q, normed, mi, every, gain, reduce_kernel, conv_back, both, mi_3, gain_3, bias_3)
    return run(body, outs, ins, "grad_reduced")


def grad_last(q, normed, mi, every, gain, s, total):
    cells, half = q.shape

    def body(q_ref, n_ref, mi_ref, every_ref, g_ref, *refs):
        low_ref, sums_ref = refs
        sums, bias_term, gain_term = back_terms(every_ref, total)
        sums_ref[...] = sums
        norm_low(low_ref, q_ref, n_ref, mi_ref, g_ref[s : s + 1], bias_term, gain_term)

    outs = [shape((cells, half), bf16), shape((2, half))]
    return run(body, outs, (q, normed, mi, every, gain), "grad_last")


def input_grad(cots, conv, late, reduce_kernel, place):
    channels = cots[0].shape[3]
    narrow = channels - reduce_kernel.shape[0]

    def body(cot0_ref, cot1_ref, *refs):
        conv_refs, late_refs, (r_ref, place_ref), out_refs = refs[:4], refs[4:6], refs[6:8], refs[8:]
        c = place_ref[1]
        for kind, (cot_ref, out_ref) in enumerate(zip((cot0_ref, cot1_ref), out_refs)):
            _, rows, cols, _ = cot_ref.shape
            half = cols // 2
            for side, core in enumerate((c, 1 - c)):
                at = pl.ds(pl.multiple_of(core * half, half), half)
                into = dot_t(late_refs[side][kind], r_ref[...]).reshape(rows, half, channels - narrow)
                base = jnp.concatenate([conv_refs[side][kind], conv_refs[2 + side][kind]], axis=1)
                base = base.astype(f32).reshape(rows, half, channels) + cot_ref[0, :, at, :].astype(f32)
                out_ref[0, :, at, :narrow] = base[..., :narrow].astype(bf16)
                out_ref[0, :, at, narrow:] = (base[..., narrow:] + into).astype(bf16)

    outs = [shape(cot.shape, bf16) for cot in cots]
    ins = (*cots, *conv[0], *conv[1], *late, reduce_kernel, place)
    return run(body, outs, ins, "input_grad", limit=12, scalars=1)


def edge_cells(low, above, place, unit):
    cells, channels = low.shape
    blocks = cells // unit + 4

    def body(*refs):
        x_ref, place_ref, out_ref = refs[0], refs[-2], refs[-1]
        if above is None:
            zeros = jnp.zeros((2, channels), f32)
            ends = x_ref[...].astype(f32).reshape(blocks - 4, unit, channels)
            first = jnp.concatenate([zeros, ends[:, 0], zeros], axis=0)
            last = jnp.concatenate([zeros, ends[:, unit - 1], zeros], axis=0)
        else:
            wide = jnp.concatenate([refs[1][...], x_ref[...], refs[2][...]], axis=0)
            ends = wide.astype(f32).reshape(blocks, unit, channels)
            first, last = ends[:, 0], ends[:, unit - 1]
        land, left = place_ref[0] == 0, place_ref[1] == 0
        last = jnp.where(land, jnp.concatenate([last[1:], last[:1]], axis=0), last)
        first = jnp.where(land, jnp.concatenate([first[-1:], first[:-1]], axis=0), first)
        out_ref[...] = jnp.where(left, last, first).astype(bf16)

    ins = (low, place) if above is None else (low, *above, place)
    return run(body, [shape((blocks, channels), bf16)], ins, "edge_cells", scalars=1)[0]


def surroundings(low, place, unit):
    e_n = lax.axis_size("e")
    above = None
    if e_n > 1:
        ahead = [(e, e + 1) for e in range(e_n - 1)]
        above = (
            lax.ppermute(low[-2 * unit :], "e", ahead),
            lax.ppermute(low[: 2 * unit], "e", [(b, a) for a, b in ahead]),
        )
    beside = lax.ppermute(edge_cells(low, above, place, unit), "c", SWAP)
    return above, beside


def shifted_columns(x_ref, above_refs, beside_ref, land, left, out_ref, unit):
    cells, channels = x_ref.shape
    blocks = cells // unit + 4
    block = lax.broadcasted_iota(jnp.int32, (blocks, unit, 1), 0)
    cell = lax.broadcasted_iota(jnp.int32, (blocks, unit, 1), 1)
    for lane in range(0, channels, 128):
        at = slice(lane, lane + 128)
        if above_refs:
            top, bottom = above_refs[0][:, at], above_refs[1][:, at]
        else:
            top = bottom = jnp.zeros((2 * unit, 128), bf16)
        wide = jnp.concatenate([top, x_ref[:, at], bottom], axis=0)
        out_ref[1, :, at] = wide
        wide = wide.astype(f32)
        beside = beside_ref[:, at].astype(f32)[:, None, :]
        for j, edge, odd in ((0, 0, 0), (2, unit - 1, 1)):
            moved = pltpu.roll(wide, 1 if j == 0 else blocks * unit - 1, 0).reshape(blocks, unit, 128)
            outer_side = (cell == edge) & (jnp.logical_not(land) | (block % 2 == odd))
            fill = jnp.where(left if j == 2 else jnp.logical_not(left), beside, 0.0)
            out_ref[j, :, at] = jnp.where(outer_side, fill, moved).reshape(blocks * unit, 128).astype(bf16)


def rows_at(i, first, count, land, unit):
    if i == 1:
        return slice(2 * unit + first, 2 * unit + first + count)
    step = jnp.where(land, 2 * unit, unit)
    return pl.ds(pl.multiple_of(2 * unit + first + (i - 1) * step, unit), count)


def conv_forward(low, above, beside, place, unit, local_kernel, global_t):
    cells, channels = low.shape
    narrow = local_kernel.shape[1] // 9
    padded = cells + 4 * unit
    extra = () if above is None else above
    start = 4 + len(extra)

    def body(*refs):
        x_ref, beside_ref, l_ref, g_ref = refs[0], *refs[1 + len(extra) : 4 + len(extra)]
        place_ref, pre_ref, cols_ref, wide_ref = refs[start:]
        land, left = place_ref[0] == 0, place_ref[1] == 0
        shifted_columns(x_ref, refs[1 : 1 + len(extra)], beside_ref, land, left, wide_ref, unit)
        cols_ref[...] = wide_ref[:, :, :narrow]
        for at in blocks_of(cells, 512):
            count = at.stop - at.start
            local = jnp.zeros((count, narrow), f32)
            patches = []
            for t in range(9):
                block = wide_ref[t % 3, rows_at(t // 3, at.start, count, land, unit), :]
                local = local + dot(block, l_ref[:, t * narrow : (t + 1) * narrow])
                patches.append(block[:, :narrow])
            pre_ref[at, :narrow] = local
            pre_ref[at, narrow:] = dot_t(jnp.concatenate(patches, axis=1), g_ref[...])

    outs = [shape((cells, channels)), shape((3, padded, narrow), bf16)]
    ins = (low, *extra, beside, local_kernel, global_t, place)
    return run(body, outs, ins, "conv_forward", [pltpu.VMEM((3, padded, channels), bf16)], 12, 1)


def conv_backward(low, above, beside, place, unit, local_kernel, global_t, kind):
    cells, channels = low.shape
    narrow = local_kernel.shape[1] // 9
    padded = cells + 4 * unit
    extra = () if above is None else above
    start = 4 + len(extra)

    def body(*refs):
        x_ref, beside_ref, l_ref, g_ref = refs[0], *refs[1 + len(extra) : 4 + len(extra)]
        place_ref, grad_ref, patches_ref, wide_ref = refs[start:]
        land, left = place_ref[0] == 0, place_ref[1] == 0
        shifted_columns(x_ref, refs[1 : 1 + len(extra)], beside_ref, land, left, wide_ref, unit)
        for at in blocks_of(cells, 512):
            count = at.stop - at.start
            into = jnp.zeros((count, narrow), f32)
            for t in range(9):
                block = wide_ref[2 - t % 3, rows_at(2 - t // 3, at.start, count, land, unit), :]
                patches_ref[at, t * narrow : (t + 1) * narrow] = block[:, :narrow]
                into = into + dot(block[:, narrow:], g_ref[:, t * narrow : (t + 1) * narrow])
            grad = dot_t(patches_ref[at, :], l_ref[...])
            grad_ref[at, :narrow] = (grad[:, :narrow] + into).astype(kind)
            grad_ref[at, narrow:] = grad[:, narrow:].astype(kind)

    outs = [shape((cells, channels), kind), shape((cells, 9 * narrow), bf16)]
    ins = (low, *extra, beside, local_kernel, global_t, place)
    return run(body, outs, ins, "conv_backward", [pltpu.VMEM((3, padded, channels), bf16)], 12, 1)


def spaced(rows, own, pad):
    row = lax.broadcasted_iota(jnp.int32, (rows, rows // own * pad), 0)
    place = lax.broadcasted_iota(jnp.int32, (rows, rows // own * pad), 1)
    return jnp.where(place == row // own * pad + row % own, 1.0, 0.0).astype(bf16)


def gathered(shard, here):
    pieces = over_line([shard] * lax.axis_size(("k", "z", "e")))
    yield
    block = in_order(pieces, here[0]).reshape((-1,) + shard.shape)
    pieces = over_plane([block] * lax.axis_size("g"))
    others = [lax.ppermute(piece, "c", SWAP) for piece in pieces]
    yield
    return pieces + others


def assemble(full_ref, piece_refs, g, c):
    count = len(piece_refs) // 2
    for step in range(count):
        full_ref[g ^ step, c] = piece_refs[step][...]
        full_ref[g ^ step, 1 - c] = piece_refs[count + step][...]


def unpack_small(pieces, here, own, half):
    count = len(pieces)
    line_n, sections, pad, columns = pieces[0].shape
    devices = line_n * count
    wide = columns - 2 * half

    def body(*refs):
        g_ref, c_ref, *out_refs = refs[count:-1]
        full_ref = refs[-1]
        assemble(full_ref, refs[:count], g_ref[0], c_ref[0])
        place = spaced(devices * own, own, pad)
        for s in range(sections):
            full = dot(place, full_ref[:, :, :, s].reshape(devices * pad, columns)).astype(bf16)
            out_refs[3 * s][...] = full[:, :wide]
            out_refs[3 * s + 1][...] = full[:, wide : wide + half]
            out_refs[3 * s + 2][...] = full[:, wide + half :]

    outs = [shape((devices * own, width), bf16) for width in (wide, half, half)] * sections
    scratch = [pltpu.VMEM((count // 2, 2) + pieces[0].shape, bf16)]
    return run(body, outs, (*pieces, *here[1:]), "unpack_small", scratch, scalars=2)


def unpack_kernels(full, sections, own_in, pad_in, own_out):
    devices, _, rows, columns = full.shape
    pad = rows - pad_in
    plain = own_in == pad_in

    def body(full_ref, *refs):
        out_refs, local_ref, global_ref, sems = refs[: 2 * sections], *refs[2 * sections :]
        copies = []
        for s in range(sections):
            target = out_refs[2 * s] if plain else local_ref.at[s]
            copies.append(pltpu.make_async_copy(full_ref.at[:, s, :pad_in, :], target, sems.at[2 * s]))
            copies.append(pltpu.make_async_copy(full_ref.at[:, s, pad_in:, :], global_ref.at[s], sems.at[2 * s + 1]))
        for copy in copies:
            copy.start()
        for copy in copies:
            copy.wait()
        for s in range(sections):
            if not plain:
                block = local_ref[s].reshape(devices * pad_in, columns)
                out_refs[2 * s][...] = dot(spaced(devices * own_in, own_in, pad_in), block).astype(bf16)
            block = global_ref[s].reshape(devices * pad, columns)
            out_refs[2 * s + 1][...] = dot(spaced(devices * own_out, own_out, pad), block).astype(bf16)

    local = (devices, pad_in, columns) if plain else (devices * own_in, columns)
    outs = [shape(dims, bf16) for dims in (local, (devices * own_out, columns))] * sections
    scratch = [
        pltpu.VMEM((8,) * 4 if plain else (sections, devices, pad_in, columns), bf16),
        pltpu.VMEM((sections, devices, pad, columns), bf16),
        pltpu.SemaphoreType.DMA((2 * sections,)),
    ]
    limit = 12 if plain else 48
    out = run(body, outs, (InPlace(full),), "unpack_kernels", scratch, limit)
    return [(out[2 * s].reshape(devices * own_in, columns), out[2 * s + 1]) for s in range(sections)]


def early_grads(x_low, patches, grad_low, shifted, summed, place, unit, own, pad):
    cells, channels = x_low.shape
    narrow = shifted.shape[2]
    broad = channels - narrow
    half = summed.shape[1]

    def body(x_ref, p_ref, g_ref, s_ref, m_ref, *refs):
        place_ref, local_ref, other_ref = refs
        land = place_ref[0] == 0
        for i in range(3):
            at = slice(3 * i * narrow, 3 * (i + 1) * narrow)
            local_ref[:, at] = outer(x_ref[...], p_ref[:, at]).astype(bf16)
        grad = dot(g_ref[:, narrow:], spaced(broad, own, pad)).astype(bf16)
        for i in range(3):
            taps = [s_ref[j, rows_at(i, 0, cells, land, unit), :] for j in range(3)]
            at = slice(3 * i * narrow, 3 * (i + 1) * narrow)
            other_ref[:, at] = outer(grad, jnp.concatenate(taps, axis=1)).astype(bf16)
        other_ref[:, 9 * narrow :] = outer(grad, m_ref[...]).astype(bf16)

    outs = [shape((channels, 9 * narrow), bf16), shape((broad // own * pad, 9 * narrow + half), bf16)]
    ins = (x_low, patches, grad_low, shifted, summed, place)
    return run(body, outs, ins, "early_grads", limit=12, scalars=1)


def late_grads(x_low, reduced_low, real, imag, mixed_low, own, pad):
    channels = x_low.shape[1]
    wide = mixed_low.shape[1]
    half = reduced_low.shape[1]
    narrow = channels - wide

    def body(x_ref, r_ref, real_ref, imag_ref, m_ref, out_ref):
        freq = jnp.concatenate([outer(real_ref[...], m_ref[...]), outer(imag_ref[...], m_ref[...])], axis=0)
        reduce = outer(x_ref[:, narrow:], r_ref[...])
        place = spaced(wide, own, pad)
        out_ref[:, :wide] = outer(place, freq.astype(bf16)).astype(bf16)
        out_ref[:, wide:] = outer(place, reduce.astype(bf16)).astype(bf16)

    outs = [shape((wide // own * pad, wide + half), bf16)]
    return run(body, outs, (x_low, reduced_low, real, imag, mixed_low), "late_grads")[0]


def core_parts(shares, here, g_n):
    parts = [part.reshape((g_n, 2, -1) + part.shape[1:]) for part in shares]
    rows, widths = parts[0].shape[2], [part.shape[3] for part in parts]
    starts = [sum(widths[:i]) for i in range(len(widths) + 1)]

    def body(*refs):
        c = refs[len(parts)][0]
        theirs_ref, mine_ref = refs[len(parts) + 1 :]
        for i, ref in enumerate(refs[: len(parts)]):
            at = slice(starts[i], starts[i + 1])
            for g in range(g_n):
                theirs_ref[g, :, at] = ref[g, 1 - c]
                mine_ref[g, :, at] = ref[g, c]

    outs = [shape((g_n, rows, starts[-1]), bf16)] * 2
    return run(body, outs, (*parts, here[2]), "core_parts", scalars=1)


def add_parts(mine, theirs, here):
    g_n = mine.shape[0]

    def body(mine_ref, theirs_ref, *refs):
        for step in range(g_n):
            g = refs[0][0] ^ step
            total = mine_ref[g].astype(f32) + theirs_ref[g].astype(f32)
            refs[1 + step][...] = total if step == 0 else total.astype(bf16)

    outs = [shape(mine.shape[1:], f32 if step == 0 else bf16) for step in range(g_n)]
    return run(body, outs, (mine, theirs, here[1]), "add_parts", scalars=1)


def add_plane(pieces, here, line_n):
    rows, columns = pieces[0].shape
    block = rows // line_n

    def body(*refs):
        here_ref, *out_refs = refs[len(pieces) :]
        for step in range(line_n):
            there = here_ref[0] ^ step
            total = None
            for ref in refs[: len(pieces)]:
                part = ref[there].astype(f32)
                total = part if total is None else total + part
            out_refs[step][...] = total if step == 0 else total.astype(bf16)

    ins = [piece.reshape(line_n, block, columns) for piece in pieces]
    outs = [shape((block, columns), f32 if step == 0 else bf16) for step in range(line_n)]
    return run(body, outs, (*ins, here[0]), "add_plane", scalars=1)


def owned(shares, here):
    g_n = lax.axis_size("g")
    line_n = lax.axis_size(("k", "z", "e"))
    theirs, mine = core_parts(shares, here, g_n)
    theirs = lax.ppermute(theirs, "c", SWAP)
    yield
    pieces = over_plane(add_parts(mine, theirs, here))
    yield
    pieces = over_line(add_plane(pieces, here, line_n))
    yield
    return pieces


def owned_groups(grads, here, alike):
    return [owned(grads, here)] if alike else [owned((grad,), here) for grad in grads]


def settle(groups):
    flat = [piece for group in groups for piece in group]

    def body(*refs):
        at = 0
        for group, out_ref in zip(groups, refs[len(flat) :]):
            total = refs[at][...]
            for ref in refs[at + 1 : at + len(group)]:
                total = total + ref[...].astype(f32)
            out_ref[...] = total
            at += len(group)

    return run(body, [shape(group[0].shape) for group in groups], flat, "settle")


def pack_sums(sums):
    widths = [item.shape[1] for item in sums]

    def body(*refs):
        refs[-1][...] = jnp.concatenate([ref[...] for ref in refs[:-1]], axis=1)

    return run(body, [shape((2, sum(widths)))], sums, "pack_sums")[0]


def results(totals, sums, other_sums, own_in, own_out, narrow, half, channels):
    sections = len(totals)
    flat = [item for group in totals for item in group]
    widths = [[item.shape[1] for item in group] for group in totals]

    def body(*refs):
        sums_ref, other_ref, local_ref, global_ref, reduce_ref, freq_ref, expand_ref, *norm_refs = refs[len(flat) :]
        first = 0
        for s in range(sections):
            group = refs[first : first + len(widths[s])]
            first += len(widths[s])

            def columns(start, count, rows):
                for ref, wide in zip(group, widths[s]):
                    if start < wide:
                        return ref[:rows, start : start + count]
                    start -= wide

            for t in range(9):
                local_ref[s, t] = columns(t * narrow, narrow, own_in)
                global_ref[t, :, s, :] = columns((9 + t) * narrow, narrow, own_out)
            expand_ref[:, s, :] = columns(18 * narrow, half, own_out)
            freq_ref[:, s, :] = columns(18 * narrow + half, 2 * half, own_out)
            reduce_ref[:, s, :] = columns(18 * narrow + 3 * half, half, own_out)
        both = sums_ref[...] + other_ref[...]
        at = 0
        for s in range(sections):
            for index, wide in enumerate((half, 2 * half, channels)):
                norm_refs[2 * index][s : s + 1, :] = both[1:2, at : at + wide]
                norm_refs[2 * index + 1][s : s + 1, :] = both[0:1, at : at + wide]
                at += wide

    outs = [
        shape((sections, 9, own_in, narrow)),
        shape((9, own_out, sections, narrow)),
        shape((own_out, sections, half)),
        shape((own_out, sections, 2 * half)),
        shape((own_out, sections, half)),
    ]
    outs += [shape((sections, wide)) for wide in (half, half, 2 * half, 2 * half, channels, channels)]
    out = run(body, outs, (*flat, sums, other_sums), "results")
    return (
        out[0],
        jnp.transpose(out[1], (2, 0, 3, 1)),
        jnp.transpose(out[2], (1, 0, 2)),
        jnp.transpose(out[3], (1, 0, 2)),
        jnp.transpose(out[4], (1, 2, 0)),
        *out[5:],
    )


def pick_tables(tables, variant):
    count = len(tables)

    def body(*refs):
        v = refs[count][0]
        copies = [
            pltpu.make_async_copy(refs[i].at[v], refs[count + 1 + i], refs[-1].at[i]) for i in range(count)
        ]
        for copy in copies:
            copy.start()
        for copy in copies:
            copy.wait()

    outs = [shape(table.shape[1:], table.dtype) for table in tables]
    scratch = [pltpu.SemaphoreType.DMA((count,))]
    return run(body, outs, (*[InPlace(table) for table in tables], variant), "pick_tables", scratch, 44, 1)


def per_device(plan, *args):
    (
        land,
        port,
        to_local,
        to_global,
        reduce_weight,
        freq_weight,
        expand_weight,
        spec_gain,
        spec_bias,
        freq_gain,
        freq_bias,
        out_gain,
        out_bias,
        cot_land,
        cot_port,
    ) = args
    rounds, forward_table, inverse_table, weight_table, point_counts = plan
    sections = to_local.shape[0]
    devices = lax.axis_size(ALL)
    own_in = to_local.shape[2]
    own_out = to_global.shape[3]
    pad = -(-own_out // 16) * 16
    narrow = to_local.shape[3]
    channels = own_in * devices
    half = reduce_weight.shape[2]
    unit = port.shape[2] // 2
    k, c, part = lax.axis_index("k"), lax.axis_index("c"), lax.axis_index(PART)
    line_here = lax.axis_index(("k", "z", "e"))
    place = jnp.stack([k, c, line_here]).astype(jnp.int32)
    here = tuple(index.astype(jnp.int32).reshape(1) for index in (line_here, lax.axis_index("g"), c))
    variant = k * lax.axis_size(PART) + part
    g_n, z_n, e_n = lax.axis_size("g"), lax.axis_size("z"), lax.axis_size("e")
    width = lax.axis_size(KIND)

    pad_in = -(-own_in // 16) * 16
    Order.last = ()

    grow = ((0, 0), (0, pad - own_out), (0, 0))
    taps_local = jnp.transpose(to_local, (0, 2, 1, 3)).reshape(sections, own_in, 9 * narrow)
    taps_local = jnp.pad(taps_local, ((0, 0), (0, pad_in - own_in), (0, 0)))
    taps_global = jnp.pad(jnp.transpose(to_global, (0, 3, 1, 2)).reshape(sections, own_out, 9 * narrow), grow)
    taps = lax.all_gather(jnp.concatenate([taps_local, taps_global], axis=1), ALL)
    x_steps = to_tile(land, port, rounds, place, here, narrow)
    advance(x_steps)
    advance(x_steps)
    packed = jnp.concatenate([freq_weight, reduce_weight, jnp.transpose(expand_weight, (0, 2, 1))], axis=2)
    small_steps = gathered(jnp.pad(packed, grow), here)
    advance(small_steps)
    tables = (jnp.asarray(forward_table), jnp.asarray(inverse_table), jnp.asarray(weight_table)[..., None])
    forward, inverse, factor = pick_tables(tables, variant.reshape(1))
    advance(small_steps)
    small = unpack_small(finish(small_steps), here, own_out, half)
    x_broad = advance(x_steps)

    cells = x_broad.shape[0]
    size = cells * lax.axis_size(PART)
    scale = 1.0 / math.sqrt(size)
    cell_total = float(g_n * z_n * size)
    point_totals = [int(item.sum()) * g_n * z_n for item in point_counts]

    def exchange(stats):
        every = lax.all_to_all(stats, KIND, 0, 0, tiled=True)
        Order.last = (every,)
        return every

    kept = []
    for s in range(sections):
        freq_kernel, reduce_kernel, expand_t = small[3 * s : 3 * s + 3]
        if s == 0:
            reduced, stats = reduce_first(x_broad, reduce_kernel, width)
        else:
            low, reduced, stats, kept[-1]["mi_3"] = reduce_next(both, every, out_gain, out_bias, s - 1, reduce_kernel, narrow)
        every = exchange(stats)
        if s == 0:
            x = low = finish(x_steps)
            cot_steps = to_tile(cot_land, cot_port, rounds, place, here)
            advance(cot_steps)
        above, beside = surroundings(low, place, unit)
        hidden_low, hidden, mi_1 = hidden_act(reduced, every, spec_gain, spec_bias, s)
        others = shared(hidden_low)
        if s > 0:
            pre, shifted = conv_forward(low, above, beside, place, unit, *kernels[s])
        else:
            advance(cot_steps)
        real, imag, mixed, stats = spectrum_forward(forward, hidden_low, others, freq_kernel, factor, scale, width)
        every = exchange(stats)
        freq_low, mi_2 = freq_act(mixed, every, freq_gain, freq_bias, s, factor, place, point_counts, e_n, z_n)
        others = shared(freq_low)
        if s == 0:
            kernels = unpack_kernels(taps, sections, own_in, pad_in, own_out)
            pre, shifted = conv_forward(low, above, beside, place, unit, *kernels[s])
        summed, both, stats = inverse_forward(inverse, freq_low, others, hidden, pre, expand_t, scale, width)
        if s == 0:
            cot = finish(cot_steps)
        every = exchange(stats)
        kept.append(
            dict(low=low, shifted=shifted, reduced=reduced, mi_1=mi_1, real=real, imag=imag, mixed=mixed, mi_2=mi_2, summed=summed, both=both)
        )
    out, q_3, sums, kept[-1]["mi_3"] = turn(both, every, out_gain, out_bias, sections - 1, x, cot)

    totals = [None] * sections
    norm_sums = [None] * sections
    out_steps = None
    grads = ()
    for s in reversed(range(sections)):
        freq_kernel, reduce_kernel, expand_t = small[3 * s : 3 * s + 3]
        item = kept[s]
        above_steps = []
        every = exchange(sums)
        low, summed, summed_low, sums_3 = grad_pre(
            q_3, item["both"], item["mi_3"], every, out_gain, s, expand_t, cell_total
        )
        others = shared(summed_low)
        if out_steps is None:
            out_steps = from_tile(out, rounds, place, here)
            advance(out_steps)
        above, beside = surroundings(low, place, unit)
        if s + 1 < sections:
            last = kept[s + 1]
            late_grad = late_grads(last["low"], reduced_low, last["real"], last["imag"], mixed_low, own_out, pad)
            above_steps = owned_groups((*grads, late_grad), here, own_in == pad)
            for steps in above_steps:
                advance(steps)

        def convolve():
            back, patches = conv_backward(low, above, beside, place, unit, *kernels[s], f32 if s > 0 else bf16)
            return back, early_grads(item["low"], patches, low, item["shifted"], item["summed"], place, unit, own_out, pad)

        if s == 0:
            conv_back, grads = convolve()
            conv_steps = [from_tile(conv_back, rounds, place, here, lanes) for lanes in (slice(0, channels // 2), slice(channels // 2, channels))]
            for steps in conv_steps:
                advance(steps)
            early_steps = owned_groups(grads, here, own_in == pad)
            for steps in early_steps + above_steps:
                advance(steps)
        q, sums, normed = spectrum_backward(
            forward, summed_low, others, item["mixed"], item["mi_2"], freq_gain, freq_bias, s, factor, scale, width
        )
        every = exchange(sums)
        mixed_low, back, sums_2 = grad_mixed(
            q, normed, item["mi_2"], every, freq_gain, s, freq_kernel, place, point_totals
        )
        others = shared(back)
        if s > 0:
            conv_back, grads = convolve()
            if s == sections - 1:
                out_parts = finish(out_steps)
        else:
            for steps in above_steps:
                advance(steps)
            conv_parts = [finish(conv_steps[0])]
            for steps in early_steps:
                advance(steps)
        q, sums, normed = inverse_backward(
            inverse, back, others, summed, item["reduced"], item["mi_1"], spec_gain, spec_bias, s, scale, width
        )
        every = exchange(sums)
        if s > 0:
            if s == sections - 1:
                land_out, port_out = join_halves(*out_parts, (land, port), place)
            below = kept[s - 1]
            reduced_low, q_3, sums, sums_1 = grad_reduced(
                q, normed, item["mi_1"], every, spec_gain, s, reduce_kernel, cell_total,
                conv_back, below["both"], below["mi_3"], out_gain, out_bias, width,
            )
        else:
            reduced_low, sums_1 = grad_last(q, normed, item["mi_1"], every, spec_gain, s, cell_total)
        norm_sums[s] = (sums_1, sums_2, sums_3)
        if above_steps:
            totals[s + 1] = above_steps

    end_steps = from_tile(reduced_low, rounds, place, here)
    advance(end_steps)
    late_grad = late_grads(kept[0]["low"], reduced_low, kept[0]["real"], kept[0]["imag"], mixed_low, own_out, pad)
    late_steps = owned((late_grad,), here)
    advance(late_steps)
    packed_sums = pack_sums([item for s in range(sections) for item in norm_sums[s]])
    other_sums = lax.ppermute(packed_sums, "k", SWAP)
    for steps in early_steps:
        advance(steps)
    advance(late_steps)
    conv_parts.append(finish(conv_steps[1]))
    end_parts = finish(end_steps)
    advance(late_steps)
    land_grad, port_grad = input_grad((cot_land, cot_port), conv_parts, end_parts, small[1], place)
    for s in range(1, sections):
        totals[s] = settle([finish(steps) for steps in totals[s]])
    totals[0] = settle([finish(steps) for steps in early_steps] + [finish(late_steps)])
    rest = results(totals, packed_sums, other_sums, own_in, own_out, narrow, half, channels)
    return (land_out, port_out, land_grad, port_grad, *rest)


def solution(mesh):
    f_n, s_n = mesh.shape["fsdp"], mesh.shape["sp"]
    e_n = s_n // 4
    fine = Mesh(np.asarray(mesh.devices).reshape(f_n // 2, 2, 2, 2, e_n), ALL)
    maps = P(("g", "c"), ("k", "z", "e"), None, None)
    split = ALL

    def whole(*args):
        land, port = args[0], args[1]
        plan = (
            routes(e_n),
            *transform_tables(e_n, land.shape[1:3], port.shape[1:3]),
        )
        weights = (
            P(None, None, split, None),
            P(None, None, None, split),
            P(None, split, None),
            P(None, split, None),
            P(None, None, split),
        )
        return jax.shard_map(
            lambda *local: per_device(plan, *local),
            mesh=fine,
            in_specs=(maps, maps, *weights, P(), P(), P(), P(), P(), P(), maps, maps),
            out_specs=(maps, maps, maps, maps, *weights, P(), P(), P(), P(), P(), P()),
            check_vma=False,
        )(*args)

    return whole
```

time: 812 us -> 444 us (0.55)
  matrix products: 124 us -> 0 us
  Pallas kernels: 0 us -> 115 us
  local copies, waits for them, and re-layouts: 162 us -> 52.9 us
  other arithmetic: 84.3 us -> 0.84 us
  blocking collectives: 153 us -> 70.6 us
  starting transfers between devices: 135 us -> 95.3 us
  between operations: 49.4 us -> 16.2 us
    all_gather x2 -> x0, blocking collectives: 153 us -> none  [gather_rows(): return lax.all_gather(shard, ALL, tiled=True)]
    dot_general x50 -> x0, matrix products: 124 us -> none  [the longest x30 82.3 us: dot(): lax.dot_general(a, b, (((1,), (0,)), ((), ())), preferred_element_type=f32)]
    pallas_call x0 -> x68, Pallas kernels: none -> 115 us  [run(): pl.pallas_call(ordered, out_shape=outs, in_specs=[HBM if item is None els...]
    all_to_all x20 -> x4, waiting for transfers between devices: 91.7 us -> 16.2 us  [exchange(): every = lax.all_to_all(stats, KIND, 0, 0, tiled=True)]
    all_to_all x0 -> x8, blocking collectives: none -> 70.6 us  [exchange(): every = lax.all_to_all(stats, KIND, 0, 0, tiled=True)]
    ppermute x29 -> x71, waiting for transfers between devices: 2.33 us -> 70.5 us  [the longest x45 63.6 us: partners(): return lax.ppermute(pieces, axes, [(i, i ^ step) for i in range(count)])]
    all_to_all x20 -> x4, starting transfers between devices: 76.2 us -> 25.2 us  [exchange(): every = lax.all_to_all(stats, KIND, 0, 0, tiled=True)]
    slice x64 -> x0, local copies, waits for them, and re-layouts: 31.2 us -> none  [the longest x33 18.7 us: unfold(): padded[t // 3:t // 3 + rows, t % 3:t % 3 + cols]]
  transfers between devices with their start and end apart: 51 -> 76, of which waited for: 16 -> 21; matrix products, arithmetic and copies ran while one was open for 34% -> 1% of each run, Pallas kernels for 0% -> 20%
where the time goes in v3:
time: 444 us; the launch traced here: 437 us
  Pallas kernels  115 us (26%)
  starting transfers between devices  95.3 us (21%)
  waiting for transfers between devices  86.7 us (20%)
  blocking collectives  70.6 us (16%)
  local copies, waits for them, and re-layouts  52.9 us (12%)
  between operations  16.2 us (4%)
    pallas_call x68, Pallas kernels, run(): pl.pallas_call(ordered, out_shape=outs, in_specs=[HBM if item is None els...  115 us
    all_to_all x8, blocking collectives, exchange(): every = lax.all_to_all(stats, KIND, 0, 0, tiled=True)  70.6 us
    ppermute x45, waiting for transfers between devices, partners(): return lax.ppermute(pieces, axes, [(i, i ^ step) for i in range(count)])  63.6 us
    ppermute x45, starting transfers between devices, partners(): return lax.ppermute(pieces, axes, [(i, i ^ step) for i in range(count)])  62.4 us
    unnamed x305, local copies, waits for them, and re-layouts  52 us
    all_to_all x4, starting transfers between devices, exchange(): every = lax.all_to_all(stats, KIND, 0, 0, tiled=True)  25.2 us
    all_to_all x4, waiting for transfers between devices, exchange(): every = lax.all_to_all(stats, KIND, 0, 0, tiled=True)  16.2 us
  transfers between devices with their start and end apart: 76, of which 21 were waited for; matrix products, arithmetic and copies ran while one was open for 1% of the time, Pallas kernels for 20%

profile of v3, /device:TPU:0, one launch (start us, length us, event | category | flops | bytes accessed | tf_op | source)
XLA Modules:
  0.0 437.2 jit_solution(14701785099639563864)
XLA Ops:
  14.5 2.6 collective-permute-start.4
  17.1 2.6 collective-permute-start.5
  22.4 6.0 %pick_tables.1 = (bf16[2,544,2048]{2,1,0:T(8,128)(2,1)S(1)}, bf16[2,1024,1088]{2,1,0:T(8,128)(2,1)}, f32[544,1]{1,0:T(8,128)S(1)}) custom-call(bf16[4,2,544,2048]{3,2,1,0:T(8,128)(2,1)} %constant.27.clone.refs_0_, bf16[4,2,1024,1088]{3,2,1,0:T(8,128)(2,1)} %constant.28.clone.refs_1_, f32[4,544,1]{2,1,0:T(8,128)S(1)} %copy-done.42, ...), custom_call_target="tpu_custom_call" | custom-call | flops 1 | bytes 1 | tf_op jit(solution)/shard_map/pick_tables/pallas_call | solution.py:415
  28.5 2.0 copy-done.2
  35.0 3.3 collective-permute-done.7.refs_1_
  38.3 5.6 %collective-permute-done.8.refs_2_ = bf16[4,2,16,768]{3,2,1,0:T(8,128)(2,1)S(1)} collective-permute-done((bf16[4,2,16,768]{3,2,1,0:T(8,128)(2,1)S(1)}, bf16[4,2,16,768]{3,2,1,0:T(8,128)(2,1)S(1)}, u32[]{:S(2)}, u32[]{:S(2)}) %collective-permute-start.8) | collective-permute-done | bytes 196640 | tf_op jit(solution)/shard_map/ppermute | solution.py:105
  46.8 1.8 collective-permute-start.3
  49.2 1.9 collective-permute-start.15
  51.2 1.8 collective-permute-start.16
  55.3 12.2 %collective-permute-done.2.refs_2_ = bf16[256,384]{1,0:T(8,128)(2,1)S(1)} collective-permute-done((bf16[256,384]{1,0:T(8,128)(2,1)}, bf16[256,384]{1,0:T(8,128)(2,1)S(1)}, u32[]{:S(2)}, u32[]{:S(2)}) %collective-permute-start.2) | collective-permute-done | bytes 196640 | tf_op jit(solution)/shard_map/ppermute | solution.py:105
  74.2 13.7 %all-to-all-start = ((f32[16,2,192]{2,1,0:T(2,128)}), f32[16,2,192]{2,1,0:T(2,128)S(1)}, u32[]{:S(2)}, u32[]{:S(2)}) async-start(f32[16,2,192]{2,1,0:T(2,128)} %get-tuple-element.205), calls=%async_computation | async-start | bytes 65536 | tf_op jit(solution)/shard_map/all_to_all | solution.py:1221
  88.0 5.5 %all-to-all-done.refs_5_.refs_1_ = f32[16,2,192]{2,1,0:T(2,128)S(1)} async-done(((f32[16,2,192]{2,1,0:T(2,128)}), f32[16,2,192]{2,1,0:T(2,128)S(1)}, u32[]{:S(2)}, u32[]{:S(2)}) %all-to-all-start) | async-done | bytes 24608 | tf_op jit(solution)/shard_map/all_to_all | solution.py:1221
  101.5 3.2 spectrum_forward.2
  104.8 8.4 %all_to_all.60.refs_1_.refs_5_ = f32[16,2,384]{2,1,0:T(2,128)S(1)} all-to-all(f32[16,2,384]{2,1,0:T(2,128)S(1)} %get-tuple-element.215), channel_id=1, replica_groups=mesh['g'=4,'c'=2,'k'=2,'z'=2,'e'=1] {'g','c','z','e'}, dimensions={0} | all-to-all | bytes 98304 | tf_op jit(solution)/shard_map/all_to_all | solution.py:1221
  113.1 2.0 freq_act.2
  116.6 2.5 copy-done.14
  120.7 5.3 %conv_forward.2 = (f32[1024,512]{1,0:T(8,128)S(1)}, bf16[3,1088,128]{2,1,0:T(8,128)(2,1)S(1)}) custom-call(bf16[1024,512]{1,0:T(8,128)(2,1)S(1)} %join_lanes.1.refs_2_.refs_0_.refs_4_, bf16[68,512]{1,0:T(8,128)(2,1)S(1)} %collective-permute-done.20.refs_1_, bf16[512,1152]{1,0:T(8,128)(2,1)S(1)} %bitcast.59, ...), custom_call_target="tpu_custom_call" | custom-call | flops 1 | bytes 1 | tf_op jit(solution)/shard_map/conv_forward/pallas_call | solution.py:415
  129.2 3.5 inverse_forward.2
  132.8 8.1 %all_to_all.61.refs_1_.refs_5_ = f32[16,2,512]{2,1,0:T(2,128)S(1)} all-to-all(f32[16,2,512]{2,1,0:T(2,128)S(1)} %get-tuple-element.223), channel_id=1, replica_groups=mesh['g'=4,'c'=2,'k'=2,'z'=2,'e'=1] {'g','c','z','e'}, dimensions={0} | all-to-all | bytes 131072 | tf_op jit(solution)/shard_map/all_to_all | solution.py:1221
  140.9 2.2 reduce_next.1
  144.5 8.5 %all_to_all.62.refs_1_ = f32[16,2,192]{2,1,0:T(2,128)S(1)} all-to-all(f32[16,2,192]{2,1,0:T(2,128)S(1)} %get-tuple-element.226), channel_id=1, replica_groups=mesh['g'=4,'c'=2,'k'=2,'z'=2,'e'=1] {'g','c','z','e'}, dimensions={0} | all-to-all | bytes 49152 | tf_op jit(solution)/shard_map/all_to_all | solution.py:1221
  156.6 5.3 %conv_forward.3 = (f32[1024,512]{1,0:T(8,128)S(1)}, bf16[3,1088,128]{2,1,0:T(8,128)(2,1)S(1)}) custom-call(bf16[1024,512]{1,0:T(8,128)(2,1)S(1)} %get-tuple-element.227.refs_0_, bf16[68,512]{1,0:T(8,128)(2,1)S(1)} %collective-permute-done.22.refs_1_, bf16[512,1152]{1,0:T(8,128)(2,1)S(1)} %bitcast.69, bf16[384,1152]{1,0:T(8,128)(2,1)S(1)} %get-tuple-element.231.refs_3_, ...), custom_call_target="tpu_custom_call" | custom-call | flops 1 | bytes 1 | tf_op jit(solution)/shard_map/conv_forward/pallas_call | solution.py:415
  162.0 3.2 spectrum_forward.3
  165.9 8.1 %all_to_all.63.refs_1_.refs_5_ = f32[16,2,384]{2,1,0:T(2,128)S(1)} all-to-all(f32[16,2,384]{2,1,0:T(2,128)S(1)} %get-tuple-element.234), channel_id=1, replica_groups=mesh['g'=4,'c'=2,'k'=2,'z'=2,'e'=1] {'g','c','z','e'}, dimensions={0} | all-to-all | bytes 98304 | tf_op jit(solution)/shard_map/all_to_all | solution.py:1221
  174.0 2.0 freq_act.3
  177.8 2.7 collective-permute-start.26
  180.6 2.5 inverse_forward.3
  186.0 3.5 all-to-all-start.5
  190.0 8.5 %collective-permute-done.25.refs_2_ = bf16[256,512]{1,0:T(8,128)(2,1)} collective-permute-done((bf16[256,512]{1,0:T(8,128)(2,1)}, bf16[256,512]{1,0:T(8,128)(2,1)}, u32[]{:S(2)}, u32[]{:S(2)}) %collective-permute-start.25) | collective-permute-done | bytes 262176 | tf_op jit(solution)/shard_map/ppermute | solution.py:105
  205.8 2.4 turn.1
  208.2 12.3 %all_to_all.64.refs_3_.refs_6_ = f32[16,2,512]{2,1,0:T(2,128)S(1)} all-to-all(f32[16,2,512]{2,1,0:T(2,128)S(1)} %get-tuple-element.247), channel_id=1, replica_groups=mesh['g'=4,'c'=2,'k'=2,'z'=2,'e'=1] {'g','c','z','e'}, dimensions={0} | all-to-all | bytes 131072 | tf_op jit(solution)/shard_map/all_to_all | solution.py:1221
  225.2 2.1 collective-permute-start.29
  228.2 2.4 spectrum_backward.2
  233.1 3.7 all-to-all-start.7
  237.2 8.0 %all-to-all-done.7.refs_3_.refs_6_ = f32[16,2,384]{2,1,0:T(2,128)S(1)} async-done(((f32[16,2,384]{2,1,0:T(2,128)}), f32[16,2,384]{2,1,0:T(2,128)S(1)}, u32[]{:S(2)}, u32[]{:S(2)}) %all-to-all-start.7) | async-done | bytes 49184 | tf_op jit(solution)/shard_map/all_to_all | solution.py:1221
  253.0 6.0 %conv_backward.2 = (f32[1024,512]{1,0:T(8,128)S(1)}, bf16[1024,1152]{1,0:T(8,128)(2,1)S(1)}) custom-call(bf16[1024,512]{1,0:T(8,128)(2,1)S(1)} %copy-done.7, bf16[68,512]{1,0:T(8,128)(2,1)} %collective-permute-done.30.refs_1_, bf16[512,1152]{1,0:T(8,128)(2,1)S(1)} %bitcast.70, bf16[384,1152]{1,0:T(8,128)(2,1)S(1)} %copy-done.27, ...), custom_call_target="tpu_custom_call" | custom-call | flops 1 | bytes 1 | tf_op jit(solution)/shard_map/conv_backward/pallas_call | solution.py:415
  259.1 5.3 %early_grads.2 = (bf16[512,1152]{1,0:T(8,128)(2,1)S(1)}, bf16[512,1344]{1,0:T(8,128)(2,1)S(1)}) custom-call(bf16[1024,512]{1,0:T(8,128)(2,1)S(1)} %get-tuple-element.227.refs_0_, bf16[1024,1152]{1,0:T(8,128)(2,1)S(1)} %get-tuple-element.259.refs_1_, bf16[1024,512]{1,0:T(8,128)(2,1)S(1)} %copy-done.8, bf16[3,1088,128]{2,1,0:T(8,128)(2,1)S(1)} %copy-done.64, ...), custom_call_target="tpu_custom_call" | custom-call | flops 1 | bytes 1 | tf_op jit(solution)/shard_map/early_grads/pallas_call | solution.py:415
  266.4 2.0 collective-permute-done.33.refs_2_
  268.5 2.8 inverse_backward.2
  271.3 8.9 %all_to_all.65.refs_2_.refs_3_ = f32[16,2,192]{2,1,0:T(2,128)S(1)} all-to-all(f32[16,2,192]{2,1,0:T(2,128)S(1)} %get-tuple-element.269), channel_id=1, replica_groups=mesh['g'=4,'c'=2,'k'=2,'z'=2,'e'=1] {'g','c','z','e'}, dimensions={0} | all-to-all | bytes 49152 | tf_op jit(solution)/shard_map/all_to_all | solution.py:1221
  282.8 2.9 grad_reduced.1
  285.7 8.1 %all_to_all.66.refs_3_.refs_6_ = f32[16,2,512]{2,1,0:T(2,128)S(1)} all-to-all(f32[16,2,512]{2,1,0:T(2,128)S(1)} %get-tuple-element.276), channel_id=1, replica_groups=mesh['g'=4,'c'=2,'k'=2,'z'=2,'e'=1] {'g','c','z','e'}, dimensions={0} | all-to-all | bytes 131072 | tf_op jit(solution)/shard_map/all_to_all | solution.py:1221
  299.1 3.0 collective-permute-done.34.refs_1_
  302.1 5.6 %conv_backward.3 = (bf16[1024,512]{1,0:T(8,128)(2,1)S(1)}, bf16[1024,1152]{1,0:T(8,128)(2,1)S(1)}) custom-call(bf16[1024,512]{1,0:T(8,128)(2,1)S(1)} %get-tuple-element.277.refs_0_.refs_1_.refs_2_, bf16[68,512]{1,0:T(8,128)(2,1)S(1)} %collective-permute-done.34.refs_1_, bf16[512,1152]{1,0:T(8,128)(2,1)S(1)} %bitcast.60, bf16[384,1152]{1,0:T(8,128)(2,1)S(1)} %copy-done.25, ...), custom_call_target="tpu_custom_call" | custom-call | flops 1 | bytes 1 | tf_op jit(solution)/shard_map/conv_backward/pallas_call | solution.py:415
  307.7 5.3 %early_grads.3 = (bf16[512,1152]{1,0:T(8,128)(2,1)S(1)}, bf16[512,1344]{1,0:T(8,128)(2,1)S(1)}) custom-call(bf16[1024,512]{1,0:T(8,128)(2,1)S(1)} %join_lanes.1.refs_2_.refs_0_.refs_4_, bf16[1024,1152]{1,0:T(8,128)(2,1)S(1)} %get-tuple-element.284.refs_1_, bf16[1024,512]{1,0:T(8,128)(2,1)S(1)} %get-tuple-element.277.refs_0_.refs_1_.refs_2_, ...), custom_call_target="tpu_custom_call" | custom-call | flops 1 | bytes 1 | tf_op jit(solution)/shard_map/early_grads/pallas_call | solution.py:415
  320.1 3.3 spectrum_backward.3
  325.3 4.4 all-to-all-start.10
  329.7 2.8 collective-permute-start.41
  332.5 2.7 all-to-all-done.10.refs_3_.refs_6_
  345.7 6.1 %collective-permute-done.36.refs_2_ = bf16[256,256]{1,0:T(8,128)(2,1)S(1)} collective-permute-done((bf16[256,256]{1,0:T(8,128)(2,1)}, bf16[256,256]{1,0:T(8,128)(2,1)S(1)}, u32[]{:S(2)}, u32[]{:S(2)}) %collective-permute-start.36) | collective-permute-done | bytes 131104 | tf_op jit(solution)/shard_map/ppermute | solution.py:105
  355.7 2.3 collective-permute-start.52
  358.0 3.6 collective-permute-start.45
  362.9 2.8 inverse_backward.3
  365.6 8.2 %all_to_all.67.refs_3_.refs_5_ = f32[16,2,192]{2,1,0:T(2,128)S(1)} all-to-all(f32[16,2,192]{2,1,0:T(2,128)S(1)} %get-tuple-element.318), channel_id=1, replica_groups=mesh['g'=4,'c'=2,'k'=2,'z'=2,'e'=1] {'g','c','z','e'}, dimensions={0} | all-to-all | bytes 49152 | tf_op jit(solution)/shard_map/all_to_all | solution.py:1221
  377.1 6.4 %collective-permute-done.46.refs_3_ = bf16[256,256]{1,0:T(8,128)(2,1)S(1)} collective-permute-done((bf16[256,256]{1,0:T(8,128)(2,1)S(1)}, bf16[256,256]{1,0:T(8,128)(2,1)S(1)}, u32[]{:S(2)}, u32[]{:S(2)}) %collective-permute-start.46) | collective-permute-done | bytes 131104 | tf_op jit(solution)/shard_map/ppermute | solution.py:105
  383.5 2.2 collective-permute-start.54
  385.9 2.3 collective-permute-start.56
  391.8 6.9 %collective-permute-done.55.refs_2_ = bf16[256,192]{1,0:T(8,128)(2,1)S(1)} collective-permute-done((bf16[256,192]{1,0:T(8,128)(2,1)S(1)}, bf16[256,192]{1,0:T(8,128)(2,1)S(1)}, u32[]{:S(2)}, u32[]{:S(2)}) %collective-permute-start.55) | collective-permute-done | bytes 98336 | tf_op jit(solution)/shard_map/ppermute | solution.py:105
  400.9 6.9 %collective-permute-done.68.refs_2_ = bf16[16,3072]{1,0:T(8,128)(2,1)S(1)} collective-permute-done((bf16[16,3072]{1,0:T(8,128)(2,1)S(1)}, bf16[16,3072]{1,0:T(8,128)(2,1)S(1)}, u32[]{:S(2)}, u32[]{:S(2)}) %collective-permute-start.68) | collective-permute-done | bytes 98336 | tf_op jit(solution)/shard_map/ppermute | solution.py:105
  413.6 2.0 collective-permute-start.62
  415.6 2.1 collective-permute-start.63
  421.2 2.7 collective-permute-start.66
  424.0 2.0 collective-permute-start.70
  426.0 1.9 input_grad.1
  (482 shorter events, 130.3 us)
Async XLA Ops:
  7.2 109.3 %all-gather.3.cloned.1.call-start = ((), (), s32[]{:S(2)}) async-start(), calls=%async_computation.12 | async-start | bytes 4866048 | tf_op jit(solution)/shard_map/all_gather | solution.py:1201
  11.7 7.9 %collective-permute-start = (bf16[2,256,512]{2,1,0:T(8,128)(2,1)S(1)}, bf16[2,256,512]{2,1,0:T(8,128)(2,1)S(1)}, u32[]{:S(2)}, u32[]{:S(2)}) collective-permute-start(bf16[2,256,512]{2,1,0:T(8,128)(2,1)S(1)} %get-tuple-element.194), channel_id=1, source_target_pairs={{0,4},{4,0},{1,5},{5,1},{2,6},{6,2},{3,7},{7,3},{8,12},{12,8},{9,1... | collective-permute-start | bytes 1572872 | tf_op jit(solution)/shard_map/ppermute | solution.py:243
  14.5 13.9 %collective-permute-start.4 = (bf16[2,16,768]{2,1,0:T(8,128)(2,1)S(1)}, bf16[2,16,768]{2,1,0:T(8,128)(2,1)S(1)}, u32[]{:S(2)}, u32[]{:S(2)}) collective-permute-start(bf16[2,16,768]{2,1,0:T(8,128)(2,1)S(1)} %fusion.6.refs_0_), channel_id=1, source_target_pairs={{0,1},{1,0},{2,3},{3,2},{4,5},{5,4},{6,7},{7,6},{8,9},{9,8},{10,11... | collective-permute-start | bytes 147464 | tf_op jit(solution)/shard_map/ppermute | solution.py:105
  17.1 11.3 %collective-permute-start.5 = (bf16[2,16,768]{2,1,0:T(8,128)(2,1)S(1)}, bf16[2,16,768]{2,1,0:T(8,128)(2,1)S(1)}, u32[]{:S(2)}, u32[]{:S(2)}) collective-permute-start(bf16[2,16,768]{2,1,0:T(8,128)(2,1)S(1)} %fusion.6.refs_0_), channel_id=1, source_target_pairs={{0,2},{1,3},{2,0},{3,1},{4,6},{5,7},{6,4},{7,5},{8,10},{9,11},{10,... | collective-permute-start | bytes 147464 | tf_op jit(solution)/shard_map/ppermute | solution.py:105
  19.7 8.8 %collective-permute-start.6 = (bf16[2,16,768]{2,1,0:T(8,128)(2,1)S(1)}, bf16[2,16,768]{2,1,0:T(8,128)(2,1)S(1)}, u32[]{:S(2)}, u32[]{:S(2)}) collective-permute-start(bf16[2,16,768]{2,1,0:T(8,128)(2,1)S(1)} %fusion.6.refs_0_), channel_id=1, source_target_pairs={{0,3},{1,2},{2,1},{3,0},{4,7},{5,6},{6,5},{7,4},{8,11},{9,10},{10,... | collective-permute-start | bytes 147464 | tf_op jit(solution)/shard_map/ppermute | solution.py:105
  30.5 7.8 %collective-permute-start.7 = (bf16[4,2,16,768]{3,2,1,0:T(8,128)(2,1)S(1)}, bf16[4,2,16,768]{3,2,1,0:T(8,128)(2,1)S(1)}, u32[]{:S(2)}, u32[]{:S(2)}) collective-permute-start(bf16[4,2,16,768]{3,2,1,0:T(8,128)(2,1)S(1)} %in_order.3.refs_0_.refs_8_), channel_id=1, source_target_pairs={{0,8},{8,0},{16,24},{24,16},{1,9},{9,1},{17,25},{25,17},{2,10},{10... | collective-permute-start | bytes 589832 | tf_op jit(solution)/shard_map/ppermute | solution.py:105
  32.2 11.6 %collective-permute-start.8 = (bf16[4,2,16,768]{3,2,1,0:T(8,128)(2,1)S(1)}, bf16[4,2,16,768]{3,2,1,0:T(8,128)(2,1)S(1)}, u32[]{:S(2)}, u32[]{:S(2)}) collective-permute-start(bf16[4,2,16,768]{3,2,1,0:T(8,128)(2,1)S(1)} %in_order.3.refs_0_.refs_8_), channel_id=1, source_target_pairs={{0,16},{8,24},{16,0},{24,8},{1,17},{9,25},{17,1},{25,9},{2,18},{10... | collective-permute-start | bytes 589832 | tf_op jit(solution)/shard_map/ppermute | solution.py:105
  33.7 10.1 %collective-permute-start.9 = (bf16[4,2,16,768]{3,2,1,0:T(8,128)(2,1)S(1)}, bf16[4,2,16,768]{3,2,1,0:T(8,128)(2,1)S(1)}, u32[]{:S(2)}, u32[]{:S(2)}) collective-permute-start(bf16[4,2,16,768]{3,2,1,0:T(8,128)(2,1)S(1)} %in_order.3.refs_0_.refs_8_), channel_id=1, source_target_pairs={{0,24},{8,16},{16,8},{24,0},{1,25},{9,17},{17,9},{25,1},{2,26},{10... | collective-permute-start | bytes 589832 | tf_op jit(solution)/shard_map/ppermute | solution.py:105
  34.0 10.4 %collective-permute-start.1 = (bf16[256,384]{1,0:T(8,128)(2,1)S(1)}, bf16[256,384]{1,0:T(8,128)(2,1)S(1)}, u32[]{:S(2)}, u32[]{:S(2)}) collective-permute-start(bf16[256,384]{1,0:T(8,128)(2,1)S(1)} %get-tuple-element.199), channel_id=1, source_target_pairs={{0,1},{1,0},{2,3},{3,2},{4,5},{5,4},{6,7},{7,6},{8,9},{9,8},{10,11... | collective-permute-start | bytes 589832 | tf_op jit(solution)/shard_map/ppermute | solution.py:105
  35.0 11.8 %collective-permute-start.10 = (bf16[4,2,16,768]{3,2,1,0:T(8,128)(2,1)S(1)}, bf16[4,2,16,768]{3,2,1,0:T(8,128)(2,1)S(1)}, u32[]{:S(2)}, u32[]{:S(2)}) collective-permute-start(bf16[4,2,16,768]{3,2,1,0:T(8,128)(2,1)S(1)} %in_order.3.refs_0_.refs_8_), channel_id=1, source_target_pairs={{0,4},{4,0},{1,5},{5,1},{2,6},{6,2},{3,7},{7,3},{8,12},{12,8},{9,1... | collective-permute-start | bytes 589832 | tf_op jit(solution)/shard_map/ppermute | solution.py:888
  38.3 10.3 %collective-permute-start.11 = (bf16[4,2,16,768]{3,2,1,0:T(8,128)(2,1)S(1)}, bf16[4,2,16,768]{3,2,1,0:T(8,128)(2,1)S(1)}, u32[]{:S(2)}, u32[]{:S(2)}) collective-permute-start(bf16[4,2,16,768]{3,2,1,0:T(8,128)(2,1)S(1)} %collective-permute-done.7.refs_1_), channel_id=1, source_target_pairs={{0,4},{4,0},{1,5},{5,1},{2,6},{6,2},{3,7},{7,3},{8,12},{12,8},{9,1... | collective-permute-start | bytes 589832 | tf_op jit(solution)/shard_map/ppermute | solution.py:888
  43.9 7.3 %collective-permute-start.13 = (bf16[4,2,16,768]{3,2,1,0:T(8,128)(2,1)S(1)}, bf16[4,2,16,768]{3,2,1,0:T(8,128)(2,1)S(1)}, u32[]{:S(2)}, u32[]{:S(2)}) collective-permute-start(bf16[4,2,16,768]{3,2,1,0:T(8,128)(2,1)S(1)} %collective-permute-done.9.refs_3_), channel_id=1, source_target_pairs={{0,4},{4,0},{1,5},{5,1},{2,6},{6,2},{3,7},{7,3},{8,12},{12,8},{9,1... | collective-permute-start | bytes 589832 | tf_op jit(solution)/shard_map/ppermute | solution.py:888
  45.1 22.4 %collective-permute-start.2 = (bf16[256,384]{1,0:T(8,128)(2,1)}, bf16[256,384]{1,0:T(8,128)(2,1)S(1)}, u32[]{:S(2)}, u32[]{:S(2)}) collective-permute-start(bf16[256,384]{1,0:T(8,128)(2,1)} %get-tuple-element.200), channel_id=1, source_target_pairs={{0,2},{1,3},{2,0},{3,1},{4,6},{5,7},{6,4},{7,5},{8,10},{9,11},{10,... | collective-permute-start | bytes 589832 | tf_op jit(solution)/shard_map/ppermute | solution.py:105
  46.8 21.4 %collective-permute-start.3 = (bf16[256,384]{1,0:T(8,128)(2,1)}, bf16[256,384]{1,0:T(8,128)(2,1)S(1)}, u32[]{:S(2)}, u32[]{:S(2)}) collective-permute-start(bf16[256,384]{1,0:T(8,128)(2,1)} %get-tuple-element.201), channel_id=1, source_target_pairs={{0,3},{1,2},{2,1},{3,0},{4,7},{5,6},{6,5},{7,4},{8,11},{9,10},{10,... | collective-permute-start | bytes 589832 | tf_op jit(solution)/shard_map/ppermute | solution.py:105
  48.6 39.3 %collective-permute-start.14 = (bf16[256,128]{1,0:T(8,128)(2,1)}, bf16[256,128]{1,0:T(8,128)(2,1)}, u32[]{:S(2)}, u32[]{:S(2)}) collective-permute-start(bf16[256,128]{1,0:T(8,128)(2,1)} %get-tuple-element.206), channel_id=1, source_target_pairs={{0,1},{1,0},{2,3},{3,2},{4,5},{5,4},{6,7},{7,6},{8,9},{9,8},{10,11... | collective-permute-start | bytes 196616 | tf_op jit(solution)/shard_map/ppermute | solution.py:105
  49.2 38.7 %collective-permute-start.15 = (bf16[256,128]{1,0:T(8,128)(2,1)}, bf16[256,128]{1,0:T(8,128)(2,1)}, u32[]{:S(2)}, u32[]{:S(2)}) collective-permute-start(bf16[256,128]{1,0:T(8,128)(2,1)} %get-tuple-element.207), channel_id=1, source_target_pairs={{0,2},{1,3},{2,0},{3,1},{4,6},{5,7},{6,4},{7,5},{8,10},{9,11},{10,... | collective-permute-start | bytes 196616 | tf_op jit(solution)/shard_map/ppermute | solution.py:105
  51.2 36.8 %collective-permute-start.16 = (bf16[256,128]{1,0:T(8,128)(2,1)}, bf16[256,128]{1,0:T(8,128)(2,1)}, u32[]{:S(2)}, u32[]{:S(2)}) collective-permute-start(bf16[256,128]{1,0:T(8,128)(2,1)} %get-tuple-element.208), channel_id=1, source_target_pairs={{0,3},{1,2},{2,1},{3,0},{4,7},{5,6},{6,5},{7,4},{8,11},{9,10},{10,... | collective-permute-start | bytes 196616 | tf_op jit(solution)/shard_map/ppermute | solution.py:105
  74.2 19.2 %all-to-all-start = ((f32[16,2,192]{2,1,0:T(2,128)}), f32[16,2,192]{2,1,0:T(2,128)S(1)}, u32[]{:S(2)}, u32[]{:S(2)}) async-start(f32[16,2,192]{2,1,0:T(2,128)} %get-tuple-element.205), calls=%async_computation | async-start | bytes 65536 | tf_op jit(solution)/shard_map/all_to_all | solution.py:1221
  116.0 10.9 %collective-permute-start.19 = (bf16[544,384]{1,0:T(8,128)(2,1)S(1)}, bf16[544,384]{1,0:T(8,128)(2,1)}, u32[]{:S(2)}, u32[]{:S(2)}) collective-permute-start(bf16[544,384]{1,0:T(8,128)(2,1)S(1)} %get-tuple-element.216.refs_1_), channel_id=1, source_target_pairs={{4,0},{0,4},{5,1},{1,5},{6,2},{2,6},{7,3},{3,7},{12,8},{8,12},{13,... | collective-permute-start | bytes 1253384 | tf_op jit(solution)/shard_map/ppermute | solution.py:296
  154.5 7.4 %collective-permute-start.21 = (bf16[1024,192]{1,0:T(8,128)(2,1)S(1)}, bf16[1024,192]{1,0:T(8,128)(2,1)S(1)}, u32[]{:S(2)}, u32[]{:S(2)}) collective-permute-start(bf16[1024,192]{1,0:T(8,128)(2,1)S(1)} %get-tuple-element.228.refs_4_.refs_1_), channel_id=1, source_target_pairs={{4,0},{0,4},{5,1},{1,5},{6,2},{2,6},{7,3},{3,7},{12,8},{8,12},{13,... | collective-permute-start | bytes 1179656 | tf_op jit(solution)/shard_map/ppermute | solution.py:296
  176.2 13.8 %collective-permute-start.24 = (bf16[256,512]{1,0:T(8,128)(2,1)}, bf16[256,512]{1,0:T(8,128)(2,1)}, u32[]{:S(2)}, u32[]{:S(2)}) collective-permute-start(bf16[256,512]{1,0:T(8,128)(2,1)} %get-tuple-element.240), channel_id=1, source_target_pairs={{0,1},{1,0},{2,3},{3,2},{4,5},{5,4},{6,7},{7,6},{8,9},{9,8},{10,11... | collective-permute-start | bytes 786440 | tf_op jit(solution)/shard_map/ppermute | solution.py:105
  176.8 21.7 %collective-permute-start.25 = (bf16[256,512]{1,0:T(8,128)(2,1)}, bf16[256,512]{1,0:T(8,128)(2,1)}, u32[]{:S(2)}, u32[]{:S(2)}) collective-permute-start(bf16[256,512]{1,0:T(8,128)(2,1)} %get-tuple-element.241), channel_id=1, source_target_pairs={{0,2},{1,3},{2,0},{3,1},{4,6},{5,7},{6,4},{7,5},{8,10},{9,11},{10,... | collective-permute-start | bytes 786440 | tf_op jit(solution)/shard_map/ppermute | solution.py:105
  177.8 20.6 %collective-permute-start.26 = (bf16[256,512]{1,0:T(8,128)(2,1)}, bf16[256,512]{1,0:T(8,128)(2,1)}, u32[]{:S(2)}, u32[]{:S(2)}) collective-permute-start(bf16[256,512]{1,0:T(8,128)(2,1)} %get-tuple-element.242), channel_id=1, source_target_pairs={{0,3},{1,2},{2,1},{3,0},{4,7},{5,6},{6,5},{7,4},{8,11},{9,10},{10,... | collective-permute-start | bytes 786440 | tf_op jit(solution)/shard_map/ppermute | solution.py:105
  186.0 15.6 %all-to-all-start.5 = ((f32[16,2,512]{2,1,0:T(2,128)}), f32[16,2,512]{2,1,0:T(2,128)S(1)}, u32[]{:S(2)}, u32[]{:S(2)}) async-start(f32[16,2,512]{2,1,0:T(2,128)} %copy-done.108), calls=%async_computation.5 | async-start | bytes 131072 | tf_op jit(solution)/shard_map/all_to_all | solution.py:1221
  221.8 6.3 %collective-permute-start.31 = (bf16[1024,192]{1,0:T(8,128)(2,1)S(1)}, bf16[1024,192]{1,0:T(8,128)(2,1)S(1)}, u32[]{:S(2)}, u32[]{:S(2)}) collective-permute-start(bf16[1024,192]{1,0:T(8,128)(2,1)S(1)} %get-tuple-element.253.refs_1_), channel_id=1, source_target_pairs={{4,0},{0,4},{5,1},{1,5},{6,2},{2,6},{7,3},{3,7},{12,8},{8,12},{13,... | collective-permute-start | bytes 1179656 | tf_op jit(solution)/shard_map/ppermute | solution.py:296
  222.9 41.5 %collective-permute-start.27 = (bf16[256,512]{1,0:T(8,128)(2,1)}, bf16[256,512]{1,0:T(8,128)(2,1)}, u32[]{:S(2)}, u32[]{:S(2)}) collective-permute-start(bf16[256,512]{1,0:T(8,128)(2,1)} %get-tuple-element.250), channel_id=1, source_target_pairs={{0,1},{1,0},{2,3},{3,2},{4,5},{5,4},{6,7},{7,6},{8,9},{9,8},{10,11... | collective-permute-start | bytes 786440 | tf_op jit(solution)/shard_map/ppermute | solution.py:105
  223.5 40.9 %collective-permute-start.28 = (bf16[256,512]{1,0:T(8,128)(2,1)}, bf16[256,512]{1,0:T(8,128)(2,1)}, u32[]{:S(2)}, u32[]{:S(2)}) collective-permute-start(bf16[256,512]{1,0:T(8,128)(2,1)} %get-tuple-element.251), channel_id=1, source_target_pairs={{0,2},{1,3},{2,0},{3,1},{4,6},{5,7},{6,4},{7,5},{8,10},{9,11},{10,... | collective-permute-start | bytes 786440 | tf_op jit(solution)/shard_map/ppermute | solution.py:105
  225.2 39.2 %collective-permute-start.29 = (bf16[256,512]{1,0:T(8,128)(2,1)}, bf16[256,512]{1,0:T(8,128)(2,1)}, u32[]{:S(2)}, u32[]{:S(2)}) collective-permute-start(bf16[256,512]{1,0:T(8,128)(2,1)} %get-tuple-element.252), channel_id=1, source_target_pairs={{0,3},{1,2},{2,1},{3,0},{4,7},{5,6},{6,5},{7,4},{8,11},{9,10},{10,... | collective-permute-start | bytes 786440 | tf_op jit(solution)/shard_map/ppermute | solution.py:105
  233.1 12.1 %all-to-all-start.7 = ((f32[16,2,384]{2,1,0:T(2,128)}), f32[16,2,384]{2,1,0:T(2,128)S(1)}, u32[]{:S(2)}, u32[]{:S(2)}) async-start(f32[16,2,384]{2,1,0:T(2,128)} %copy-done.111), calls=%async_computation.7 | async-start | bytes 98304 | tf_op jit(solution)/shard_map/all_to_all | solution.py:1221
  236.8 12.6 %collective-permute-start.30 = (bf16[68,512]{1,0:T(8,128)(2,1)}, bf16[68,512]{1,0:T(8,128)(2,1)}, u32[]{:S(2)}, u32[]{:S(2)}) collective-permute-start(bf16[68,512]{1,0:T(8,128)(2,1)} %copy-done.86), channel_id=1, source_target_pairs={{0,4},{4,0},{1,5},{5,1},{2,6},{6,2},{3,7},{7,3},{8,12},{12,8},{9,1... | collective-permute-start | bytes 208904 | tf_op jit(solution)/shard_map/ppermute | solution.py:787
  265.8 14.3 %collective-permute-start.32 = (bf16[2,256,512]{2,1,0:T(8,128)(2,1)S(1)}, bf16[2,256,512]{2,1,0:T(8,128)(2,1)S(1)}, u32[]{:S(2)}, u32[]{:S(2)}) collective-permute-start(bf16[2,256,512]{2,1,0:T(8,128)(2,1)S(1)} %get-tuple-element.265), channel_id=1, source_target_pairs={{0,4},{4,0},{1,5},{5,1},{2,6},{6,2},{3,7},{7,3},{8,12},{12,8},{9,1... | collective-permute-start | bytes 1572872 | tf_op jit(solution)/shard_map/ppermute | solution.py:278
  298.5 19.0 %collective-permute-start.38 = (bf16[4,64,3072]{2,1,0:T(8,128)(2,1)S(1)}, bf16[4,64,3072]{2,1,0:T(8,128)(2,1)S(1)}, u32[]{:S(2)}, u32[]{:S(2)}) collective-permute-start(bf16[4,64,3072]{2,1,0:T(8,128)(2,1)S(1)} %get-tuple-element.282.refs_4_), channel_id=1, source_target_pairs={{0,4},{4,0},{1,5},{5,1},{2,6},{6,2},{3,7},{7,3},{8,12},{12,8},{9,1... | collective-permute-start | bytes 4718600 | tf_op jit(solution)/shard_map/ppermute | solution.py:1052
  316.3 36.6 %collective-permute-start.48 = (bf16[4,64,2496]{2,1,0:T(8,128)(2,1)}, bf16[4,64,2496]{2,1,0:T(8,128)(2,1)}, u32[]{:S(2)}, u32[]{:S(2)}) collective-permute-start(bf16[4,64,2496]{2,1,0:T(8,128)(2,1)} %get-tuple-element.294.refs_2_), channel_id=1, source_target_pairs={{0,4},{4,0},{1,5},{5,1},{2,6},{6,2},{3,7},{7,3},{8,12},{12,8},{9,1... | collective-permute-start | bytes 3833864 | tf_op jit(solution)/shard_map/ppermute | solution.py:1052
  316.9 22.0 %collective-permute-start.35 = (bf16[256,256]{1,0:T(8,128)(2,1)}, bf16[256,256]{1,0:T(8,128)(2,1)}, u32[]{:S(2)}, u32[]{:S(2)}) collective-permute-start(bf16[256,256]{1,0:T(8,128)(2,1)} %get-tuple-element.288), channel_id=1, source_target_pairs={{0,1},{1,0},{2,3},{3,2},{4,5},{5,4},{6,7},{7,6},{8,9},{9,8},{10,11... | collective-permute-start | bytes 393224 | tf_op jit(solution)/shard_map/ppermute | solution.py:105
  318.5 20.6 %collective-permute-start.39 = (bf16[64,3072]{1,0:T(8,128)(2,1)}, bf16[64,3072]{1,0:T(8,128)(2,1)}, u32[]{:S(2)}, u32[]{:S(2)}) collective-permute-start(bf16[64,3072]{1,0:T(8,128)(2,1)} %get-tuple-element.296), channel_id=1, source_target_pairs={{0,8},{8,0},{16,24},{24,16},{1,9},{9,1},{17,25},{25,17},{2,10},{10... | collective-permute-start | bytes 1179656 | tf_op jit(solution)/shard_map/ppermute | solution.py:105
  319.3 21.5 %collective-permute-start.40 = (bf16[64,3072]{1,0:T(8,128)(2,1)}, bf16[64,3072]{1,0:T(8,128)(2,1)}, u32[]{:S(2)}, u32[]{:S(2)}) collective-permute-start(bf16[64,3072]{1,0:T(8,128)(2,1)} %get-tuple-element.297), channel_id=1, source_target_pairs={{0,16},{8,24},{16,0},{24,8},{1,17},{9,25},{17,1},{25,9},{2,18},{10... | collective-permute-start | bytes 1179656 | tf_op jit(solution)/shard_map/ppermute | solution.py:105
  325.3 9.9 %all-to-all-start.10 = ((f32[16,2,384]{2,1,0:T(2,128)}), f32[16,2,384]{2,1,0:T(2,128)S(1)}, u32[]{:S(2)}, u32[]{:S(2)}) async-start(f32[16,2,384]{2,1,0:T(2,128)} %get-tuple-element.303), calls=%async_computation.10 | async-start | bytes 98304 | tf_op jit(solution)/shard_map/all_to_all | solution.py:1221
  329.7 13.1 %collective-permute-start.41 = (bf16[64,3072]{1,0:T(8,128)(2,1)}, bf16[64,3072]{1,0:T(8,128)(2,1)}, u32[]{:S(2)}, u32[]{:S(2)}) collective-permute-start(bf16[64,3072]{1,0:T(8,128)(2,1)} %copy-done.131), channel_id=1, source_target_pairs={{0,24},{8,16},{16,8},{24,0},{1,25},{9,17},{17,9},{25,1},{2,26},{10... | collective-permute-start | bytes 1179656 | tf_op jit(solution)/shard_map/ppermute | solution.py:105
  338.9 19.1 %collective-permute-start.47 = (bf16[544,384]{1,0:T(8,128)(2,1)S(1)}, bf16[544,384]{1,0:T(8,128)(2,1)S(1)}, u32[]{:S(2)}, u32[]{:S(2)}) collective-permute-start(bf16[544,384]{1,0:T(8,128)(2,1)S(1)} %get-tuple-element.311.refs_1_), channel_id=1, source_target_pairs={{4,0},{0,4},{5,1},{1,5},{6,2},{2,6},{7,3},{3,7},{12,8},{8,12},{13,... | collective-permute-start | bytes 1253384 | tf_op jit(solution)/shard_map/ppermute | solution.py:296
  339.1 12.7 %collective-permute-start.36 = (bf16[256,256]{1,0:T(8,128)(2,1)}, bf16[256,256]{1,0:T(8,128)(2,1)S(1)}, u32[]{:S(2)}, u32[]{:S(2)}) collective-permute-start(bf16[256,256]{1,0:T(8,128)(2,1)} %copy-done.138), channel_id=1, source_target_pairs={{0,2},{1,3},{2,0},{3,1},{4,6},{5,7},{6,4},{7,5},{8,10},{9,11},{10,... | collective-permute-start | bytes 393224 | tf_op jit(solution)/shard_map/ppermute | solution.py:105
  340.9 10.9 %collective-permute-start.37 = (bf16[256,256]{1,0:T(8,128)(2,1)}, bf16[256,256]{1,0:T(8,128)(2,1)S(1)}, u32[]{:S(2)}, u32[]{:S(2)}) collective-permute-start(bf16[256,256]{1,0:T(8,128)(2,1)} %copy-done.137), channel_id=1, source_target_pairs={{0,3},{1,2},{2,1},{3,0},{4,7},{5,6},{6,5},{7,4},{8,11},{9,10},{10,... | collective-permute-start | bytes 393224 | tf_op jit(solution)/shard_map/ppermute | solution.py:105
  342.8 32.8 %collective-permute-start.44 = (bf16[256,256]{1,0:T(8,128)(2,1)}, bf16[256,256]{1,0:T(8,128)(2,1)S(1)}, u32[]{:S(2)}, u32[]{:S(2)}) collective-permute-start(bf16[256,256]{1,0:T(8,128)(2,1)} %copy-done.136), channel_id=1, source_target_pairs={{0,1},{1,0},{2,3},{3,2},{4,5},{5,4},{6,7},{7,6},{8,9},{9,8},{10,11... | collective-permute-start | bytes 393224 | tf_op jit(solution)/shard_map/ppermute | solution.py:105
  354.5 29.1 %collective-permute-start.50 = (bf16[64,2496]{1,0:T(8,128)(2,1)S(1)}, bf16[64,2496]{1,0:T(8,128)(2,1)S(1)}, u32[]{:S(2)}, u32[]{:S(2)}) collective-permute-start(bf16[64,2496]{1,0:T(8,128)(2,1)S(1)} %get-tuple-element.325), channel_id=1, source_target_pairs={{0,8},{8,0},{16,24},{24,16},{1,9},{9,1},{17,25},{25,17},{2,10},{10... | collective-permute-start | bytes 958472 | tf_op jit(solution)/shard_map/ppermute | solution.py:105
  355.3 30.5 %collective-permute-start.51 = (bf16[64,2496]{1,0:T(8,128)(2,1)S(1)}, bf16[64,2496]{1,0:T(8,128)(2,1)S(1)}, u32[]{:S(2)}, u32[]{:S(2)}) collective-permute-start(bf16[64,2496]{1,0:T(8,128)(2,1)S(1)} %get-tuple-element.326), channel_id=1, source_target_pairs={{0,16},{8,24},{16,0},{24,8},{1,17},{9,25},{17,1},{25,9},{2,18},{10... | collective-permute-start | bytes 958472 | tf_op jit(solution)/shard_map/ppermute | solution.py:105
  355.7 30.2 %collective-permute-start.52 = (bf16[64,2496]{1,0:T(8,128)(2,1)S(1)}, bf16[64,2496]{1,0:T(8,128)(2,1)S(1)}, u32[]{:S(2)}, u32[]{:S(2)}) collective-permute-start(bf16[64,2496]{1,0:T(8,128)(2,1)S(1)} %get-tuple-element.327), channel_id=1, source_target_pairs={{0,24},{8,16},{16,8},{24,0},{1,25},{9,17},{17,9},{25,1},{2,26},{10... | collective-permute-start | bytes 958472 | tf_op jit(solution)/shard_map/ppermute | solution.py:105
  358.0 17.8 %collective-permute-start.45 = (bf16[256,256]{1,0:T(8,128)(2,1)S(1)}, bf16[256,256]{1,0:T(8,128)(2,1)S(1)}, u32[]{:S(2)}, u32[]{:S(2)}) collective-permute-start(bf16[256,256]{1,0:T(8,128)(2,1)S(1)} %copy-done.135), channel_id=1, source_target_pairs={{0,2},{1,3},{2,0},{3,1},{4,6},{5,7},{6,4},{7,5},{8,10},{9,11},{10,... | collective-permute-start | bytes 393224 | tf_op jit(solution)/shard_map/ppermute | solution.py:105
  375.6 12.6 %collective-permute-start.49 = (bf16[4,64,576]{2,1,0:T(8,128)(2,1)S(1)}, bf16[4,64,576]{2,1,0:T(8,128)(2,1)S(1)}, u32[]{:S(2)}, u32[]{:S(2)}) collective-permute-start(bf16[4,64,576]{2,1,0:T(8,128)(2,1)S(1)} %get-tuple-element.324.refs_6_), channel_id=1, source_target_pairs={{0,4},{4,0},{1,5},{5,1},{2,6},{6,2},{3,7},{7,3},{8,12},{12,8},{9,1... | collective-permute-start | bytes 884744 | tf_op jit(solution)/shard_map/ppermute | solution.py:1052
  375.8 7.7 %collective-permute-start.46 = (bf16[256,256]{1,0:T(8,128)(2,1)S(1)}, bf16[256,256]{1,0:T(8,128)(2,1)S(1)}, u32[]{:S(2)}, u32[]{:S(2)}) collective-permute-start(bf16[256,256]{1,0:T(8,128)(2,1)S(1)} %copy-done.133), channel_id=1, source_target_pairs={{0,3},{1,2},{2,1},{3,0},{4,7},{5,6},{6,5},{7,4},{8,11},{9,10},{10,... | collective-permute-start | bytes 393224 | tf_op jit(solution)/shard_map/ppermute | solution.py:105
  383.5 26.2 %collective-permute-start.43 = (bf16[2,256,256]{2,1,0:T(8,128)(2,1)S(1)}, bf16[2,256,256]{2,1,0:T(8,128)(2,1)S(1)}, u32[]{:S(2)}, u32[]{:S(2)}) collective-permute-start(bf16[2,256,256]{2,1,0:T(8,128)(2,1)S(1)} %get-tuple-element.307), channel_id=1, source_target_pairs={{0,4},{4,0},{1,5},{5,1},{2,6},{6,2},{3,7},{7,3},{8,12},{12,8},{9,1... | collective-permute-start | bytes 786440 | tf_op jit(solution)/shard_map/ppermute | solution.py:278
  383.5 8.3 %collective-permute-start.54 = (bf16[256,192]{1,0:T(8,128)(2,1)S(1)}, bf16[256,192]{1,0:T(8,128)(2,1)S(1)}, u32[]{:S(2)}, u32[]{:S(2)}) collective-permute-start(bf16[256,192]{1,0:T(8,128)(2,1)S(1)} %get-tuple-element.338), channel_id=1, source_target_pairs={{0,1},{1,0},{2,3},{3,2},{4,5},{5,4},{6,7},{7,6},{8,9},{9,8},{10,11... | collective-permute-start | bytes 294920 | tf_op jit(solution)/shard_map/ppermute | solution.py:105
  385.7 13.0 %collective-permute-start.55 = (bf16[256,192]{1,0:T(8,128)(2,1)S(1)}, bf16[256,192]{1,0:T(8,128)(2,1)S(1)}, u32[]{:S(2)}, u32[]{:S(2)}) collective-permute-start(bf16[256,192]{1,0:T(8,128)(2,1)S(1)} %get-tuple-element.339), channel_id=1, source_target_pairs={{0,2},{1,3},{2,0},{3,1},{4,6},{5,7},{6,4},{7,5},{8,10},{9,11},{10,... | collective-permute-start | bytes 294920 | tf_op jit(solution)/shard_map/ppermute | solution.py:105
  385.9 12.9 %collective-permute-start.56 = (bf16[256,192]{1,0:T(8,128)(2,1)S(1)}, bf16[256,192]{1,0:T(8,128)(2,1)S(1)}, u32[]{:S(2)}, u32[]{:S(2)}) collective-permute-start(bf16[256,192]{1,0:T(8,128)(2,1)S(1)} %get-tuple-element.340), channel_id=1, source_target_pairs={{0,3},{1,2},{2,1},{3,0},{4,7},{5,6},{6,5},{7,4},{8,11},{9,10},{10,... | collective-permute-start | bytes 294920 | tf_op jit(solution)/shard_map/ppermute | solution.py:105
  388.2 12.6 %collective-permute-start.67 = (bf16[16,3072]{1,0:T(8,128)(2,1)S(1)}, bf16[16,3072]{1,0:T(8,128)(2,1)S(1)}, u32[]{:S(2)}, u32[]{:S(2)}) collective-permute-start(bf16[16,3072]{1,0:T(8,128)(2,1)S(1)} %get-tuple-element.355), channel_id=1, source_target_pairs={{0,1},{1,0},{2,3},{3,2},{4,5},{5,4},{6,7},{7,6},{8,9},{9,8},{10,11... | collective-permute-start | bytes 294920 | tf_op jit(solution)/shard_map/ppermute | solution.py:105
  391.8 32.2 %collective-permute-start.53 = (bf16[2,256,256]{2,1,0:T(8,128)(2,1)S(1)}, bf16[2,256,256]{2,1,0:T(8,128)(2,1)S(1)}, u32[]{:S(2)}, u32[]{:S(2)}) collective-permute-start(bf16[2,256,256]{2,1,0:T(8,128)(2,1)S(1)} %get-tuple-element.337), channel_id=1, source_target_pairs={{0,4},{4,0},{1,5},{5,1},{2,6},{6,2},{3,7},{7,3},{8,12},{12,8},{9,1... | collective-permute-start | bytes 786440 | tf_op jit(solution)/shard_map/ppermute | solution.py:278
  398.7 9.0 %collective-permute-start.68 = (bf16[16,3072]{1,0:T(8,128)(2,1)S(1)}, bf16[16,3072]{1,0:T(8,128)(2,1)S(1)}, u32[]{:S(2)}, u32[]{:S(2)}) collective-permute-start(bf16[16,3072]{1,0:T(8,128)(2,1)S(1)} %get-tuple-element.356), channel_id=1, source_target_pairs={{0,2},{1,3},{2,0},{3,1},{4,6},{5,7},{6,4},{7,5},{8,10},{9,11},{10,... | collective-permute-start | bytes 294920 | tf_op jit(solution)/shard_map/ppermute | solution.py:105
  398.7 10.3 %collective-permute-start.69 = (bf16[16,3072]{1,0:T(8,128)(2,1)S(1)}, bf16[16,3072]{1,0:T(8,128)(2,1)S(1)}, u32[]{:S(2)}, u32[]{:S(2)}) collective-permute-start(bf16[16,3072]{1,0:T(8,128)(2,1)S(1)} %get-tuple-element.357), channel_id=1, source_target_pairs={{0,3},{1,2},{2,1},{3,0},{4,7},{5,6},{6,5},{7,4},{8,11},{9,10},{10,... | collective-permute-start | bytes 294920 | tf_op jit(solution)/shard_map/ppermute | solution.py:105
  400.8 20.5 %collective-permute-start.57 = (bf16[2,256,192]{2,1,0:T(8,128)(2,1)S(1)}, bf16[2,256,192]{2,1,0:T(8,128)(2,1)S(1)}, u32[]{:S(2)}, u32[]{:S(2)}) collective-permute-start(bf16[2,256,192]{2,1,0:T(8,128)(2,1)S(1)} %get-tuple-element.342), channel_id=1, source_target_pairs={{0,4},{4,0},{1,5},{5,1},{2,6},{6,2},{3,7},{7,3},{8,12},{12,8},{9,1... | collective-permute-start | bytes 589832 | tf_op jit(solution)/shard_map/ppermute | solution.py:278
  409.7 5.9 %collective-permute-start.60 = (bf16[64,576]{1,0:T(8,128)(2,1)S(1)}, bf16[64,576]{1,0:T(8,128)(2,1)S(1)}, u32[]{:S(2)}, u32[]{:S(2)}) collective-permute-start(bf16[64,576]{1,0:T(8,128)(2,1)S(1)} %get-tuple-element.345), channel_id=1, source_target_pairs={{0,24},{8,16},{16,8},{24,0},{1,25},{9,17},{17,9},{25,1},{2,26},{10... | collective-permute-start | bytes 221192 | tf_op jit(solution)/shard_map/ppermute | solution.py:105
  413.0 6.0 %collective-permute-start.61 = (bf16[16,2496]{1,0:T(8,128)(2,1)S(1)}, bf16[16,2496]{1,0:T(8,128)(2,1)S(1)}, u32[]{:S(2)}, u32[]{:S(2)}) collective-permute-start(bf16[16,2496]{1,0:T(8,128)(2,1)S(1)} %get-tuple-element.349), channel_id=1, source_target_pairs={{0,1},{1,0},{2,3},{3,2},{4,5},{5,4},{6,7},{7,6},{8,9},{9,8},{10,11... | collective-permute-start | bytes 239624 | tf_op jit(solution)/shard_map/ppermute | solution.py:105
  413.6 7.2 %collective-permute-start.62 = (bf16[16,2496]{1,0:T(8,128)(2,1)S(1)}, bf16[16,2496]{1,0:T(8,128)(2,1)S(1)}, u32[]{:S(2)}, u32[]{:S(2)}) collective-permute-start(bf16[16,2496]{1,0:T(8,128)(2,1)S(1)} %get-tuple-element.350), channel_id=1, source_target_pairs={{0,2},{1,3},{2,0},{3,1},{4,6},{5,7},{6,4},{7,5},{8,10},{9,11},{10,... | collective-permute-start | bytes 239624 | tf_op jit(solution)/shard_map/ppermute | solution.py:105
  415.6 13.5 %collective-permute-start.63 = (bf16[16,2496]{1,0:T(8,128)(2,1)S(1)}, bf16[16,2496]{1,0:T(8,128)(2,1)S(1)}, u32[]{:S(2)}, u32[]{:S(2)}) collective-permute-start(bf16[16,2496]{1,0:T(8,128)(2,1)S(1)} %get-tuple-element.351), channel_id=1, source_target_pairs={{0,3},{1,2},{2,1},{3,0},{4,7},{5,6},{6,5},{7,4},{8,11},{9,10},{10,... | collective-permute-start | bytes 239624 | tf_op jit(solution)/shard_map/ppermute | solution.py:105
  419.0 10.1 %collective-permute-start.64 = (bf16[16,576]{1,0:T(8,128)(2,1)S(1)}, bf16[16,576]{1,0:T(8,128)(2,1)S(1)}, u32[]{:S(2)}, u32[]{:S(2)}) collective-permute-start(bf16[16,576]{1,0:T(8,128)(2,1)S(1)} %get-tuple-element.352), channel_id=1, source_target_pairs={{0,1},{1,0},{2,3},{3,2},{4,5},{5,4},{6,7},{7,6},{8,9},{9,8},{10,11... | collective-permute-start | bytes 55304 | tf_op jit(solution)/shard_map/ppermute | solution.py:105
  420.8 8.3 %collective-permute-start.65 = (bf16[16,576]{1,0:T(8,128)(2,1)S(1)}, bf16[16,576]{1,0:T(8,128)(2,1)S(1)}, u32[]{:S(2)}, u32[]{:S(2)}) collective-permute-start(bf16[16,576]{1,0:T(8,128)(2,1)S(1)} %get-tuple-element.353), channel_id=1, source_target_pairs={{0,2},{1,3},{2,0},{3,1},{4,6},{5,7},{6,4},{7,5},{8,10},{9,11},{10,... | collective-permute-start | bytes 55304 | tf_op jit(solution)/shard_map/ppermute | solution.py:105
  421.2 7.8 %collective-permute-start.66 = (bf16[16,576]{1,0:T(8,128)(2,1)S(1)}, bf16[16,576]{1,0:T(8,128)(2,1)S(1)}, u32[]{:S(2)}, u32[]{:S(2)}) collective-permute-start(bf16[16,576]{1,0:T(8,128)(2,1)S(1)} %get-tuple-element.354), channel_id=1, source_target_pairs={{0,3},{1,2},{2,1},{3,0},{4,7},{5,6},{6,5},{7,4},{8,11},{9,10},{10,... | collective-permute-start | bytes 55304 | tf_op jit(solution)/shard_map/ppermute | solution.py:105
  (163 other events, 1417.6 us)
Sparse Core Ops, SparseCore 0:
  11.4 77.2 all-gather.2
